TPU v7x, 32 devices: a whole 2x2x4 slice. The times are simulated.
32 devices in a mesh: batch: 4 (over y, core), chan: 8 (over z, x).
Axes of the slice: x: 2, y: 2, z: 4, core: 2. Of those that a mesh axis runs over, the one named last changes fastest.
Arguments:
- inputs: bfloat16 [512, 65536], P('chan', 'batch'), may hold values from -6 to 6
- lengths: int32 [64], P('batch'), may hold values from 1 to 1024, 49152 in all
- cotangent: bfloat16 [512, 65536], P('chan', 'batch'), may hold values from -6 to 6
- ln_gain: float32 [2, 512], P(None, 'chan'), may hold values from 0.5 to 1.5
- ln_bias: float32 [2, 512], P(None, 'chan'), may hold values from -3 to 3
- log_step: float32 [2, 512], P(None, 'chan'), may hold values from -6.9 to -2.3
- skip_gain: float32 [2, 512], P(None, 'chan'), may hold values from -4 to 4
- lin_bias: float32 [2, 2, 512], P(None, None, 'chan'), may hold values from -3 to 3
- log_decay: float32 [2, 512, 64], P(None, 'chan'), may hold values from -1 to 1
- frequency: float32 [2, 512, 64], P(None, 'chan'), may hold values from 0 to 4
- w_re: float32 [2, 512, 64], P(None, 'chan'), may hold values from -3 to 3
- w_im: float32 [2, 512, 64], P(None, 'chan'), may hold values from -3 to 3
- lin_weight: float32 [2, 512, 2, 512], P(None, 'chan'), may hold values from -0.25 to 0.25
- lin_moment: float32 [2, 512, 2, 512], P(None, 'chan'), may hold values from -24 to 24
- lin_square: float32 [2, 512, 2, 512], P(None, 'chan'), may hold values from 1.114112 to 4.58752
- vec_moment: float32 [2, 6, 512], P(None, None, 'chan'), may hold values from -48 to 48
- vec_square: float32 [2, 6, 512], P(None, None, 'chan'), may hold values from 5.89824 to 23.59296
- state_moment: float32 [2, 4, 512, 64], P(None, None, 'chan'), may hold values from -48 to 48
- state_square: float32 [2, 4, 512, 64], P(None, None, 'chan'), may hold values from 5.89824 to 23.59296
Outputs:
- output: float32 [512, 65536], P('chan', 'batch')
- input_grad: float32 [512, 65536], P('chan', 'batch')
- lin_first: float32 [2, 512, 2, 512], P(None, 'chan')
- lin_second: float32 [2, 512, 2, 512], P(None, 'chan')
- lin_new: float32 [2, 512, 2, 512], P(None, 'chan')
- vec_first: float32 [2, 6, 512], P(None, None, 'chan')
- vec_second: float32 [2, 6, 512], P(None, None, 'chan')
- vec_new: float32 [2, 6, 512], P(None, None, 'chan')
- state_first: float32 [2, 4, 512, 64], P(None, None, 'chan')
- state_second: float32 [2, 4, 512, 64], P(None, None, 'chan')
- state_new: float32 [2, 4, 512, 64], P(None, None, 'chan')
Inputs may be any that keep to these rules, and one draw needn't show every extreme that they name: `lengths`: in every draw some sequence has exactly 1024 valid tokens.
All inputs are finite; a program needn't handle non-finite values. No bound on the sum of `lengths` on one device may be relied on, other than what follows from the above.
Results may differ from a plain program's by a relative error of at most 0.0061.
Values may be sent and summed in bfloat16 or wider, within the bound.
A program may use at most 256 MiB of HBM per device.

v0:
```python
import math

import jax
import jax.numpy as jnp
from jax import lax
from jax.sharding import PartitionSpec as P

LAYERS = 2
BUCKET = 1024
STEP = 10


def tables(length):
    full_width = 2 * length
    row_ids = lax.iota(jnp.int32, length)[:, None]
    col_ids = lax.iota(jnp.int32, length)[None, :]
    turn_all = (row_ids * col_ids % full_width).astype(jnp.float32) * (2.0 * math.pi / full_width)
    cosine = jnp.cos(turn_all)
    sine_table = jnp.sin(turn_all)
    weights = jnp.where(lax.iota(jnp.int32, length) == 0, 1.0, 2.0).astype(jnp.float32)[None, :]
    alternate = (1 - 2 * (lax.iota(jnp.int32, length) % 2)).astype(jnp.float32)
    return (cosine, sine_table, cosine * weights, sine_table * weights, alternate)


def mixer(normed, log_decay, frequency, w_re, w_im, log_step, skip_gain):
    top_prec = lax.Precision.HIGHEST
    chan_count = normed.shape[0]
    seq_count = normed.shape[1] // BUCKET
    step_size = jnp.exp(log_step)[:, None]
    decay_rate = step_size * jnp.exp(log_decay)
    turn_rate = step_size * frequency
    places = lax.iota(jnp.float32, BUCKET)
    decay_all = jnp.exp(-decay_rate[..., None] * places)
    soft = decay_all / jnp.sum(decay_all, -1, keepdims=True)
    phase_all = turn_rate[..., None] * places
    kernel = jnp.sum(
        (w_re[..., None] * jnp.cos(phase_all) - w_im[..., None] * jnp.sin(phase_all)) * soft, 1
    )
    cosine, sine_table, cos_back, sin_back, alternate = tables(BUCKET)
    signal = normed.reshape(chan_count, seq_count, BUCKET)
    sig_re = jnp.einsum("csl,lk->csk", signal, cosine, precision=top_prec)
    sig_im = -jnp.einsum("csl,lk->csk", signal, sine_table, precision=top_prec)
    sig_top = jnp.sum(signal * alternate, -1)
    ker_re = jnp.dot(kernel, cosine, precision=top_prec)[:, None, :]
    ker_im = -jnp.dot(kernel, sine_table, precision=top_prec)[:, None, :]
    ker_top = jnp.sum(kernel * alternate, -1)[:, None]
    prod_re = sig_re * ker_re - sig_im * ker_im
    prod_im = sig_re * ker_im + sig_im * ker_re
    prod_top = sig_top * ker_top
    conv_out = jnp.einsum("csk,lk->csl", prod_re, cos_back, precision=top_prec)
    conv_out = conv_out - jnp.einsum("csk,lk->csl", prod_im, sin_back, precision=top_prec)
    conv_out = conv_out + prod_top[..., None] * alternate
    conv_out = conv_out / (2.0 * BUCKET)
    pre_act = conv_out.reshape(normed.shape) + skip_gain[:, None] * normed
    return jax.nn.gelu(pre_act)


def adam(weight, grad, first, second, rate):
    first_new = 0.9 * first + 0.1 * grad
    second_new = 0.999 * second + 0.001 * grad * grad
    fixed_first = first_new / (1.0 - 0.9**STEP)
    fixed_second = second_new / (1.0 - 0.999**STEP)
    new_weight = weight - rate * (fixed_first / (jnp.sqrt(fixed_second) + 1e-08) + 0.01 * weight)
    return (first_new, second_new, new_weight)


def local(
    inputs,
    lengths,
    cotangent,
    ln_gain,
    ln_bias,
    log_step,
    skip_gain,
    lin_bias,
    log_decay,
    frequency,
    w_re,
    w_im,
    lin_weight,
    lin_moment,
    lin_square,
    vec_moment,
    vec_square,
    state_moment,
    state_square,
):
    chan_total = inputs.shape[0] * lax.axis_size("chan")
    tok_count = inputs.shape[1]
    places = lax.iota(jnp.int32, BUCKET)
    valid = (places[None, :] < lengths[:, None]).astype(jnp.float32).reshape(1, tok_count)
    weights_low = lin_weight.astype(jnp.bfloat16)
    stream = inputs.astype(jnp.float32)
    saved = []
    for layer_idx in range(LAYERS):
        sums = lax.psum((jnp.sum(stream, 0), jnp.sum(stream * stream, 0)), "chan")
        mean_val = sums[0] / chan_total
        variance = sums[1] / chan_total - mean_val * mean_val
        inv_std = lax.rsqrt(variance + 1e-05)[None, :]
        centred = (stream - mean_val[None, :]) * inv_std
        normed = centred * ln_gain[layer_idx][:, None] + ln_bias[layer_idx][:, None]
        activated, mixer_back = jax.vjp(
            mixer,
            normed,
            log_decay[layer_idx],
            frequency[layer_idx],
            w_re[layer_idx],
            w_im[layer_idx],
            log_step[layer_idx],
            skip_gain[layer_idx],
        )
        act_low = activated.astype(jnp.bfloat16)
        act_all = lax.all_gather(act_low, "chan", axis=0, tiled=True)
        mixed = jnp.einsum(
            "ht,cjh->cjt", act_all, weights_low[layer_idx], preferred_element_type=jnp.float32
        )
        kept = act_all
        mixed = mixed + lin_bias[layer_idx].T[:, :, None]
        gate_in = mixed[:, 0]
        gate_val = mixed[:, 1]
        stream = stream + valid * gate_in * jax.nn.sigmoid(gate_val)
        saved.append((centred, inv_std, mixer_back, kept, gate_in, gate_val))
    back_stream = cotangent.astype(jnp.float32)
    lin_grads = [None] * LAYERS
    vec_grads = [None] * LAYERS
    state_grads = [None] * LAYERS
    for layer_idx in reversed(range(LAYERS)):
        centred, inv_std, mixer_back, kept, gate_in, gate_val = saved[layer_idx]
        sigma = jax.nn.sigmoid(gate_val)
        gated_back = back_stream * valid
        grad_mixed = jnp.stack(
            [gated_back * sigma, gated_back * gate_in * sigma * (1.0 - sigma)], 1
        ).astype(jnp.bfloat16)
        bias_grad = jnp.sum(grad_mixed.astype(jnp.float32), 2).T
        weight_grad = jnp.einsum(
            "ht,cjt->cjh", kept, grad_mixed, preferred_element_type=jnp.float32
        )
        act_part = jnp.einsum(
            "cjt,cjh->ht", grad_mixed, weights_low[layer_idx], preferred_element_type=jnp.float32
        )
        act_grad = lax.psum_scatter(act_part, "chan", scatter_dimension=0, tiled=True)
        normed_grad, decay_grad, freq_grad, re_grad, im_grad, step_grad, skip_grad = mixer_back(
            act_grad
        )
        gain_grad = jnp.sum(normed_grad * centred, 1)
        shift_grad = jnp.sum(normed_grad, 1)
        centred_grad = normed_grad * ln_gain[layer_idx][:, None]
        back_sums = lax.psum((jnp.sum(centred_grad, 0), jnp.sum(centred_grad * centred, 0)), "chan")
        back_stream = back_stream + inv_std * (
            centred_grad
            - back_sums[0][None, :] / chan_total
            - centred * back_sums[1][None, :] / chan_total
        )
        lin_grads[layer_idx] = weight_grad
        vec_grads[layer_idx] = jnp.stack(
            [gain_grad, shift_grad, step_grad, skip_grad, bias_grad[0], bias_grad[1]]
        )
        state_grads[layer_idx] = jnp.stack([decay_grad, freq_grad, re_grad, im_grad])
    lin_total, vec_total, state_total = lax.psum(
        (jnp.stack(lin_grads), jnp.stack(vec_grads), jnp.stack(state_grads)), "batch"
    )
    vec_old = jnp.stack([ln_gain, ln_bias, log_step, skip_gain, lin_bias[:, 0], lin_bias[:, 1]], 1)
    state_old = jnp.stack([log_decay, frequency, w_re, w_im], 1)
    lin_first, lin_second, lin_new = adam(lin_weight, lin_total, lin_moment, lin_square, 0.05)
    vec_first, vec_second, vec_new = adam(vec_old, vec_total, vec_moment, vec_square, 0.2)
    state_first, state_second, state_new = adam(
        state_old, state_total, state_moment, state_square, 0.2
    )
    return (
        stream,
        back_stream,
        lin_first,
        lin_second,
        lin_new,
        vec_first,
        vec_second,
        vec_new,
        state_first,
        state_second,
        state_new,
    )


def solution(mesh):
    in_specs = (
        P("chan", "batch"),
        P("batch"),
        P("chan", "batch"),
        P(None, "chan"),
        P(None, "chan"),
        P(None, "chan"),
        P(None, "chan"),
        P(None, None, "chan"),
        P(None, "chan", None),
        P(None, "chan", None),
        P(None, "chan", None),
        P(None, "chan", None),
        P(None, "chan", None, None),
        P(None, "chan", None, None),
        P(None, "chan", None, None),
        P(None, None, "chan"),
        P(None, None, "chan"),
        P(None, None, "chan", None),
        P(None, None, "chan", None),
    )
    out_specs = (
        P("chan", "batch"),
        P("chan", "batch"),
        P(None, "chan", None, None),
        P(None, "chan", None, None),
        P(None, "chan", None, None),
        P(None, None, "chan"),
        P(None, None, "chan"),
        P(None, None, "chan"),
        P(None, None, "chan", None),
        P(None, None, "chan", None),
        P(None, None, "chan", None),
    )
    return jax.shard_map(local, mesh=mesh, in_specs=in_specs, out_specs=out_specs, check_vma=False)
```

profile of v0, /device:TPU:0, one launch (start us, length us, event | category | flops | bytes accessed | tf_op | source)
XLA Modules:
  0.0 2829.7 jit_solution(2015931908689452443)
XLA Ops:
  20.0 130.4 %multiply_reduce_fusion.10 = (f32[64,1024]{1,0:T(8,128)S(1)}, f32[64,1024]{1,0:T(8,128)S(1)}) fusion(f32[64,64]{1,0:T(8,128)S(1)} %fusion.9, f32[64,64]{1,0:T(8,128)S(1)} %get-tuple-element.118, f32[64,64]{1,0:T(8,128)S(1)} %get-tuple-element.116, f32[64,64]{1,0:T(8,128)S(1)} %get-tuple-element.129, f32[64,64]{1,0:T(8,128)S(1)} %get-tuple-element.112, ...), kind=kLoop, calls=%fused_computation.22 | loop fusion | flops 66977792 | bytes 688128 | tf_op jit(solution)/shard_map/jvp()/reduce_sum | solution.py:36
  191.9 31.4 %fusion.82 = f32[64,16,1024]{2,1,0:T(8,128)S(1)} fusion(f32[64,16,1024]{2,1,0:T(8,128)S(1)} %bitcast.275), kind=kOutput, calls=%fused_computation.125 | convolution fusion | flops 12899581952 | bytes 8388608 | tf_op jit(solution)/shard_map/jvp(csl,lk->csk)/dot_general | solution.py:42
  223.3 31.6 %fusion.90 = f32[64,16,1024]{2,1,0:T(8,128)S(1)} fusion(f32[64,16,1024]{2,1,0:T(8,128)S(1)} %bitcast.276), kind=kOutput, calls=%fused_computation.133 | convolution fusion | flops 12899581952 | bytes 8388608 | tf_op jit(solution)/shard_map/jvp(csl,lk->csk)/dot_general | solution.py:41
  255.0 31.0 %fusion.66 = f32[64,16,1024]{2,1,0:T(8,128)S(1)} fusion(f32[64,16,1024]{2,1,0:T(8,128)S(1)} %fusion.90, f32[64,16,1024]{2,1,0:T(8,128)S(1)} %fusion.82, f32[1024]{0:T(1024)S(1)} %fusion.271, f32[64,1024]{1,0:T(8,128)S(1)} %fusion.241, f32[64,1024]{1,0:T(8,128)S(1)} %fusion.188), kind=kOutput, calls=%fused_computation.109 | convolution fusion | flops 12904824832 | bytes 13111296 | tf_op jit(solution)/shard_map/jvp(csk,lk->csl)/dot_general | solution.py:51
  286.1 33.6 %add_multiply_fusion.1 = f32[64,16,1024]{2,1,0:T(8,128)S(1)} fusion(f32[64,16,1024]{2,1,0:T(8,128)S(1)} %fusion.66, f32[64,16]{1,0:T(8,128)S(1)} %broadcast_multiply_fusion.7, f32[1024]{0:T(1024)S(1)} %fusion.268, f32[1024]{0:T(1024)S(1)} %fusion.271, f32[64,16,1024]{2,1,0:T(8,128)S(1)} %fusion.90, f32[64,16,1024]{2,1,0:T(8,128)S(1)} %fusion.82, ...), kind=kOutput, calls=%fused_computation.189 | convolution fusion | flops 12909019136 | bytes 17313792 | tf_op jit(solution)/shard_map/jvp(csk,lk->csl)/dot_general | solution.py:50
  346.4 212.0 %all-gather.3.cloned.1.call-done = bf16[512,16384]{1,0:T(8,128)(2,1)} async-done(((bf16[64,16384]{1,0:T(8,128)(2,1)}), bf16[512,16384]{1,0:T(8,128)(2,1)}) %all-gather.3.cloned.1.call-update) | async-done | bytes 16777232 | tf_op jit(solution)/shard_map/all_gather | solution.py:113
  589.8 50.0 %all-reduce.15.cloned.1.call-done = (f32[16384]{0:T(1024)}, f32[16384]{0:T(1024)}) async-done(((f32[16384]{0:T(1024)}, f32[16384]{0:T(1024)}), (f32[16384]{0:T(1024)}, f32[16384]{0:T(1024)})) %all-reduce.15.cloned.1.call-update) | async-done | bytes 131088 | tf_op jit(solution)/shard_map/psum | solution.py:96
  646.3 31.4 %fusion.80 = f32[64,16,1024]{2,1,0:T(8,128)S(1)} fusion(f32[64,16,1024]{2,1,0:T(8,128)S(1)} %bitcast.278), kind=kOutput, calls=%fused_computation.123 | convolution fusion | flops 12899581952 | bytes 8388608 | tf_op jit(solution)/shard_map/jvp(csl,lk->csk)/dot_general | solution.py:42
  677.7 31.6 %fusion.88 = f32[64,16,1024]{2,1,0:T(8,128)S(1)} fusion(f32[64,16,1024]{2,1,0:T(8,128)S(1)} %bitcast.279), kind=kOutput, calls=%fused_computation.131 | convolution fusion | flops 12899581952 | bytes 8388608 | tf_op jit(solution)/shard_map/jvp(csl,lk->csk)/dot_general | solution.py:41
  709.4 31.2 %fusion.64 = f32[64,16,1024]{2,1,0:T(8,128)S(1)} fusion(f32[64,16,1024]{2,1,0:T(8,128)S(1)} %fusion.88, f32[64,16,1024]{2,1,0:T(8,128)S(1)} %fusion.80, f32[64,1024]{1,0:T(8,128)S(1)} %fusion.244, f32[64,1024]{1,0:T(8,128)S(1)} %fusion.183, f32[1024]{0:T(1024)S(1)} %fusion.271), kind=kOutput, calls=%fused_computation.107 | convolution fusion | flops 12904824832 | bytes 13111296 | tf_op jit(solution)/shard_map/jvp(csk,lk->csl)/dot_general | solution.py:51
  740.7 33.6 %add_multiply_fusion = f32[64,16,1024]{2,1,0:T(8,128)S(1)} fusion(f32[64,16,1024]{2,1,0:T(8,128)S(1)} %fusion.64, f32[64,16]{1,0:T(8,128)S(1)} %broadcast_multiply_fusion.5, f32[1024]{0:T(1024)S(1)} %fusion.268, f32[1024]{0:T(1024)S(1)} %fusion.271, f32[64,16,1024]{2,1,0:T(8,128)S(1)} %fusion.88, f32[64,16,1024]{2,1,0:T(8,128)S(1)} %fusion.80, ...), kind=kOutput, calls=%fused_computation.176 | convolution fusion | flops 12909019136 | bytes 17313792 | tf_op jit(solution)/shard_map/jvp(csk,lk->csl)/dot_general | solution.py:50
  782.2 227.0 %all-gather.5.cloned.1.call-done = bf16[512,16384]{1,0:T(8,128)(2,1)} async-done(((bf16[64,16384]{1,0:T(8,128)(2,1)}), bf16[512,16384]{1,0:T(8,128)(2,1)}) %all-gather.5.cloned.1.call-update) | async-done | bytes 16777232 | tf_op jit(solution)/shard_map/all_gather | solution.py:113
  1036.3 541.4 %reduce-scatter.3.cloned.1.call-done = f32[64,16384]{1,0:T(8,128)} async-done(((f32[512,16384]{1,0:T(8,128)}), f32[64,16384]{1,0:T(8,128)}) %reduce-scatter.3.cloned.1.call-update) | async-done | bytes 4194320 | tf_op jit(solution)/shard_map/reduce_scatter | solution.py:141
  1587.5 32.4 %fusion.62 = f32[64,16,1024]{2,1,0:T(8,128)S(1)} fusion(f32[64,16,1024]{2,1,0:T(8,128)S(1)} %bitcast.271, f32[1024]{0:T(1024)S(1)} %fusion.271), kind=kOutput, calls=%fused_computation.105 | convolution fusion | flops 12902727680 | bytes 8392704 | tf_op jit(solution)/shard_map/transpose(jvp(csk,lk->csl))/dot_general | solution.py:51
  1622.1 35.0 %multiply_reduce_fusion.13 = (f32[64,1024]{1,0:T(8,128)S(1)}, f32[64,1024]{1,0:T(8,128)}, f32[64,1024]{1,0:T(8,128)}, f32[64,1024]{1,0:T(8,128)}, f32[64,16,1024]{2,1,0:T(8,128)S(1)}) fusion(f32[64,16,1024]{2,1,0:T(8,128)S(1)} %copy-done.82, f32[64,16,1024]{2,1,0:T(8,128)S(1)} %copy-done.80, f32[64,16,1024]{2,1,0:T(8,128)S(1)} %fusion.62, ...), kind=kOutput, calls=%fused_computation.136 | convolution fusion | flops 12910854144 | bytes 22024192 | tf_op jit(solution)/shard_map/transpose(jvp(csk,lk->csl))/dot_general | solution.py:50
  1657.2 31.3 %fusion.78 = f32[64,16,1024]{2,1,0:T(8,128)S(1)} fusion(f32[64,16,1024]{2,1,0:T(8,128)S(1)} %get-tuple-element.142, f32[64,16,1024]{2,1,0:T(8,128)S(1)} %fusion.62, f32[64,1024]{1,0:T(8,128)S(1)} %fusion.244, f32[64,1024]{1,0:T(8,128)S(1)} %fusion.183), kind=kOutput, calls=%fused_computation.121 | convolution fusion | flops 12904824832 | bytes 13107200 | tf_op jit(solution)/shard_map/transpose(jvp(csl,lk->csk))/dot_general | solution.py:42
  1688.5 32.8 %add_add_fusion.1 = f32[64,16,1024]{2,1,0:T(8,128)S(1)} fusion(f32[64,16,1024]{2,1,0:T(8,128)S(1)} %fusion.78, f32[64,16]{1,0:T(8,128)S(1)} %get-tuple-element.125, f32[1024]{0:T(1024)S(1)} %fusion.268, f32[64,16,1024]{2,1,0:T(8,128)S(1)} %get-tuple-element.142, f32[64,16,1024]{2,1,0:T(8,128)S(1)} %fusion.62, f32[64,1024]{1,0:T(8,128)S(1)} %fusion.244, ...), kind=kOutput, calls=%fused_computation.164 | convolution fusion | flops 12905873408 | bytes 17309696 | tf_op jit(solution)/shard_map/transpose(jvp(csl,lk->csk))/dot_general | solution.py:41
  1728.3 68.8 %all-reduce.13.cloned.1.call-done = (f32[16384]{0:T(1024)}, f32[16384]{0:T(1024)}) async-done(((f32[16384]{0:T(1024)}, f32[16384]{0:T(1024)}), (f32[16384]{0:T(1024)}, f32[16384]{0:T(1024)})) %all-reduce.13.cloned.1.call-update) | async-done | bytes 131088 | tf_op jit(solution)/shard_map/psum | solution.py:148
  1842.4 20.7 fusion.229
  1882.1 68.7 %multiply_reduce_fusion.5 = f32[64,64]{1,0:T(8,128)S(1)} fusion(f32[64,64]{1,0:T(8,128)S(1)} %multiply_divide_fusion, f32[64,1024]{1,0:T(8,128)S(1)} %fusion.235, f32[64,64]{1,0:T(8,128)S(1)} %copy-done.47, f32[64,64]{1,0:T(8,128)S(1)} %copy-done.41, f32[64,64]{1,0:T(8,128)S(1)} %copy-done.49, f32[64,64]{1,0:T(8,128)S(1)} %copy-done.39), kind=kLoop, calls=%fused_computation.17 | loop fusion | flops 37744640 | bytes 360448 | tf_op jit(solution)/shard_map/transpose(jvp())/reduce_sum | solution.py:34
  1950.8 80.8 %multiply_reduce_fusion.4 = (f32[64,64]{1,0:T(8,128)S(1)}, f32[64,64]{1,0:T(8,128)S(1)}, f32[64,64]{1,0:T(8,128)S(1)}, f32[64,64]{1,0:T(8,128)S(1)}) fusion(f32[64,64]{1,0:T(8,128)S(1)} %neg.148, f32[64,1024]{1,0:T(8,128)S(1)} %fusion.235, f32[64,64]{1,0:T(8,128)S(1)} %copy-done.33, f32[64,64]{1,0:T(8,128)S(1)} %copy-done.47, f32[64,64]{1,0:T(8,128)S(1)} %copy-done.41, ...), kind=kLoop, calls=%fused_computation.16 | loop fusion | flops 109035520 | bytes 425984 | tf_op jit(solution)/shard_map/transpose(jvp())/reduce_sum | solution.py:33
  2048.0 319.7 %reduce-scatter.5.cloned.1.call-done = f32[64,16384]{1,0:T(8,128)} async-done(((f32[512,16384]{1,0:T(8,128)}), f32[64,16384]{1,0:T(8,128)}) %reduce-scatter.5.cloned.1.call-update) | async-done | bytes 4194320 | tf_op jit(solution)/shard_map/reduce_scatter | solution.py:141
  2376.6 32.4 %fusion.60 = f32[64,16,1024]{2,1,0:T(8,128)S(1)} fusion(f32[64,16,1024]{2,1,0:T(8,128)S(1)} %bitcast.269, f32[1024]{0:T(1024)S(1)} %fusion.271), kind=kOutput, calls=%fused_computation.103 | convolution fusion | flops 12902727680 | bytes 8392704 | tf_op jit(solution)/shard_map/transpose(jvp(csk,lk->csl))/dot_general | solution.py:51
  2409.2 34.4 %multiply_reduce_fusion.19 = (f32[64,1024]{1,0:T(8,128)S(1)}, f32[64,1024]{1,0:T(8,128)S(1)}, f32[64,1024]{1,0:T(8,128)S(1)}, f32[64,1024]{1,0:T(8,128)S(1)}, f32[64,16,1024]{2,1,0:T(8,128)S(1)}) fusion(f32[64,16,1024]{2,1,0:T(8,128)S(1)} %copy-done.78, f32[64,16,1024]{2,1,0:T(8,128)S(1)} %copy-done.76, f32[64,16,1024]{2,1,0:T(8,128)S(1)} %fusion.60, ...), kind=kOutput, calls=%fused_computation.142 | convolution fusion | flops 12910854144 | bytes 22024192 | tf_op jit(solution)/shard_map/transpose(jvp(csk,lk->csl))/dot_general | solution.py:50
  2443.6 19.4 fusion.232
  2463.0 19.5 fusion.238
  2482.5 68.7 %multiply_reduce_fusion.8 = f32[64,64]{1,0:T(8,128)S(1)} fusion(f32[64,64]{1,0:T(8,128)S(1)} %multiply_divide_fusion.1, f32[64,1024]{1,0:T(8,128)S(1)} %fusion.238, f32[64,64]{1,0:T(8,128)S(1)} %copy-done.43, f32[64,64]{1,0:T(8,128)S(1)} %copy-done.37, f32[64,64]{1,0:T(8,128)S(1)} %copy-done.45, f32[64,64]{1,0:T(8,128)S(1)} %copy-done.35), kind=kLoop, calls=%fused_computation.20 | loop fusion | flops 37744640 | bytes 360448 | tf_op jit(solution)/shard_map/transpose(jvp())/reduce_sum | solution.py:34
  2551.3 80.3 %multiply_reduce_fusion.7 = (f32[64,64]{1,0:T(8,128)S(1)}, f32[64,64]{1,0:T(8,128)S(1)}, f32[64,64]{1,0:T(8,128)S(1)}, f32[64,64]{1,0:T(8,128)S(1)}) fusion(f32[64,64]{1,0:T(8,128)S(1)} %neg.143, f32[64,1024]{1,0:T(8,128)S(1)} %fusion.238, f32[64,64]{1,0:T(8,128)S(1)} %copy-done.31, f32[64,64]{1,0:T(8,128)S(1)} %copy-done.43, f32[64,64]{1,0:T(8,128)S(1)} %copy-done.37, ...), kind=kLoop, calls=%fused_computation.19 | loop fusion | flops 109035520 | bytes 425984 | tf_op jit(solution)/shard_map/transpose(jvp())/reduce_sum | solution.py:33
  2632.0 31.3 %fusion.76 = f32[64,16,1024]{2,1,0:T(8,128)S(1)} fusion(f32[64,16,1024]{2,1,0:T(8,128)S(1)} %get-tuple-element.143, f32[64,16,1024]{2,1,0:T(8,128)S(1)} %fusion.60, f32[64,1024]{1,0:T(8,128)S(1)} %copy-done.84, f32[64,1024]{1,0:T(8,128)S(1)} %copy-done.86), kind=kOutput, calls=%fused_computation.119 | convolution fusion | flops 12904824832 | bytes 13107200 | tf_op jit(solution)/shard_map/transpose(jvp(csl,lk->csk))/dot_general | solution.py:42
  2663.3 32.8 %add_add_fusion = f32[64,16,1024]{2,1,0:T(8,128)S(1)} fusion(f32[64,16,1024]{2,1,0:T(8,128)S(1)} %fusion.76, f32[64,16]{1,0:T(8,128)S(1)} %get-tuple-element.123, f32[1024]{0:T(1024)S(1)} %fusion.268, f32[64,16,1024]{2,1,0:T(8,128)S(1)} %get-tuple-element.143, f32[64,16,1024]{2,1,0:T(8,128)S(1)} %fusion.60, f32[64,1024]{1,0:T(8,128)S(1)} %copy-done.84, ...), kind=kOutput, calls=%fused_computation.149 | convolution fusion | flops 12905873408 | bytes 17309696 | tf_op jit(solution)/shard_map/transpose(jvp(csl,lk->csk))/dot_general | solution.py:41
  2713.4 65.5 %all-reduce.11.cloned.1.call-done = (f32[16384]{0:T(1024)}, f32[16384]{0:T(1024)}) async-done(((f32[16384]{0:T(1024)}, f32[16384]{0:T(1024)}), (f32[16384]{0:T(1024)}, f32[16384]{0:T(1024)})) %all-reduce.11.cloned.1.call-update) | async-done | bytes 131088 | tf_op jit(solution)/shard_map/psum | solution.py:148
  2786.7 29.9 %all-reduce.19.cloned.1.call-done = (f32[2,64,2,512]{3,1,2,0:T(8,128)}, f32[2,4,64,64]{3,2,1,0:T(8,128)}) async-done(((f32[2,64,2,512]{3,1,2,0:T(8,128)}, f32[2,4,64,64]{3,2,1,0:T(8,128)}), (f32[2,64,2,512]{3,1,2,0:T(8,128)}, f32[2,4,64,64]{3,2,1,0:T(8,128)})) %all-reduce.19.cloned.1.call-update) | async-done | bytes 655376 | tf_op jit(solution)/shard_map/psum | solution.py:159
  (284 shorter events, 293.6 us)
Async XLA Ops:
  7.2 180.2 %all-reduce.17.cloned.1.call-start = ((), (), s32[]{:S(2)}) async-start(), calls=%async_computation.9 | async-start | bytes 262144 | tf_op jit(solution)/shard_map/psum | solution.py:96
  10.3 548.1 %all-gather.3.cloned.1.call-start = ((), (), s32[]{:S(2)}) async-start(), calls=%async_computation.2 | async-start | bytes 18874368 | tf_op jit(solution)/shard_map/all_gather | solution.py:113
  16.8 133.7 %copy-start.32 = (f32[64,64]{1,0:T(8,128)}, f32[64,64]{1,0:T(8,128)S(1)}, u32[]{:S(2)}) copy-start(f32[64,64]{1,0:T(8,128)S(1)} %fusion.9) | copy-start | bytes 49156
  19.9 130.5 %copy-start.30 = (f32[64,64]{1,0:T(8,128)}, f32[64,64]{1,0:T(8,128)S(1)}, u32[]{:S(2)}) copy-start(f32[64,64]{1,0:T(8,128)S(1)} %fusion.14) | copy-start | bytes 49156
  168.7 117.3 %copy-start.83 = (f32[64,1024]{1,0:T(8,128)}, f32[64,1024]{1,0:T(8,128)S(1)}, u32[]{:S(2)}) copy-start(f32[64,1024]{1,0:T(8,128)S(1)} %fusion.241) | copy-start | bytes 786436
  187.1 99.0 %copy-start.85 = (f32[64,1024]{1,0:T(8,128)}, f32[64,1024]{1,0:T(8,128)S(1)}, u32[]{:S(2)}) copy-start(f32[64,1024]{1,0:T(8,128)S(1)} %fusion.188) | copy-start | bytes 786436
  187.1 135.1 %copy-start.55 = (f32[64]{0:T(128)}, f32[64]{0:T(128)S(1)}, u32[]{:S(2)}) copy-start(f32[64]{0:T(128)S(1)} %get-tuple-element.133) | copy-start | bytes 772
  187.2 135.0 %copy-start.50 = (f32[64]{0:T(128)}, f32[64]{0:T(128)S(1)}, u32[]{:S(2)}) copy-start(f32[64]{0:T(128)S(1)} %get-tuple-element.144) | copy-start | bytes 772
  187.2 135.0 %copy-start.52 = (f32[64]{0:T(128)}, f32[64]{0:T(128)S(1)}, u32[]{:S(2)}) copy-start(f32[64]{0:T(128)S(1)} %get-tuple-element.137) | copy-start | bytes 772
  187.3 67.6 %copy-start.65 = (f32[64]{0:T(128)}, f32[64]{0:T(128)S(1)}, u32[]{:S(2)}) copy-start(f32[64]{0:T(128)S(1)} %get-tuple-element.78) | copy-start | bytes 772
  188.2 134.0 %copy-start.14 = (f32[16384]{0:T(1024)}, f32[16384]{0:T(1024)S(1)}, u32[]{:S(2)}) copy-start(f32[16384]{0:T(1024)S(1)} %get-tuple-element.120) | copy-start | bytes 196612
  188.3 134.0 %copy-start.16 = (f32[16384]{0:T(1024)}, f32[16384]{0:T(1024)S(1)}, u32[]{:S(2)}) copy-start(f32[16384]{0:T(1024)S(1)} %get-tuple-element.121) | copy-start | bytes 196612
  327.9 311.8 %all-reduce.15.cloned.1.call-start = ((), (), s32[]{:S(2)}) async-start(), calls=%async_computation.8 | async-start | bytes 262144 | tf_op jit(solution)/shard_map/psum | solution.py:96
  571.4 437.8 %all-gather.5.cloned.1.call-start = ((), (), s32[]{:S(2)}) async-start(), calls=%async_computation.3 | async-start | bytes 18874368 | tf_op jit(solution)/shard_map/all_gather | solution.py:113
  782.1 795.5 %reduce-scatter.3.cloned.1.call-start = ((), (), s32[]{:S(2)}) async-start(), calls=%async_computation.4 | async-start | bytes 37748736 | tf_op jit(solution)/shard_map/reduce_scatter | solution.py:141
  1036.2 760.9 %all-reduce.13.cloned.1.call-start = ((), (), s32[]{:S(2)}) async-start(), calls=%async_computation.7 | async-start | bytes 262144 | tf_op jit(solution)/shard_map/psum | solution.py:148
  1728.0 639.7 %reduce-scatter.5.cloned.1.call-start = ((), (), s32[]{:S(2)}) async-start(), calls=%async_computation.5 | async-start | bytes 37748736 | tf_op jit(solution)/shard_map/reduce_scatter | solution.py:141
  1804.3 227.3 %copy-start.9 = (bf16[64,1,16384]{2,0,1:T(8,128)(2,1)}, bf16[64,1,16384]{2,0,1:T(8,128)(2,1)S(1)}, u32[]{:S(2)}) copy-start(bf16[64,1,16384]{2,0,1:T(8,128)(2,1)S(1)} %get-tuple-element.101) | copy-start | bytes 6291460
  1825.2 953.7 %all-reduce.11.cloned.1.call-start = ((), (), s32[]{:S(2)}) async-start(), calls=%async_computation.6 | async-start | bytes 262144 | tf_op jit(solution)/shard_map/psum | solution.py:148
  2044.2 323.6 %copy-start.5 = (bf16[64,16384]{1,0:T(8,128)(2,1)S(1)}, bf16[64,16384]{1,0:T(8,128)(2,1)}, u32[]{:S(2)}) copy-start(bf16[64,16384]{1,0:T(8,128)(2,1)} %param.19) | copy-start | bytes 6291460
  2044.2 323.6 %copy-start.15 = (f32[16384]{0:T(1024)S(1)}, f32[16384]{0:T(1024)}, u32[]{:S(2)}) copy-start(f32[16384]{0:T(1024)} %copy-done.14) | copy-start | bytes 196612
  2044.2 323.6 %copy-start.17 = (f32[16384]{0:T(1024)S(1)}, f32[16384]{0:T(1024)}, u32[]{:S(2)}) copy-start(f32[16384]{0:T(1024)} %copy-done.16) | copy-start | bytes 196612
  2044.2 323.6 %copy-start.51 = (f32[64]{0:T(128)S(1)}, f32[64]{0:T(128)}, u32[]{:S(2)}) copy-start(f32[64]{0:T(128)} %copy-done.50) | copy-start | bytes 772
  2044.2 323.6 %copy-start.53 = (f32[64]{0:T(128)S(1)}, f32[64]{0:T(128)}, u32[]{:S(2)}) copy-start(f32[64]{0:T(128)} %copy-done.52) | copy-start | bytes 772
  2044.2 323.6 %copy-start.56 = (f32[64]{0:T(128)S(1)}, f32[64]{0:T(128)}, u32[]{:S(2)}) copy-start(f32[64]{0:T(128)} %copy-done.55) | copy-start | bytes 772
  2551.2 80.3 %copy-start.20 = (f32[2,64,64]{2,1,0:T(8,128)S(1)}, f32[2,64,64]{2,1,0:T(8,128)}, u32[]{:S(2)}) copy-start(f32[2,64,64]{2,1,0:T(8,128)} %param.27) | copy-start | bytes 98308
  2551.2 80.5 %copy-start.21 = (f32[2,64,64]{2,1,0:T(8,128)S(1)}, f32[2,64,64]{2,1,0:T(8,128)}, u32[]{:S(2)}) copy-start(f32[2,64,64]{2,1,0:T(8,128)} %param.28) | copy-start | bytes 98308
  2551.2 80.6 %copy-start.62 = (f32[64]{0:T(128)S(1)}, f32[64]{0:T(128)}, u32[]{:S(2)}) copy-start(f32[64]{0:T(128)} %copy-done.61) | copy-start | bytes 772
  2551.3 80.6 %copy-start.64 = (f32[64]{0:T(128)S(1)}, f32[64]{0:T(128)}, u32[]{:S(2)}) copy-start(f32[64]{0:T(128)} %copy-done.63) | copy-start | bytes 772
  2551.3 80.7 %copy-start.84 = (f32[64,1024]{1,0:T(8,128)S(1)}, f32[64,1024]{1,0:T(8,128)}, u32[]{:S(2)}) copy-start(f32[64,1024]{1,0:T(8,128)} %copy-done.83) | copy-start | bytes 786436
  2551.3 80.7 %copy-start.86 = (f32[64,1024]{1,0:T(8,128)S(1)}, f32[64,1024]{1,0:T(8,128)}, u32[]{:S(2)}) copy-start(f32[64,1024]{1,0:T(8,128)} %copy-done.85) | copy-start | bytes 786436
  2710.7 105.9 %all-reduce.19.cloned.1.call-start = ((), (), s32[]{:S(2)}) async-start(), calls=%async_computation.10 | async-start | bytes 1572864 | tf_op jit(solution)/shard_map/psum | solution.py:159
  (65 other events, 1043.6 us)
Sparse Core Ops, SparseCore 0:
  12.0 72.5 all-reduce.16
  328.0 230.3 all-gather.2
  571.5 68.1 all-reduce.14
  782.3 226.8 all-gather.4
  1036.3 541.2 reduce-scatter.2
  1728.2 68.8 all-reduce.12
  1825.4 542.3 reduce-scatter.4
  2710.8 68.0 all-reduce.10
  2782.5 33.9 all-reduce.18
where the time goes:
time: 2840 us; the launch traced here: 2830 us
  waiting for transfers between devices  1510 us (53%)
  matrix products  738 us (26%)
  other arithmetic  517 us (18%)
  local copies, waits for them, and re-layouts  37.5 us (1%)
    reduce_scatter x2, waiting for transfers between devices, local(): lax.psum_scatter(act_part, 'chan', scatter_dimension=0, tiled=True)  861 us
    all_gather x2, waiting for transfers between devices, local(): act_all = lax.all_gather(act_low, 'chan', axis=0, tiled=True)  439 us
    reduce_sum x2, other arithmetic, mixer(): decay_all = jnp.exp(-decay_rate[..., None] * places)  161 us
    reduce_sum x4, other arithmetic, mixer(): soft = decay_all / jnp.sum(decay_all, -1, keepdims=True)  144 us
    dot_general x4, matrix products, mixer(): conv_out = jnp.einsum('csk,lk->csl', prod_re, cos_back, precision=top_prec)  137 us
    psum x2, waiting for transfers between devices, local(): lax.psum((jnp.sum(centred_grad, 0), jnp.sum(centred_grad * centred, 0)),...  134 us
    reduce_sum x1, other arithmetic, mixer(): jnp.sum((w_re[..., None] * jnp.cos(phase_all) - w_im[..., None] * jnp.sin...  130 us
    dot_general x4, matrix products, mixer(): sig_re = jnp.einsum('csl,lk->csk', signal, cosine, precision=top_prec)  129 us
  transfers between devices with their start and end apart: 9, of which 8 were waited for; matrix products, arithmetic and copies ran while one was open for 16% of the time, Pallas kernels for 0%

commit v1 on v0

--- a/solution.py
+++ b/solution.py
@@ -8,6 +8,236 @@
 LAYERS = 2
 BUCKET = 1024
 STEP = 10
+
+
+def transforms():
+    rows = lax.iota(jnp.int32, BUCKET)[:, None]
+    cols = lax.iota(jnp.int32, BUCKET)[None, :]
+    turn = (rows * cols % (2 * BUCKET)).astype(jnp.float32) * (math.pi / BUCKET)
+    alternate = (1 - 2 * (rows % 2)).astype(jnp.float32)
+    cosine = jnp.cos(turn)
+    minus_sine = jnp.where(cols == 0, alternate, -jnp.sin(turn))
+    forward = jnp.concatenate([cosine, minus_sine], 1)
+    weights = jnp.where(cols == 0, 1.0, 2.0) / (2.0 * BUCKET)
+    inverse = jnp.concatenate([cosine * weights, minus_sine * weights], 1).T
+    return forward.astype(jnp.bfloat16), inverse.astype(jnp.bfloat16)
+
+
+def dot(a, b):
+    return jnp.dot(a.astype(jnp.bfloat16), b, preferred_element_type=jnp.float32)
+
+
+def powers(decay_rate, turn_rate, places):
+    size = jnp.exp(-decay_rate[..., None] * places)
+    phase = turn_rate[..., None] * places
+    return size * jnp.cos(phase), size * jnp.sin(phase), size
+
+
+def state_tables(log_decay, frequency, log_step):
+    step_size = jnp.exp(log_step)[..., None]
+    decay_rate = step_size * jnp.exp(log_decay)
+    turn_rate = step_size * frequency
+    fine = lax.iota(jnp.float32, 32)
+    lo_re, lo_im, lo = powers(decay_rate, turn_rate, fine)
+    hi_re, hi_im, hi = powers(decay_rate, turn_rate, fine * 32.0)
+    total = jnp.sum(lo, -1) * jnp.sum(hi, -1)
+    moment = jnp.sum(lo * fine, -1) * jnp.sum(hi, -1) + jnp.sum(lo, -1) * jnp.sum(hi * (fine * 32.0), -1)
+    return decay_rate, turn_rate, lo_re, lo_im, hi_re, hi_im, total, moment
+
+
+def make_kernel(log_decay, frequency, w_re, w_im, log_step):
+    _, _, lo_re, lo_im, hi_re, hi_im, total, _ = state_tables(log_decay, frequency, log_step)
+    a_re = (w_re / total)[..., None]
+    a_im = (w_im / total)[..., None]
+    c_re = a_re * hi_re - a_im * hi_im
+    c_im = a_re * hi_im + a_im * hi_re
+    out = jnp.sum(c_re[..., :, None] * lo_re[..., None, :] - c_im[..., :, None] * lo_im[..., None, :], -3)
+    return out.reshape(out.shape[:-2] + (BUCKET,))
+
+
+def kernel_back(grad, log_decay, frequency, w_re, w_im, log_step):
+    decay_rate, turn_rate, lo_re, lo_im, hi_re, hi_im, total, moment = state_tables(log_decay, frequency, log_step)
+    fine = lax.iota(jnp.float32, 32)
+    g = grad.reshape(grad.shape[:-1] + (1, 32, 32))
+    t_re = jnp.sum(g * lo_re[..., None, :], -1)
+    t_im = jnp.sum(g * lo_im[..., None, :], -1)
+    g_fine = g * fine
+    u_re = jnp.sum(g_fine * lo_re[..., None, :], -1) + t_re * (fine * 32.0)
+    u_im = jnp.sum(g_fine * lo_im[..., None, :], -1) + t_im * (fine * 32.0)
+    c_re = jnp.sum(t_re * hi_re - t_im * hi_im, -1) / total
+    c_im = jnp.sum(t_re * hi_im + t_im * hi_re, -1) / total
+    d_re = jnp.sum(u_re * hi_re - u_im * hi_im, -1) / total
+    d_im = jnp.sum(u_re * hi_im + u_im * hi_re, -1) / total
+    turn_grad = -(w_re * d_im + w_im * d_re)
+    decay_grad = (w_re * c_re - w_im * c_im) * (moment / total) - (w_re * d_re - w_im * d_im)
+    step_grad = jnp.sum(decay_grad * decay_rate + turn_grad * turn_rate, -1)
+    freq_grad = turn_grad * jnp.exp(log_step)[..., None]
+    return decay_grad * decay_rate, freq_grad, c_re, -c_im, step_grad
+
+
+def adam(weight, grad, first, second, rate):
+    first_new = 0.9 * first + 0.1 * grad
+    second_new = 0.999 * second + 0.001 * grad * grad
+    fixed_first = first_new / (1.0 - 0.9**STEP)
+    fixed_second = second_new / (1.0 - 0.999**STEP)
+    new_weight = weight - rate * (fixed_first / (jnp.sqrt(fixed_second) + 1e-08) + 0.01 * weight)
+    return (first_new, second_new, new_weight)
+
+
+def spread(block, axis):
+    count = lax.axis_size(axis)
+    return lax.all_to_all(jnp.broadcast_to(block[None], (count,) + block.shape), axis, 0, 0, tiled=True)
+
+
+def local(
+    inputs, lengths, cotangent, ln_gain, ln_bias, log_step, skip_gain, lin_bias, log_decay, frequency,
+    w_re, w_im, lin_weight, lin_moment, lin_square, vec_moment, vec_square, state_moment, state_square,
+):
+    n_chan = lax.axis_size("chan")
+    n_batch = lax.axis_size("batch")
+    own = inputs.shape[0]
+    chans = own * n_chan
+    toks = inputs.shape[1] // n_chan
+    seqs = toks // BUCKET
+    part = own // n_batch
+    me = lax.axis_index("chan")
+    row = lax.axis_index("batch")
+    lens = lax.dynamic_slice_in_dim(lengths, me * seqs, seqs)
+    places = lax.iota(jnp.int32, BUCKET)
+    valid = (places[None, :] < lens[:, None]).astype(jnp.float32).reshape(1, toks)
+    forward, inverse = transforms()
+    bin_zero = (lax.iota(jnp.int32, BUCKET) == 0)[None, :]
+
+    def mine(a):
+        return lax.dynamic_slice_in_dim(a, row * part, part, 1)
+
+    state_args = [mine(a) for a in (log_decay, frequency, w_re, w_im, log_step)]
+    ker_own = make_kernel(*state_args)
+    w_own = lax.dynamic_slice_in_dim(lin_weight, row * part, part, 1).reshape(LAYERS, part, 2 * chans)
+    pack = jnp.stack([ker_own.reshape(LAYERS, part, BUCKET), w_own.reshape(LAYERS, part, BUCKET)], 1).astype(jnp.bfloat16)
+    vec_own = jnp.concatenate([ln_gain, ln_bias, skip_gain, lin_bias.reshape(LAYERS * 2, own)], 0)
+    vec_all = spread(vec_own, "chan").transpose(1, 0, 2).reshape(10, chans)
+    gains, shifts, skips = vec_all[0:2], vec_all[2:4], vec_all[4:6]
+    biases = vec_all[6:10].reshape(LAYERS, 2, chans)
+    pack = spread(pack, "chan")
+    pack = spread(pack, "batch")
+    pack = pack.transpose(2, 3, 1, 0, 4, 5)
+    kers = pack[:, 0].reshape(LAYERS, chans, BUCKET)
+    weights = pack[:, 1].reshape(LAYERS, chans, 2, chans)
+
+    first_low = lax.all_to_all(inputs, "chan", 1, 0, tiled=True)
+    cot_low = lax.all_to_all(cotangent, "chan", 1, 0, tiled=True)
+    stream0 = first_low.astype(jnp.float32)
+    stream = stream0
+
+    def spectrum(signal):
+        halves = [dot(signal[:, s * BUCKET : (s + 1) * BUCKET], forward) for s in range(seqs)]
+        return [(h[:, :BUCKET], h[:, BUCKET:]) for h in halves]
+
+    def back_to_time(spec):
+        return jnp.concatenate([dot(jnp.concatenate([r, i], 1), inverse) for r, i in spec], 1)
+
+    def times(a, b):
+        a_re, a_im = a
+        b_re, b_im = b
+        cross = a_im * b_im
+        return a_re * b_re - jnp.where(bin_zero, 0.0, cross), jnp.where(bin_zero, cross, a_re * b_im + a_im * b_re)
+
+    def times_conj(a, b):
+        a_re, a_im = a
+        b_re, b_im = b
+        cross = a_im * b_im
+        return a_re * b_re + jnp.where(bin_zero, 0.0, cross), jnp.where(bin_zero, cross, a_re * b_im - a_im * b_re)
+
+    saved = []
+    for i in range(LAYERS):
+        mean_val = jnp.mean(stream, 0, keepdims=True)
+        variance = jnp.mean(stream * stream, 0, keepdims=True) - mean_val * mean_val
+        inv_std = lax.rsqrt(variance + 1e-05)
+        centred = (stream - mean_val) * inv_std
+        normed = centred * gains[i][:, None] + shifts[i][:, None]
+        ker_both = dot(kers[i], forward)
+        ker_spec = (ker_both[:, :BUCKET], ker_both[:, BUCKET:])
+        sig_spec = spectrum(normed)
+        pre = back_to_time([times(s, ker_spec) for s in sig_spec]) + skips[i][:, None] * normed
+        act = jax.nn.gelu(pre).astype(jnp.bfloat16)
+        mixed = jnp.einsum("jch,ht->cjt", weights[i], act, preferred_element_type=jnp.float32)
+        gate_in = mixed[0] + biases[i, 0][:, None]
+        gate_val = mixed[1] + biases[i, 1][:, None]
+        stream = stream + valid * gate_in * jax.nn.sigmoid(gate_val)
+        saved.append((centred, inv_std, normed, ker_spec, sig_spec, pre, act, gate_in, gate_val))
+    out_delta = (stream - stream0).astype(jnp.bfloat16)
+    out_delta = lax.all_to_all(out_delta, "chan", 0, 1, tiled=True)
+    output = inputs.astype(jnp.float32) + out_delta.astype(jnp.float32)
+
+    back0 = cot_low.astype(jnp.float32)
+    back = back0
+    packs = [None] * LAYERS
+    vecs = [None] * LAYERS
+    for i in reversed(range(LAYERS)):
+        centred, inv_std, normed, ker_spec, sig_spec, pre, act, gate_in, gate_val = saved[i]
+        sigma = jax.nn.sigmoid(gate_val)
+        gated = back * valid
+        grad_in = (gated * sigma).astype(jnp.bfloat16)
+        grad_val = (gated * gate_in * sigma * (1.0 - sigma)).astype(jnp.bfloat16)
+        grad_mixed = jnp.stack([grad_in, grad_val], 0)
+        bias_grad = jnp.sum(grad_mixed.astype(jnp.float32), 2)
+        weight_grad = jnp.einsum("cjt,ht->jch", grad_mixed, act, preferred_element_type=jnp.float32)
+        act_grad = jnp.einsum("jch,cjt->ht", weights[i], grad_mixed, preferred_element_type=jnp.float32)
+        _, gelu_back = jax.vjp(jax.nn.gelu, pre)
+        (pre_grad,) = gelu_back(act_grad)
+        grad_spec = spectrum(pre_grad)
+        normed_grad = back_to_time([times_conj(ker_spec, g) for g in grad_spec]) + skips[i][:, None] * pre_grad
+        cross = [times_conj(s, g) for s, g in zip(sig_spec, grad_spec)]
+        cross = [(sum(c[0] for c in cross), sum(c[1] for c in cross))]
+        ker_grad = back_to_time(cross)
+        skip_grad = jnp.sum(pre_grad * normed, 1)
+        gain_grad = jnp.sum(normed_grad * centred, 1)
+        shift_grad = jnp.sum(normed_grad, 1)
+        cent_grad = normed_grad * gains[i][:, None]
+        sum_a = jnp.mean(cent_grad, 0, keepdims=True)
+        sum_b = jnp.mean(cent_grad * centred, 0, keepdims=True)
+        back = back + inv_std * (cent_grad - sum_a - centred * sum_b)
+        packs[i] = jnp.stack([ker_grad.reshape(n_chan, n_batch, part, BUCKET), weight_grad.reshape(n_chan, n_batch, part, BUCKET)], 2)
+        vecs[i] = jnp.stack([gain_grad, shift_grad, skip_grad, bias_grad[0], bias_grad[1]])
+    in_delta = (back - back0).astype(jnp.bfloat16)
+    in_delta = lax.all_to_all(in_delta, "chan", 0, 1, tiled=True)
+    input_grad = cotangent.astype(jnp.float32) + in_delta.astype(jnp.float32)
+
+    grads = jnp.stack(packs, 2).astype(jnp.bfloat16)
+    grads = lax.all_to_all(grads, "batch", 1, 1, tiled=True)
+    grads = jnp.sum(grads.astype(jnp.float32), 1).astype(jnp.bfloat16)
+    grads = lax.all_to_all(grads, "chan", 0, 0, tiled=True)
+    grads = jnp.sum(grads.astype(jnp.float32), 0)
+    vec_part = jnp.stack(vecs).reshape(LAYERS, 5, n_chan, own).transpose(2, 0, 1, 3)
+    vec_part = jnp.sum(lax.all_to_all(vec_part, "chan", 0, 0, tiled=True), 0)
+
+    state_parts = kernel_back(grads[:, 0], *state_args)
+    step_grad = state_parts[4]
+    state_grad = jnp.stack(state_parts[:4], 1)
+    send = jnp.concatenate(
+        [state_grad.reshape(-1), grads[:, 1].reshape(-1), step_grad.reshape(-1), vec_part.reshape(-1)]
+    )
+    got = spread(send, "batch").reshape(n_batch, -1)
+    sizes = [state_grad.size, grads[:, 1].size, step_grad.size, vec_part.size]
+    cuts = [sum(sizes[:k]) for k in range(5)]
+    state_total = got[:, cuts[0] : cuts[1]].reshape((n_batch,) + state_grad.shape).transpose(1, 2, 0, 3, 4)
+    state_total = state_total.reshape(LAYERS, 4, own, -1)
+    lin_total = got[:, cuts[1] : cuts[2]].reshape(n_batch, LAYERS, part, 2, chans).transpose(1, 0, 2, 3, 4)
+    lin_total = lin_total.reshape(LAYERS, own, 2, chans)
+    step_total = got[:, cuts[2] : cuts[3]].reshape(n_batch, LAYERS, part).transpose(1, 0, 2).reshape(LAYERS, own)
+    vec_sum = jnp.sum(got[:, cuts[3] : cuts[4]], 0).reshape(LAYERS, 5, own)
+    vec_total = jnp.stack([vec_sum[:, 0], vec_sum[:, 1], step_total, vec_sum[:, 2], vec_sum[:, 3], vec_sum[:, 4]], 1)
+
+    vec_old = jnp.stack([ln_gain, ln_bias, log_step, skip_gain, lin_bias[:, 0], lin_bias[:, 1]], 1)
+    state_old = jnp.stack([log_decay, frequency, w_re, w_im], 1)
+    lin_first, lin_second, lin_new = adam(lin_weight, lin_total, lin_moment, lin_square, 0.05)
+    vec_first, vec_second, vec_new = adam(vec_old, vec_total, vec_moment, vec_square, 0.2)
+    state_first, state_second, state_new = adam(state_old, state_total, state_moment, state_square, 0.2)
+    return (
+        output, input_grad, lin_first, lin_second, lin_new, vec_first, vec_second, vec_new,
+        state_first, state_second, state_new,
+    )
 
 
 def tables(length):
@@ -55,16 +285,7 @@
     return jax.nn.gelu(pre_act)
 
 
-def adam(weight, grad, first, second, rate):
-    first_new = 0.9 * first + 0.1 * grad
-    second_new = 0.999 * second + 0.001 * grad * grad
-    fixed_first = first_new / (1.0 - 0.9**STEP)
-    fixed_second = second_new / (1.0 - 0.999**STEP)
-    new_weight = weight - rate * (fixed_first / (jnp.sqrt(fixed_second) + 1e-08) + 0.01 * weight)
-    return (first_new, second_new, new_weight)
-
-
-def local(
+def wide_local(
     inputs,
     lengths,
     cotangent,
@@ -216,4 +437,12 @@
         P(None, None, "chan", None),
         P(None, None, "chan", None),
     )
-    return jax.shard_map(local, mesh=mesh, in_specs=in_specs, out_specs=out_specs, check_vma=False)
+    n_chan = mesh.shape["chan"]
+
+    def run(*args):
+        own_seqs = args[1].shape[0] // mesh.shape["batch"]
+        fits = own_seqs % n_chan == 0 and args[3].shape[1] // n_chan % mesh.shape["batch"] == 0
+        body = local if fits else wide_local
+        return jax.shard_map(body, mesh=mesh, in_specs=in_specs, out_specs=out_specs, check_vma=False)(*args)
+
+    return run

time: 2840 us -> 622 us (0.22)
  waiting for transfers between devices: 1510 us -> 192 us
  matrix products: 738 us -> 103 us
  other arithmetic: 517 us -> 191 us
  starting transfers between devices: 0.55 us -> 56.3 us
  local copies, waits for them, and re-layouts: 37.5 us -> 67.4 us
    reduce_scatter x2 -> x0, waiting for transfers between devices: 861 us -> none  [local(): lax.psum_scatter(act_part, 'chan', scatter_dimension=0, tiled=True)]
    dot_general x30 -> x26, matrix products: 738 us -> 103 us  [the longest x20 68.2 us: dot(): jnp.dot(a.astype(jnp.bfloat16), b, preferred_element_type=jnp.float32)]
    all_gather x2 -> x0, waiting for transfers between devices: 439 us -> none  [local(): act_all = lax.all_gather(act_low, 'chan', axis=0, tiled=True)]
    reduce_sum x21 -> x14, other arithmetic: 458 us -> 39.8 us  [the longest x1 17.8 us: kernel_back(): u_im = jnp.sum(g_fine * lo_im[..., None, :], -1) + t_im * (fine * 32.0)]
    psum x5 -> x0, waiting for transfers between devices: 214 us -> none  [the longest x2 134 us: local(): lax.psum((jnp.sum(centred_grad, 0), jnp.sum(centred_grad * centred, 0)),...]
    all_to_all x0 -> x11, waiting for transfers between devices: none -> 192 us  [the longest x4 44.6 us: spread(): lax.all_to_all(jnp.broadcast_to(block[None], (count,) + block.shape), axi...]
    another operation x8 -> x19, other arithmetic: 17.8 us -> 87.2 us  [the longest x11 80.3 us: run(): jax.shard_map(body, mesh=mesh, in_specs=in_specs, out_specs=out_specs, ch...]
    all_to_all x0 -> x11, starting transfers between devices: none -> 56.3 us  [the longest x4 21.6 us: spread(): lax.all_to_all(jnp.broadcast_to(block[None], (count,) + block.shape), axi...]
  transfers between devices with their start and end apart: 9 -> 11, of which waited for: 8 -> 8; matrix products, arithmetic and copies ran while one was open for 16% -> 34% of each run, Pallas kernels for 0% -> 0%
where the time goes in v1:
time: 622 us; the launch traced here: 612 us
  waiting for transfers between devices  192 us (31%)
  other arithmetic  191 us (31%)
  matrix products  103 us (17%)
  local copies, waits for them, and re-layouts  67.4 us (11%)
  starting transfers between devices  56.3 us (9%)
    another operation x11, other arithmetic, run(): jax.shard_map(body, mesh=mesh, in_specs=in_specs, out_specs=out_specs, ch...  80.3 us
    dot_general x20, matrix products, dot(): jnp.dot(a.astype(jnp.bfloat16), b, preferred_element_type=jnp.float32)  68.2 us
    all_to_all x4, waiting for transfers between devices, spread(): lax.all_to_all(jnp.broadcast_to(block[None], (count,) + block.shape), axi...  44.6 us
    all_to_all x1, waiting for transfers between devices, local(): grads = lax.all_to_all(grads, 'batch', 1, 1, tiled=True)  41.3 us
    all_to_all x1, waiting for transfers between devices, local(): out_delta = lax.all_to_all(out_delta, 'chan', 0, 1, tiled=True)  40.9 us
    all_to_all x1, waiting for transfers between devices, local(): in_delta = lax.all_to_all(in_delta, 'chan', 0, 1, tiled=True)  36.8 us
    unnamed x254, local copies, waits for them, and re-layouts  22 us
    all_to_all x4, starting transfers between devices, spread(): lax.all_to_all(jnp.broadcast_to(block[None], (count,) + block.shape), axi...  21.6 us
  transfers between devices with their start and end apart: 11, of which 8 were waited for; matrix products, arithmetic and copies ran while one was open for 34% of the time, Pallas kernels for 0%

profile of v1, /device:TPU:0, one launch (start us, length us, event | category | flops | bytes accessed | tf_op | source)
XLA Modules:
  0.0 612.2 jit_solution(9537762540429697598)
XLA Ops:
  2.1 7.3 %all-to-all-start.1 = ((f32[8,1,640]{2,1,0:T(1,128)}), f32[8,1,640]{2,1,0:T(1,128)S(1)}, u32[]{:S(2)}, u32[]{:S(2)}) async-start(f32[8,1,640]{2,1,0:T(1,128)} %reshape.627), calls=%async_computation.1 | async-start | bytes 40960 | tf_op jit(solution)/shard_map/all_to_all | solution.py:89
  19.2 6.0 subtract_reduce_fusion
  26.6 6.0 all-to-all-start.2
  34.1 24.0 %all-to-all-done.2 = bf16[8,2,2,16,1024]{4,3,2,1,0:T(8,128)(2,1)S(1)} async-done(((bf16[8,2,2,16,1024]{4,3,2,1,0:T(8,128)(2,1)}), bf16[8,2,2,16,1024]{4,3,2,1,0:T(8,128)(2,1)S(1)}, u32[]{:S(2)}, u32[]{:S(2)}) %all-to-all-start.2) | async-done | bytes 1048608 | tf_op jit(solution)/shard_map/all_to_all | solution.py:89
  62.2 16.9 %fusion.78 = bf16[1024,1024]{1,0:T(8,128)(2,1)} fusion(f32[1024]{0:T(1024)S(1)} %fusion.181, pred[1024]{0:T(1024)(128)(4,1)S(1)} %iota_compare_fusion), kind=kLoop, calls=%fused_computation.140 | loop fusion | flops 16777216 | bytes 2102272 | tf_op jit(solution)/shard_map/convert.60 | solution.py:446
  79.2 18.6 %multiply_convert_fusion.5 = (bf16[1024,1024]{1,0:T(8,128)(2,1)}, bf16[1024,1024]{1,0:T(8,128)(2,1)}) fusion(f32[1024]{0:T(1024)S(1)} %select_multiply_fusion, f32[1024]{0:T(1024)S(1)} %fusion.181, pred[1024]{0:T(1024)(128)(4,1)S(1)} %iota_compare_fusion), kind=kLoop, calls=%fused_computation.132 | loop fusion | flops 20971520 | bytes 4203520 | tf_op jit(solution)/shard_map/convert.51 | solution.py:446
  99.1 11.2 %all-to-all-done = bf16[64,8,2048]{2,0,1:T(8,128)(2,1)S(1)} async-done(((bf16[64,8,2048]{2,0,1:T(8,128)(2,1)}), bf16[64,8,2048]{2,0,1:T(8,128)(2,1)S(1)}, u32[]{:S(2)}, u32[]{:S(2)}) %all-to-all-start) | async-done | bytes 2097184 | tf_op jit(solution)/shard_map/all_to_all | solution.py:128
  121.2 16.3 %fusion.133 = bf16[1024,1024]{1,0:T(8,128)(2,1)} fusion(), kind=kLoop, calls=%fused_computation.220 | loop fusion | flops 15728640 | bytes 2097152 | tf_op jit(solution)/shard_map/convert.59 | solution.py:446
  151.2 14.9 %all-to-all-done.3 = bf16[4,8,2,2,16,1024]{5,4,1,3,2,0:T(8,128)(2,1)} async-done(((bf16[4,8,2,2,16,1024]{5,4,1,3,2,0:T(8,128)(2,1)}), bf16[4,8,2,2,16,1024]{5,4,1,3,2,0:T(8,128)(2,1)}, u32[]{:S(2)}, u32[]{:S(2)}) %all-to-all-start.3) | async-done | bytes 4194336 | tf_op jit(solution)/shard_map/all_to_all | solution.py:89
  185.3 5.7 subtract_convert_fusion.3
  206.6 6.1 fusion.79
  219.4 5.0 fusion.208
  239.9 5.7 convolution_bitcast_fusion
  245.6 8.3 %fusion.33 = (bf16[1,512,2048]{2,1,0:T(8,128)(2,1)S(1)}, bf16[1,512,2048]{2,1,0:T(8,128)(2,1)S(1)}, f32[1,512,2048]{2,1,0:T(8,128)}, f32[1,512,2048]{2,1,0:T(8,128)}) fusion(bf16[64,8,2048]{2,0,1:T(8,128)(2,1)} %all-to-all-done.5, f32[2048]{0:T(1024)S(1)} %bitcast.328, f32[512]{0:T(512)S(1)} %bitcast.352, f32[2,512,2048]{2,1,0:T(8,128)} %convolution_bitcast_fusion, ...), kind=kLoop, calls=%fused_computation.65 | loop fusion | flops 14680064 | bytes 23080960 | tf_op jit(solution)/shard_map/convert_element_type | solution.py:181
  256.0 7.0 %fusion.221 = (bf16[512,2048]{1,0:T(8,128)(2,1)S(1)}, f32[512,2048]{1,0:T(8,128)}) fusion(f32[512]{0:T(512)S(1)} %add.410, f32[512,2048]{1,0:T(8,128)S(1)} %copy-done.4, f32[512]{0:T(512)S(1)} %mul.1224, f32[512]{0:T(512)S(1)} %mul.1255, f32[512,1024]{1,0:T(8,128)S(1)} %copy-done.65, f32[512,1024]{1,0:T(8,128)S(1)} %copy-done.67, ...), kind=kOutput, calls=%fused_computation.374 | convolution fusion | flops 2175795200 | bytes 19929088 | tf_op jit(solution)/shard_map/jch,cjt->ht/dot_general | solution.py:186
  273.1 5.1 fusion.98
  291.4 6.4 %fusion.222 = (bf16[512,2048]{1,0:T(8,128)(2,1)S(1)}, f32[512,2048]{1,0:T(8,128)}) fusion(f32[512,2048]{1,0:T(8,128)S(1)} %copy-done.34, bf16[512,2,512]{0,2,1:T(8,128)(2,1)S(1)} %copy-done.74, bf16[1,512,2048]{2,1,0:T(8,128)(2,1)S(1)} %fusion.81, bf16[1,512,2048]{2,1,0:T(8,128)(2,1)S(1)} %get-tuple-element.124), kind=kOutput, calls=%fused_computation.375 | convolution fusion | flops 2170552320 | bytes 15728640 | tf_op jit(solution)/shard_map/jch,cjt->ht/dot_general | solution.py:186
  304.6 7.4 %fusion.146 = bf16[512,2,512]{0,2,1:T(8,128)(2,1)} fusion(bf16[1,512,2048]{2,1,0:T(8,128)(2,1)} %copy-done.16, bf16[1,512,2048]{2,1,0:T(8,128)(2,1)S(1)} %get-tuple-element.136, f32[512,1024]{1,0:T(8,128)} %copy-done.64, f32[512,1024]{1,0:T(8,128)} %copy-done.66, f32[512,2048]{1,0:T(8,128)S(1)} %copy-done.4, f32[512]{0:T(512)S(1)} %mul.1255, ...), kind=kOutput, calls=%fused_computation.237 | convolution fusion | flops 2171076608 | bytes 13637632 | tf_op jit(solution)/shard_map/cjt,ht->jch/dot_general | solution.py:185
  315.4 6.1 fusion.149
  339.6 5.1 fusion.110
  353.4 6.2 %all-to-all-start.9 = ((f32[8,1,640]{2,1,0:T(1,128)}), f32[8,1,640]{2,1,0:T(1,128)S(1)}, u32[]{:S(2)}, u32[]{:S(2)}) async-start(f32[8,1,640]{2,1,0:T(1,128)} %reshape.629), calls=%async_computation.9 | async-start | bytes 40960 | tf_op jit(solution)/shard_map/all_to_all | solution.py:213
  359.6 5.4 fusion.140
  372.7 5.0 all-to-all-start.7
  377.9 6.7 %fusion.57 = bf16[8,64,2048]{2,1,0:T(8,128)(2,1)} fusion(bf16[64,8,2048]{2,0,1:T(8,128)(2,1)S(1)} %copy-done.1, f32[8,64,2048]{2,1,0:T(8,128)} %get-tuple-element.129, f32[8,64,2048]{2,1,0:T(8,128)} %bitcast.295, f32[8,64,2048]{2,1,0:T(8,128)} %bitcast.296, f32[8,64]{1,0:T(8,128)S(1)} %add.424, f32[8,64]{1,0:T(8,128)S(1)} %add.421, f32[2048]{0:T(1024)S(1)} %bitcast.331), kind=kLoop, calls=%fused_computation.99 | loop fusion | flops 11534336 | bytes 16789504 | tf_op jit(solution)/shard_map/convert_element_type | solution.py:169
  384.6 41.3 %all-to-all-done.7 = bf16[8,4,2,2,16,1024]{5,4,0,3,2,1:T(8,128)(2,1)} async-done(((bf16[8,4,2,2,16,1024]{5,4,0,3,2,1:T(8,128)(2,1)}), bf16[8,4,2,2,16,1024]{5,4,0,3,2,1:T(8,128)(2,1)}, u32[]{:S(2)}, u32[]{:S(2)}) %all-to-all-start.7) | async-done | bytes 4194336 | tf_op jit(solution)/shard_map/all_to_all | solution.py:208
  425.9 6.0 all-to-all-start.4
  431.9 7.2 %fusion.37 = bf16[512,2048]{1,0:T(8,128)(2,1)} fusion(bf16[64,8,2048]{2,0,1:T(8,128)(2,1)} %all-to-all-done.5, f32[512,2048]{1,0:T(8,128)} %copy-done.5, bf16[64,8,2048]{2,0,1:T(8,128)(2,1)S(1)} %copy-done.1, f32[512,2048]{1,0:T(8,128)} %get-tuple-element.123, f32[2048]{0:T(1024)S(1)} %broadcast_multiply_fusion, f32[2048]{0:T(1024)S(1)} %broadcast_multiply_fusion.1, ...), kind=kLoop, calls=%fused_computation.69 | loop fusion | flops 12582912 | bytes 14714880 | tf_op jit(solution)/shard_map/convert_element_type | solution.py:203
  439.2 40.9 %all-to-all-done.4 = bf16[8,64,2048]{2,1,0:T(8,128)(2,1)} async-done(((bf16[8,64,2048]{2,1,0:T(8,128)(2,1)}), bf16[8,64,2048]{2,1,0:T(8,128)(2,1)}, u32[]{:S(2)}, u32[]{:S(2)}) %all-to-all-start.4) | async-done | bytes 2097184 | tf_op jit(solution)/shard_map/all_to_all | solution.py:170
  495.5 36.8 %all-to-all-done.6 = bf16[8,64,2048]{2,1,0:T(8,128)(2,1)} async-done(((bf16[8,64,2048]{2,1,0:T(8,128)(2,1)}), bf16[8,64,2048]{2,1,0:T(8,128)(2,1)}, u32[]{:S(2)}, u32[]{:S(2)}) %all-to-all-start.6) | async-done | bytes 2097184 | tf_op jit(solution)/shard_map/all_to_all | solution.py:204
  545.7 16.6 %all-to-all-done.8 = bf16[8,2,2,16,1024]{4,3,2,1,0:T(8,128)(2,1)} async-done(((bf16[8,2,2,16,1024]{4,3,2,1,0:T(8,128)(2,1)}), bf16[8,2,2,16,1024]{4,3,2,1,0:T(8,128)(2,1)}, u32[]{:S(2)}, u32[]{:S(2)}) %all-to-all-start.8) | async-done | bytes 1048608 | tf_op jit(solution)/shard_map/all_to_all | solution.py:210
  565.0 17.8 %multiply_reduce_fusion = (f32[2,16,64,32]{2,3,1,0:T(8,128)S(1)}, f32[2,16,64,32]{2,3,1,0:T(8,128)S(1)}, f32[2,16,64,32]{2,3,1,0:T(8,128)S(1)}, f32[2,16,64,32]{2,3,1,0:T(8,128)S(1)}) fusion(f32[2,16,32,32]{3,2,1,0:T(8,128)S(1)} %iota_multiply_fusion, f32[2,16,64,32]{2,3,1,0:T(8,128)S(1)} %copy-done.32, f32[2,16,32,32]{3,2,1,0:T(8,128)} %copy-done.33, ...), kind=kLoop, calls=%fused_computation | loop fusion | flops 16515072 | bytes 1835008 | tf_op jit(solution)/shard_map/reduce_sum | solution.py:66
  597.6 5.8 all-to-all-done.10
  (412 shorter events, 224.7 us)
Async XLA Ops:
  2.1 23.4 %all-to-all-start.1 = ((f32[8,1,640]{2,1,0:T(1,128)}), f32[8,1,640]{2,1,0:T(1,128)S(1)}, u32[]{:S(2)}, u32[]{:S(2)}) async-start(f32[8,1,640]{2,1,0:T(1,128)} %reshape.627), calls=%async_computation.1 | async-start | bytes 40960 | tf_op jit(solution)/shard_map/all_to_all | solution.py:89
  26.6 31.4 %all-to-all-start.2 = ((bf16[8,2,2,16,1024]{4,3,2,1,0:T(8,128)(2,1)}), bf16[8,2,2,16,1024]{4,3,2,1,0:T(8,128)(2,1)S(1)}, u32[]{:S(2)}, u32[]{:S(2)}) async-start(bf16[8,2,2,16,1024]{4,3,2,1,0:T(8,128)(2,1)} %broadcast_in_dim.243), calls=%async_computation.2 | async-start | bytes 2097152 | tf_op jit(solution)/shard_map/all_to_all | solution.py:89
  32.6 29.5 %copy-start.119 = (s32[16]{0:T(128)S(1)}, s32[16]{0:T(128)}, u32[]{:S(2)}) copy-start(s32[16]{0:T(128)} %param.20) | copy-start | bytes 196
  58.1 52.2 %all-to-all-start = ((bf16[64,8,2048]{2,0,1:T(8,128)(2,1)}), bf16[64,8,2048]{2,0,1:T(8,128)(2,1)S(1)}, u32[]{:S(2)}, u32[]{:S(2)}) async-start(bf16[64,8,2048]{2,0,1:T(8,128)(2,1)} %bitcast.307), calls=%async_computation | async-start | bytes 4194304 | tf_op jit(solution)/shard_map/all_to_all | solution.py:128
  110.3 96.2 %copy-start = (bf16[64,8,2048]{2,0,1:T(8,128)(2,1)}, bf16[64,8,2048]{2,0,1:T(8,128)(2,1)S(1)}, u32[]{:S(2)}) copy-start(bf16[64,8,2048]{2,0,1:T(8,128)(2,1)S(1)} %all-to-all-done) | copy-start | bytes 6291460
  113.0 53.1 %all-to-all-start.3 = ((bf16[4,8,2,2,16,1024]{5,4,1,3,2,0:T(8,128)(2,1)}), bf16[4,8,2,2,16,1024]{5,4,1,3,2,0:T(8,128)(2,1)}, u32[]{:S(2)}, u32[]{:S(2)}) async-start(bf16[4,8,2,2,16,1024]{5,4,1,3,2,0:T(8,128)(2,1)} %broadcast_in_dim.244), calls=%async_computation.3 | async-start | bytes 8388608 | tf_op jit(solution)/shard_map/all_to_all | solution.py:89
  139.0 67.5 %copy-start.103 = (f32[512]{0:T(512)}, f32[512]{0:T(512)S(1)}, u32[]{:S(2)}) copy-start(f32[512]{0:T(512)S(1)} %add.378) | copy-start | bytes 6148
  139.1 67.4 %copy-start.100 = (f32[512]{0:T(512)}, f32[512]{0:T(512)S(1)}, u32[]{:S(2)}) copy-start(f32[512]{0:T(512)S(1)} %mul.1152) | copy-start | bytes 6148
  140.2 66.3 %copy-start.105 = (f32[512]{0:T(512)}, f32[512]{0:T(512)S(1)}, u32[]{:S(2)}) copy-start(f32[512]{0:T(512)S(1)} %mul.1290) | copy-start | bytes 6148
  141.1 65.4 %copy-start.80 = (f32[2048]{0:T(1024)}, f32[2048]{0:T(1024)S(1)}, u32[]{:S(2)}) copy-start(f32[2048]{0:T(1024)S(1)} %get-tuple-element.191) | copy-start | bytes 24580
  141.1 65.4 %copy-start.82 = (f32[2048]{0:T(1024)}, f32[2048]{0:T(1024)S(1)}, u32[]{:S(2)}) copy-start(f32[2048]{0:T(1024)S(1)} %get-tuple-element.192) | copy-start | bytes 24580
  166.1 79.5 %all-to-all-start.5 = ((bf16[64,8,2048]{2,0,1:T(8,128)(2,1)}), bf16[64,8,2048]{2,0,1:T(8,128)(2,1)}, u32[]{:S(2)}, u32[]{:S(2)}) async-start(bf16[64,8,2048]{2,0,1:T(8,128)(2,1)} %bitcast.306), calls=%async_computation.5 | async-start | bytes 4194304 | tf_op jit(solution)/shard_map/all_to_all | solution.py:129
  353.4 19.3 %all-to-all-start.9 = ((f32[8,1,640]{2,1,0:T(1,128)}), f32[8,1,640]{2,1,0:T(1,128)S(1)}, u32[]{:S(2)}, u32[]{:S(2)}) async-start(f32[8,1,640]{2,1,0:T(1,128)} %reshape.629), calls=%async_computation.9 | async-start | bytes 40960 | tf_op jit(solution)/shard_map/all_to_all | solution.py:213
  372.7 53.3 %all-to-all-start.7 = ((bf16[8,4,2,2,16,1024]{5,4,0,3,2,1:T(8,128)(2,1)}), bf16[8,4,2,2,16,1024]{5,4,0,3,2,1:T(8,128)(2,1)}, u32[]{:S(2)}, u32[]{:S(2)}) async-start(bf16[8,4,2,2,16,1024]{5,4,0,3,2,1:T(8,128)(2,1)} %copy.209), calls=%async_computation.7 | async-start | bytes 8388608 | tf_op jit(solution)/shard_map/all_to_all | solution.py:208
  425.9 54.2 %all-to-all-start.4 = ((bf16[8,64,2048]{2,1,0:T(8,128)(2,1)}), bf16[8,64,2048]{2,1,0:T(8,128)(2,1)}, u32[]{:S(2)}, u32[]{:S(2)}) async-start(bf16[8,64,2048]{2,1,0:T(8,128)(2,1)} %fusion.57), calls=%async_computation.4 | async-start | bytes 4194304 | tf_op jit(solution)/shard_map/all_to_all | solution.py:170
  439.2 45.3 %copy-start.111 = (f32[2,2,64]{2,1,0:T(2,128)S(1)}, f32[2,2,64]{2,1,0:T(2,128)}, u32[]{:S(2)}) copy-start(f32[2,2,64]{2,1,0:T(2,128)} %param.26) | copy-start | bytes 3076
  439.2 45.3 %copy-start.114 = (f32[2,64]{1,0:T(2,128)S(1)}, f32[2,64]{1,0:T(2,128)}, u32[]{:S(2)}) copy-start(f32[2,64]{1,0:T(2,128)} %param.24) | copy-start | bytes 1540
  439.2 45.3 %copy-start.115 = (f32[2,64]{1,0:T(2,128)S(1)}, f32[2,64]{1,0:T(2,128)}, u32[]{:S(2)}) copy-start(f32[2,64]{1,0:T(2,128)} %param.25) | copy-start | bytes 1540
  439.2 45.3 %copy-start.116 = (f32[2,64]{1,0:T(2,128)S(1)}, f32[2,64]{1,0:T(2,128)}, u32[]{:S(2)}) copy-start(f32[2,64]{1,0:T(2,128)} %param.23) | copy-start | bytes 1540
  439.2 45.3 %copy-start.117 = (f32[2,64]{1,0:T(2,128)S(1)}, f32[2,64]{1,0:T(2,128)}, u32[]{:S(2)}) copy-start(f32[2,64]{1,0:T(2,128)} %param.22) | copy-start | bytes 1540
  480.1 52.2 %all-to-all-start.6 = ((bf16[8,64,2048]{2,1,0:T(8,128)(2,1)}), bf16[8,64,2048]{2,1,0:T(8,128)(2,1)}, u32[]{:S(2)}, u32[]{:S(2)}) async-start(bf16[8,64,2048]{2,1,0:T(8,128)(2,1)} %bitcast.308), calls=%async_computation.6 | async-start | bytes 4194304 | tf_op jit(solution)/shard_map/all_to_all | solution.py:204
  493.2 43.6 %copy-start.24 = (bf16[64,16384]{1,0:T(8,128)(2,1)S(1)}, bf16[64,16384]{1,0:T(8,128)(2,1)}, u32[]{:S(2)}) copy-start(bf16[64,16384]{1,0:T(8,128)(2,1)} %param.19) | copy-start | bytes 6291460
  532.2 30.1 %all-to-all-start.8 = ((bf16[8,2,2,16,1024]{4,3,2,1,0:T(8,128)(2,1)}), bf16[8,2,2,16,1024]{4,3,2,1,0:T(8,128)(2,1)}, u32[]{:S(2)}, u32[]{:S(2)}) async-start(bf16[8,2,2,16,1024]{4,3,2,1,0:T(8,128)(2,1)} %copy.211), calls=%async_computation.8 | async-start | bytes 2097152 | tf_op jit(solution)/shard_map/all_to_all | solution.py:210
  545.7 37.0 %copy-start.85 = (f32[2,16,64]{2,1,0:T(8,128)S(1)}, f32[2,16,64]{2,1,0:T(8,128)}, u32[]{:S(2)}) copy-start(f32[2,16,64]{2,1,0:T(8,128)} %copy-done.84) | copy-start | bytes 24580
  545.7 37.0 %copy-start.89 = (f32[2,16,64]{2,1,0:T(8,128)S(1)}, f32[2,16,64]{2,1,0:T(8,128)}, u32[]{:S(2)}) copy-start(f32[2,16,64]{2,1,0:T(8,128)} %copy-done.88) | copy-start | bytes 24580
  563.8 22.5 %copy-start.90 = (f32[2,64,64]{2,1,0:T(8,128)S(1)}, f32[2,64,64]{2,1,0:T(8,128)}, u32[]{:S(2)}) copy-start(f32[2,64,64]{2,1,0:T(8,128)} %param.29) | copy-start | bytes 98308
  563.8 22.5 %copy-start.91 = (f32[2,64,64]{2,1,0:T(8,128)S(1)}, f32[2,64,64]{2,1,0:T(8,128)}, u32[]{:S(2)}) copy-start(f32[2,64,64]{2,1,0:T(8,128)} %param.30) | copy-start | bytes 98308
  563.8 22.5 %copy-start.93 = (f32[2,16,64]{2,1,0:T(8,128)S(1)}, f32[2,16,64]{2,1,0:T(8,128)}, u32[]{:S(2)}) copy-start(f32[2,16,64]{2,1,0:T(8,128)} %copy-done.92) | copy-start | bytes 24580
  563.9 22.5 %copy-start.94 = (f32[2,64,64]{2,1,0:T(8,128)S(1)}, f32[2,64,64]{2,1,0:T(8,128)}, u32[]{:S(2)}) copy-start(f32[2,64,64]{2,1,0:T(8,128)} %param.27) | copy-start | bytes 98308
  563.9 22.5 %copy-start.97 = (f32[2,16,64]{2,1,0:T(8,128)S(1)}, f32[2,16,64]{2,1,0:T(8,128)}, u32[]{:S(2)}) copy-start(f32[2,16,64]{2,1,0:T(8,128)} %copy-done.96) | copy-start | bytes 24580
  564.9 28.1 %copy-start.25 = (bf16[64,16384]{1,0:T(8,128)(2,1)S(1)}, bf16[64,16384]{1,0:T(8,128)(2,1)}, u32[]{:S(2)}) copy-start(bf16[64,16384]{1,0:T(8,128)(2,1)} %param.21) | copy-start | bytes 6291460
  589.5 13.8 %all-to-all-start.10 = ((f32[4,1,41632]{2,1,0:T(1,128)}), f32[4,1,41632]{2,1,0:T(1,128)S(1)}, u32[]{:S(2)}, u32[]{:S(2)}) async-start(f32[4,1,41632]{2,1,0:T(1,128)} %broadcast_in_dim.249), calls=%async_computation.10 | async-start | bytes 1335296 | tf_op jit(solution)/shard_map/all_to_all | solution.py:89
  (101 other events, 595.1 us)

commit v2 on v0

--- a/solution.py
+++ b/solution.py
@@ -1,13 +1,1136 @@
+import functools
 import math
 
 import jax
 import jax.numpy as jnp
+import numpy as np
 from jax import lax
+from jax.experimental import pallas as pl
+from jax.experimental.pallas import tpu as pltpu
 from jax.sharding import PartitionSpec as P
 
 LAYERS = 2
 BUCKET = 1024
 STEP = 10
+
+
+QUARTER = BUCKET // 4
+HALF_ROOT = math.sqrt(0.5)
+STEP_ROWS = 16
+UNROLL = 4
+CONV_ROWS = 512
+CHUNK_ROWS = 256
+MAT_ROWS = 512
+LIN_ROWS = 256
+ROOM = 59 * 2**20
+GROUPS = ((0, 256), (256, 256), (512, 512), (1024, 512), (1536, 512))
+GELU_A = math.sqrt(2.0 / math.pi)
+GELU_B = GELU_A * 0.044715
+
+
+def transform_tables():
+    place = np.arange(QUARTER)[:, None]
+    to_spec, to_time = [], []
+    for residue in (0, 4):
+        bins = np.arange(QUARTER // 2)[None, :]
+        turn = (8 * bins + residue) * place % (2 * BUCKET) * (math.pi / BUCKET)
+        cosine, sine = np.cos(turn), -np.sin(turn)
+        weights = np.full_like(cosine, 2.0)
+        if residue == 0:
+            sine[:, 0] = 1 - 2 * (place[:, 0] % 2)
+            weights[:, 0] = 1.0
+        to_spec.append(np.concatenate([cosine, sine], 1))
+        to_time.append(np.concatenate([cosine * weights, sine * weights], 1).T / (2 * BUCKET))
+    for residue in (1, 2, 3):
+        bins = np.arange(QUARTER)[None, :]
+        turn = (8 * bins + residue) * place % (2 * BUCKET) * (math.pi / BUCKET)
+        cosine, sine = np.cos(turn), np.sin(turn)
+        sign = 1.0 if residue == 3 else -1.0
+        to_spec.append(np.block([[cosine, -sine], [sign * sine, sign * cosine]]))
+        to_time.append(np.block([[cosine.T, sine.T], [-sine.T, cosine.T]]) / BUCKET)
+    small = [np.stack(side[:2]).astype(jnp.bfloat16) for side in (to_spec, to_time)]
+    large = [np.stack(side[2:]).astype(jnp.bfloat16) for side in (to_spec, to_time)]
+    return small[0], large[0], small[1], large[1]
+
+
+def quarters(x):
+    return [x[:, q * QUARTER : (q + 1) * QUARTER] for q in range(4)]
+
+
+def fold(x0, x1, x2, x3):
+    even, odd = x0 + x2, x1 + x3
+    diff = x1 - x3
+    turned, tilted = diff * HALF_ROOT, odd * HALF_ROOT
+    return even + odd, even - odd, x0 + turned, x2 + tilted, x0 - x2, diff, x0 - turned, x2 - tilted
+
+
+def unfold(y0, y4, r1, i1, r2, i2, r3, i3):
+    even, odd = y0 + y4, y0 - y4
+    r_sum, r_diff, i_sum, i_diff = r1 + r3, r1 - r3, i1 + i3, i1 - i3
+    return (
+        even + (r2 + r_sum),
+        odd - i2 + (r_diff - i_sum) * HALF_ROOT,
+        even - (r2 + i_diff),
+        odd + i2 - (r_diff + i_sum) * HALF_ROOT,
+    )
+
+
+def dot(a, b):
+    return jnp.dot(a, b, preferred_element_type=jnp.float32)
+
+
+def product(a, b, first, conj):
+    half = a.shape[1] // 2
+    ar, ai, br, bi = a[:, :half], a[:, half:], b[:, :half], b[:, half:]
+    cross = ai * bi
+    if conj:
+        imag = ar * bi - ai * br
+    else:
+        imag = ar * bi + ai * br
+    if first:
+        lone = lax.broadcasted_iota(jnp.int32, cross.shape, 1) == 0
+        imag = jnp.where(lone, cross, imag)
+        cross = jnp.where(lone, 0.0, cross)
+    real = ar * br + cross if conj else ar * br - cross
+    return jnp.concatenate([real, imag], 1)
+
+
+def table_of(small, large, group):
+    return small[group] if group < 2 else large[group - 2]
+
+
+def put_folded(dest, rows, parts):
+    lower = pl.ds(rows.start + dest.shape[0] // 2, rows.size)
+    for k, part in enumerate(parts):
+        dest[rows if k < 4 else lower, k % 4 * QUARTER : (k % 4 + 1) * QUARTER] = part.astype(dest.dtype)
+
+
+def get_folded(src, rows, at, width):
+    if at >= BUCKET:
+        rows, at = pl.ds(rows.start + src.shape[0] // 2, rows.size), at - BUCKET
+    return src[rows, at : at + width]
+
+
+def get_unfolded(src, rows):
+    return unfold(*[src[rows, k * QUARTER : (k + 1) * QUARTER] for k in range(8)])
+
+
+def steps(total, size, body):
+    def one(k, carry):
+        body(pl.ds(pl.multiple_of(k * size, size), size), k)
+        return carry
+
+    lax.fori_loop(0, total // size, one, 0, unroll=UNROLL if size == STEP_ROWS else 1)
+
+
+def kernel_spectrum(ker, folded, spec, small, large, chunk):
+    chans = ker.shape[0]
+
+    def fold_rows(rows, _):
+        put_folded(folded, rows, fold(*quarters(ker[rows, :].astype(jnp.float32))))
+
+    steps(chans, STEP_ROWS, fold_rows)
+
+    def transform_rows(rows, _):
+        for g, (at, width) in enumerate(GROUPS):
+            spec[rows, at : at + width] = dot(get_folded(folded, rows, at, width), table_of(small, large, g))
+
+    steps(chans, chunk, transform_rows)
+
+
+def token_stats(stream, chans):
+    def add(k, carry):
+        v = stream[pl.ds(pl.multiple_of(k * STEP_ROWS, STEP_ROWS), STEP_ROWS), :].astype(jnp.float32)
+        return carry + v[:8] + v[8:]
+
+    total = lax.fori_loop(0, chans // STEP_ROWS, add, jnp.zeros((8, BUCKET), jnp.float32), unroll=UNROLL)
+    mean_val = jnp.sum(total, 0, keepdims=True) / chans
+
+    def add_square(k, carry):
+        v = stream[pl.ds(pl.multiple_of(k * STEP_ROWS, STEP_ROWS), STEP_ROWS), :].astype(jnp.float32) - mean_val
+        v = v * v
+        return carry + v[:8] + v[8:]
+
+    total = lax.fori_loop(0, chans // STEP_ROWS, add_square, jnp.zeros((8, BUCKET), jnp.float32), unroll=UNROLL)
+    return mean_val, lax.rsqrt(jnp.sum(total, 0, keepdims=True) / chans + 1e-05)
+
+
+def lanes(x):
+    total = x[:, :128]
+    for k in range(1, x.shape[1] // 128):
+        total = total + x[:, k * 128 : (k + 1) * 128]
+    return total
+
+
+GAIN, SHIFT, SKIP, BIAS_IN, BIAS_VAL = range(5)
+MESH = pl.DeviceIdType.MESH
+
+
+def bit_of(index, place):
+    return lax.rem(lax.div(index, 1 << place), 2)
+
+
+def flip(index, place):
+    return index + (1 - 2 * bit_of(index, place)) * (1 << place)
+
+
+def peers_of(n_chan):
+    me, row = lax.axis_index("chan"), lax.axis_index("batch")
+    others = []
+    for k in range(1, n_chan):
+        other = me
+        for place in range(n_chan.bit_length() - 1):
+            other = flip(other, place) if k >> place & 1 else other
+        others.append(other)
+    return me, row, others
+
+
+def greet(targets):
+    barrier = pltpu.get_barrier_semaphore()
+    for target in targets:
+        pl.semaphore_signal(barrier, inc=1, device_id=target, device_id_type=MESH)
+    pl.semaphore_wait(barrier, len(targets))
+
+
+LANES = 128
+POWERS = 8
+LOW_STAGE = 1
+
+
+def halving(n_chan, n_batch):
+    me, row = lax.axis_index("chan"), lax.axis_index("batch")
+    chan_bits, batch_bits = n_chan.bit_length() - 1, n_batch.bit_length() - 1
+    out = [(bit_of(me, k), (row, flip(me, k))) for k in reversed(range(chan_bits))]
+    return out + [(bit_of(row, k), (flip(row, k), me)) for k in reversed(range(batch_bits))]
+
+
+def doubled_powers(decay_rate, turn_rate):
+    spans = [2.0**k for k in range(BUCKET.bit_length() - 1)]
+    sizes = [jnp.exp(-span * decay_rate) for span in spans]
+    total, moment = jnp.ones_like(decay_rate), jnp.zeros_like(decay_rate)
+    for span, size in zip(spans, sizes):
+        moment = moment * (1.0 + size) + span * size * total
+        total = total * (1.0 + size)
+    powers = []
+    for span, size in list(zip(spans, sizes))[:POWERS]:
+        powers += [size * jnp.cos(span * turn_rate), size * jnp.sin(span * turn_rate)]
+    return powers, total, moment
+
+
+def times(a, b):
+    return a[0] * b[0] - a[1] * b[1], a[0] * b[1] + a[1] * b[0]
+
+
+def columns_of(rows):
+    pad = jnp.zeros((LANES - rows.shape[0], LANES), jnp.float32)
+    return jnp.transpose(jnp.concatenate([rows, pad], 0))
+
+
+def near_powers(params):
+    lane = lax.broadcasted_iota(jnp.int32, (params.shape[0], LANES), 1)
+    value = None
+    for k in range(POWERS - 1):
+        power = params[:, 2 * k : 2 * k + 1], params[:, 2 * k + 1 : 2 * k + 2]
+        here = (lane & (1 << k)) != 0
+        if value is None:
+            value = jnp.where(here, power[0], 1.0), jnp.where(here, power[1], 0.0)
+        else:
+            moved = times(value, power)
+            value = jnp.where(here, moved[0], value[0]), jnp.where(here, moved[1], value[1])
+    far = params[:, 2 * POWERS - 2 : 2 * POWERS - 1], params[:, 2 * POWERS - 1 : 2 * POWERS]
+    return value, tuple(jnp.broadcast_to(f, lane.shape) for f in far)
+
+
+def halves(x):
+    half = x.shape[0] // 2
+    return [jnp.sum(x[:half], 0, keepdims=True), jnp.sum(x[half:], 0, keepdims=True)]
+
+
+def kernel_rows(params):
+    value, far = near_powers(params)
+    value = times(value, (params[:, 2 * POWERS : 2 * POWERS + 1], params[:, 2 * POWERS + 1 : 2 * POWERS + 2]))
+    out = [halves(value[0])]
+    for _ in range(1, BUCKET // LANES):
+        value = times(value, far)
+        out.append(halves(value[0]))
+    return [jnp.concatenate([row[c] for row in out], 0) for c in range(2)]
+
+
+def state_rows(params, grads):
+    value, far = near_powers(params)
+    half = params.shape[0] // 2
+    place = lax.broadcasted_iota(jnp.int32, (1, LANES), 1).astype(jnp.float32)
+    plain = weighted = None
+    for k in reversed(range(BUCKET // LANES)):
+        rows = [g[:, k * LANES : (k + 1) * LANES] for g in grads]
+        g = jnp.concatenate([jnp.broadcast_to(r, (half, LANES)) for r in rows], 0)
+        w = jnp.concatenate([jnp.broadcast_to(r * (place + float(k * LANES)), (half, LANES)) for r in rows], 0)
+        if plain is None:
+            plain, weighted = (g, jnp.zeros_like(g)), (w, jnp.zeros_like(g))
+        else:
+            plain, weighted = times(plain, far), times(weighted, far)
+            plain, weighted = (plain[0] + g, plain[1]), (weighted[0] + w, weighted[1])
+    cols = times(plain, value) + times(weighted, value)
+    lane = lax.broadcasted_iota(jnp.int32, value[0].shape, 1)
+    out = jnp.zeros_like(value[0])
+    for k, col in enumerate(cols):
+        out = jnp.where(lane == k, jnp.sum(col, 1, keepdims=True), out)
+    return jnp.transpose(out)[:8]
+
+
+def remote(src, dst, send, recv, target):
+    return pltpu.make_async_remote_copy(
+        src_ref=src, dst_ref=dst, send_sem=send, recv_sem=recv, device_id=target, device_id_type=MESH
+    )
+
+
+def halving_bits(n_chan, n_batch):
+    return n_chan.bit_length() + n_batch.bit_length() - 2
+
+
+def to_tokens(src, dst, send, recv, own_sem):
+    own, toks = src.shape[0], dst.shape[1]
+    n_chan = dst.shape[0] // own
+    me, row, others = peers_of(n_chan)
+    rows = pl.ds(pl.multiple_of(me * own, own), own)
+    copies = [pltpu.make_async_copy(src.at[:, pl.ds(pl.multiple_of(me * toks, toks), toks)], dst.at[rows], own_sem)]
+    for k, other in enumerate(others):
+        copies.append(
+            pltpu.make_async_remote_copy(
+                src_ref=src.at[:, pl.ds(pl.multiple_of(other * toks, toks), toks)],
+                dst_ref=dst.at[rows],
+                send_sem=send.at[k],
+                recv_sem=recv.at[k],
+                device_id=(row, other),
+                device_id_type=MESH,
+            )
+        )
+    return copies
+
+
+def to_channels(src, dst, send, recv, own_sem):
+    own, toks = dst.shape[0], src.shape[1]
+    n_chan = src.shape[0] // own
+    me, row, others = peers_of(n_chan)
+    cols = pl.ds(pl.multiple_of(me * toks, toks), toks)
+    copies = [pltpu.make_async_copy(src.at[pl.ds(pl.multiple_of(me * own, own), own)], dst.at[:, cols], own_sem)]
+    for k, other in enumerate(others):
+        copies.append(
+            pltpu.make_async_remote_copy(
+                src_ref=src.at[pl.ds(pl.multiple_of(other * own, own), own)],
+                dst_ref=dst.at[:, cols],
+                send_sem=send.at[k],
+                recv_sem=recv.at[k],
+                device_id=(row, other),
+                device_id_type=MESH,
+            )
+        )
+    return copies
+
+
+def forward_kernel(
+    n_chan, first, mask, ker, weight, vec, fs, fl, ts, tl, cot_own,
+    cot, delta_out, stat, hat_out, pre_out, act_out, sigma_out, slope_out, spec_out,
+    stream, hat, ker_spec, folded, mixed, send, recv, own_sem,
+):
+    layer, seq = pl.program_id(0), pl.program_id(1)
+    chans = first.shape[0]
+    stream = stream.at[seq]
+
+    @pl.when((layer == 0) & (seq == 0))
+    def _():
+        me, row, others = peers_of(n_chan)
+        greet([(row, other) for other in others])
+        for copy in to_tokens(cot_own, cot, send, recv, own_sem):
+            copy.start()
+
+    @pl.when(layer == 0)
+    def _():
+        def widen(rows, _):
+            stream[rows, :] = first[rows, :].astype(jnp.float32)
+
+        steps(chans, STEP_ROWS, widen)
+
+    @pl.when(seq == 0)
+    def _():
+        kernel_spectrum(ker.at[0], folded, ker_spec, fs, fl, CONV_ROWS)
+
+    mean_val, inv_std = token_stats(stream, chans)
+    stat[0, 0, 0:1, :] = mean_val
+    stat[0, 0, 1:2, :] = inv_std
+
+    def normalise(rows, _):
+        v = (stream[rows, :] - stat[0, 0, 0:1, :]) * stat[0, 0, 1:2, :]
+        hat[rows, :] = v
+        hat_out[0, rows, :] = v.astype(hat_out.dtype)
+        v = v * vec[0, rows, GAIN : GAIN + 1] + vec[0, rows, SHIFT : SHIFT + 1]
+        put_folded(folded, rows, fold(*quarters(v)))
+
+    steps(chans, STEP_ROWS, normalise)
+
+    def convolve(rows, _):
+        for g, (at, width) in enumerate(GROUPS):
+            spec = dot(get_folded(folded, rows, at, width), table_of(fs, fl, g))
+            spec_out[0, rows, at : at + width] = spec.astype(jnp.bfloat16)
+            both = product(ker_spec[rows, at : at + width], spec, g == 0, False)
+            mixed[rows, at : at + width] = dot(both.astype(jnp.bfloat16), table_of(ts, tl, g))
+
+    steps(chans, CONV_ROWS, convolve)
+
+    def activate(rows, _):
+        gain, shift, skip = [vec[0, rows, k : k + 1] for k in (GAIN, SHIFT, SKIP)]
+        gain, shift = gain * skip, shift * skip
+        for q, part in enumerate(get_unfolded(mixed, rows)):
+            cols = slice(q * QUARTER, (q + 1) * QUARTER)
+            pre = part + (gain * hat[rows, cols] + shift)
+            pre_out[0, rows, cols] = pre.astype(pre_out.dtype)
+            soft = jnp.tanh(pre * (GELU_A + GELU_B * (pre * pre)))
+            act_out[0, rows, cols] = (0.5 * pre * (1.0 + soft)).astype(jnp.bfloat16)
+
+    steps(chans, STEP_ROWS, activate)
+
+    block = 2 * LIN_ROWS
+    for t in range(4):
+        cols = slice(t * QUARTER, (t + 1) * QUARTER)
+
+        def linear(rows, k, cols=cols):
+            mixed[:block, :QUARTER] = dot(weight[0, rows, :], act_out[0, :, cols])
+            for o in range(LIN_ROWS // 16):
+                at = pl.ds(pl.multiple_of(k * LIN_ROWS + o * 16, 16), 16)
+                gate = mixed[o * 32 : o * 32 + 16, :QUARTER] + vec[0, at, BIAS_IN : BIAS_IN + 1]
+                value = mixed[o * 32 + 16 : o * 32 + 32, :QUARTER] + vec[0, at, BIAS_VAL : BIAS_VAL + 1]
+                sigma = 0.5 * jnp.tanh(0.5 * value) + 0.5
+                gated = gate * sigma
+                sigma_out[0, at, cols] = sigma.astype(sigma_out.dtype)
+                slope_out[0, at, cols] = (gated - gated * sigma).astype(slope_out.dtype)
+                moved = stream[at, cols] + mask[0, :, cols] * gated
+                stream[at, cols] = moved
+                delta_out[at, cols] = (moved - first[at, cols].astype(jnp.float32)).astype(jnp.bfloat16)
+
+        steps(2 * chans, block, linear)
+
+    @pl.when((layer == pl.num_programs(0) - 1) & (seq == pl.num_programs(1) - 1))
+    def _():
+        for copy in to_tokens(cot_own, cot, send, recv, own_sem):
+            copy.wait()
+
+
+def whole(a):
+    return pl.BlockSpec(a.shape, lambda i, s, n=a.ndim: (0,) * n, pipeline_mode=pl.Buffered(1))
+
+
+ANYWHERE = pl.BlockSpec(memory_space=pl.ANY)
+
+
+def forward_pass(first, mask, kers, weights, vecs, tables, cot_own, n_chan):
+    chans, toks = first.shape
+    seqs, layers = toks // BUCKET, kers.shape[0]
+    shape, low = jax.ShapeDtypeStruct, jnp.bfloat16
+    layered = lambda a: pl.BlockSpec((1,) + a.shape[1:], lambda i, s: (i, 0, 0))
+    saved = pl.BlockSpec((1, chans, BUCKET), lambda i, s: (i, 0, s))
+    return pl.pallas_call(
+        functools.partial(forward_kernel, n_chan),
+        grid=(layers, seqs),
+        in_specs=[
+            pl.BlockSpec((chans, BUCKET), lambda i, s: (0, s)),
+            pl.BlockSpec((1, 1, BUCKET), lambda i, s: (s, 0, 0)),
+            layered(kers), layered(weights), layered(vecs),
+            *[whole(t) for t in tables],
+            ANYWHERE,
+        ],
+        out_specs=[
+            ANYWHERE,
+            pl.BlockSpec((chans, BUCKET), lambda i, s: (0, lax.select(i == layers - 1, s, 0))),
+            pl.BlockSpec((1, 1, 8, BUCKET), lambda i, s: (i, s, 0, 0)),
+            saved, saved, saved, saved, saved,
+            pl.BlockSpec((1, chans, 2 * BUCKET), lambda i, s: (i, 0, s)),
+        ],
+        out_shape=[
+            shape((chans, toks), low),
+            shape((chans, toks), low),
+            shape((layers, seqs, 8, BUCKET), jnp.float32),
+            shape((layers, chans, toks), low),
+            shape((layers, chans, toks), low),
+            shape((layers, chans, toks), low),
+            shape((layers, chans, toks), low),
+            shape((layers, chans, toks), low),
+            shape((layers, chans, 2 * toks), low),
+        ],
+        scratch_shapes=[
+            pltpu.VMEM((seqs, chans, BUCKET), jnp.float32),
+            pltpu.VMEM((chans, BUCKET), jnp.float32),
+            pltpu.VMEM((chans, 2 * BUCKET), jnp.float32),
+            pltpu.VMEM((2 * chans, BUCKET), low),
+            pltpu.VMEM((chans, 2 * BUCKET), jnp.float32),
+            pltpu.SemaphoreType.DMA((n_chan - 1,)),
+            pltpu.SemaphoreType.DMA((n_chan - 1,)),
+            pltpu.SemaphoreType.DMA,
+        ],
+        compiler_params=pltpu.CompilerParams(vmem_limit_bytes=ROOM, collective_id=2, has_side_effects=True),
+        cost_estimate=pl.CostEstimate(flops=24 * 10**9, bytes_accessed=40 * 2**20, transcendentals=0),
+        name="forward_pass",
+    )(first, mask, kers, weights, vecs, *tables, cot_own)
+
+
+def backward_kernel(
+    n_chan, n_batch, first, mask, stat, hat, pre, act, sigma_in, slope_in, spec, ker, weight_t, vec, fs, fl, ts, tl, params,
+    delta_own,
+    delta, back_all, state_all, lin_all, vec_all,
+    back, ker_spec, spec_grad, folded, mixed, sums, pre_grad, back_low, lin_grad, vec_grad, vec_cols, vec_rows, vec_got, vec_own,
+    ker_kept, ker_sums, ker_sent, ker_got, lin_sums, lin_sent, lin_got, low_sent, low_got, ker_final, lin_final, state_own,
+    send, recv, own_sem, back_send, back_recv, back_own, part_send, part_recv, ready, vec_send, vec_recv, vec_sem,
+    all_send, all_recv, all_own,
+):
+    step, seq = pl.program_id(0), pl.program_id(1)
+    layers, seqs = lin_grad.shape[0], back_low.shape[0]
+    chans = first.shape[0]
+    own = chans // n_chan
+    everything = back
+    back = back.at[seq]
+    part = ker_final.shape[1]
+    me, row, others = peers_of(n_chan)
+    rows_of = [lax.rem(row + k, n_batch) for k in range(1, n_batch)]
+    path = list(reversed(halving(n_chan, n_batch)))
+    bits, batch_bits = len(path), n_batch.bit_length() - 1
+    total = 1 << bits
+    core_bit = path[0][0]
+    moves = to_channels(delta_own, delta, send, recv, own_sem)
+
+    def back_moves(k):
+        cols = pl.ds(pl.multiple_of((me * seqs + k) * BUCKET, BUCKET), BUCKET)
+        mine = back_low.at[k, pl.ds(pl.multiple_of(me * own, own), own)]
+        copies = [pltpu.make_async_copy(mine, back_all.at[:, cols], back_own.at[k])]
+        for j, other in enumerate(others):
+            source = back_low.at[k, pl.ds(pl.multiple_of(other * own, own), own)]
+            copies.append(remote(source, back_all.at[:, cols], back_send.at[k, j], back_recv.at[k, j], (row, other)))
+        return copies
+
+    groups = [[0], [1], [2, 3], [4]]
+    count, at, gone = [], [0], 0
+    for group in groups:
+        gone += len(group)
+        count.append(total >> gone)
+        at.append(at[-1] + count[-1] * ((1 << len(group)) - 1))
+    last_stage = len(groups) - 1
+
+    def side(s, mask):
+        chan, batch, index = me, row, 0
+        for t, dim in enumerate(groups[s]):
+            bit = path[dim][0]
+            across = mask >> t & 1
+            index = index + (1 - bit if across else bit) * (1 << t)
+            if across and dim < batch_bits:
+                batch = flip(batch, dim)
+            elif across:
+                chan = flip(chan, dim - batch_bits)
+        return (batch, chan), index
+
+    def masks(s):
+        return range(1, 1 << len(groups[s]))
+
+    def sums_at(s):
+        return sum(count[1 : s + 1])
+
+    def slot(kind, s, mask, sent):
+        first = (mask - 1) * count[s]
+        if kind == 0 or s == 0:
+            return at[s] + first
+        if s == LOW_STAGE:
+            return first
+        return first + at[s] - at[LOW_STAGE + 1] + (0 if sent else at[LOW_STAGE])
+
+    def stage(kind, layer, s, mask):
+        to, got = pl.ds(slot(kind, s, mask, True), count[s]), pl.ds(slot(kind, s, mask, False), count[s])
+        if kind == 0:
+            src, dst = ker_sent.at[to], ker_got.at[got]
+        elif s == 0:
+            src, dst = lin_grad.at[layer, :, 1 - core_bit], lin_got.at[got]
+        elif s == LOW_STAGE:
+            src, dst = low_sent.at[to], low_got.at[got]
+        else:
+            src, dst = lin_sent.at[to], lin_got.at[got]
+        k = at_peer[s] + mask - 1
+        return remote(src, dst, part_send.at[kind, k], part_recv.at[kind, k], side(s, mask)[0])
+
+    at_peer = [0]
+    for s in range(len(groups)):
+        at_peer.append(at_peer[-1] + (1 << len(groups[s])) - 1)
+
+    def begin(kind, layer, s):
+        for mask in masks(s):
+            if layer != layers - 1:
+                pl.semaphore_wait(ready.at[kind, at_peer[s] + mask - 1], 1)
+            stage(kind, layer, s, mask).start()
+
+    def advance(kind, layer, s):
+        for mask in masks(s):
+            stage(kind, layer, s, mask).wait()
+
+        def value(b):
+            if kind == 0:
+                result = ker_kept[b] if s == 0 else ker_sums[sums_at(s - 1) + b]
+            else:
+                result = lin_grad[layer, b, core_bit] if s == 0 else lin_sums[sums_at(s - 1) + b]
+            for mask in masks(s):
+                got = ker_got if kind == 0 else low_got if s == LOW_STAGE else lin_got
+                result = result + got[slot(kind, s, mask, False) + b].astype(jnp.float32)
+            return result
+
+        if s == last_stage:
+            final = ker_final if kind == 0 else lin_final
+            final[layer] = value(0)
+        else:
+            wide = 1 << len(groups[s + 1])
+
+            def one(b, carry):
+                sums = ker_sums if kind == 0 else lin_sums
+                sums[sums_at(s) + b] = value(wide * b + side(s + 1, 0)[1])
+                for mask in masks(s + 1):
+                    moved = value(wide * b + side(s + 1, mask)[1])
+                    to = slot(kind, s + 1, mask, True) + b
+                    if kind == 0:
+                        ker_sent[to] = moved.astype(jnp.bfloat16)
+                    elif s + 1 == LOW_STAGE:
+                        low_sent[to] = moved.astype(jnp.bfloat16)
+                    else:
+                        lin_sent[to] = moved
+                return carry
+
+            lax.fori_loop(0, count[s + 1], one, 0)
+        if layer == layers - 1:
+            for mask in masks(s):
+                there = side(s, mask)[0]
+                pl.semaphore_signal(ready.at[kind, at_peer[s] + mask - 1], inc=1, device_id=there, device_id_type=MESH)
+        if s < last_stage:
+            begin(kind, layer, s + 1)
+
+    def spread(own_ref, everyone, k):
+        copies = [pltpu.make_async_copy(own_ref, everyone.at[row], all_own.at[k])]
+        for j, other in enumerate(rows_of):
+            copies.append(remote(own_ref, everyone.at[row], all_send.at[k, j], all_recv.at[k, j], (other, me)))
+        return copies
+
+    def spreads(kind, layer):
+        if kind == 0:
+            half = pl.ds(layer * part // 2, part // 2)
+            return spread(state_own.at[half], state_all.at[:, half], layer)
+        return spread(lin_final.at[layer], lin_all.at[:, layer], layers + layer)
+
+    def vec_moves():
+        copies = [pltpu.make_async_copy(vec_rows.at[me], vec_got.at[me], vec_sem)]
+        for k, other in enumerate(others):
+            copies.append(remote(vec_rows.at[other], vec_got.at[me], vec_send.at[k], vec_recv.at[k], (row, other)))
+        return copies
+
+    def run(copies):
+        for copy in copies:
+            copy.start()
+
+    def states(layer):
+        def one(h, carry):
+            at = layer * part // 2 + h
+            state_own[at] = state_rows(columns_of(params[at]), [ker_final[layer, pl.ds(2 * h + c, 1), :] for c in range(2)])
+            return carry
+
+        lax.fori_loop(0, part // 2, one, 0, unroll=4)
+
+    begins = (step == 0) & (seq == 0)
+    next_layer = (step == 1) & (seq == 0)
+    ends = (step == layers - 1) & (seq == seqs - 1)
+    top, bottom = layers - 1, 0
+
+    @pl.when(begins)
+    def _():
+        greet([(row, other) for other in others] + [(other, me) for other in rows_of])
+        run(moves)
+        vec_cols[...] = jnp.zeros_like(vec_cols)
+
+    @pl.when(step == 0)
+    def _():
+        def widen(rows, _):
+            back[rows, :] = first[rows, :].astype(jnp.float32)
+
+        steps(chans, STEP_ROWS, widen)
+
+    @pl.when(seq == 0)
+    def _():
+        kernel_spectrum(ker.at[0], folded, ker_spec, fs, fl, CONV_ROWS)
+        vec_grad[...] = jnp.zeros_like(vec_grad)
+        spec_grad[...] = jnp.zeros_like(spec_grad)
+
+    def gates(rows, k):
+        gated = back[rows, :] * mask[0]
+        left = (gated * sigma_in[0, rows, :].astype(jnp.float32)).astype(jnp.bfloat16)
+        right = (gated * slope_in[0, rows, :].astype(jnp.float32)).astype(jnp.bfloat16)
+        at = pl.multiple_of(k * 32, 32)
+        folded[pl.ds(at, 16), :] = left
+        folded[pl.ds(at + 16, 16), :] = right
+        vec_grad[3, rows, :] += lanes(left.astype(jnp.float32))
+        vec_grad[4, rows, :] += lanes(right.astype(jnp.float32))
+
+    steps(chans, STEP_ROWS, gates)
+
+    layer = layers - 1 - step
+    width = 2 * chans // total
+    blocks = MAT_ROWS // (2 * width)
+
+    def lin_back(rows, k):
+        value = lax.dot_general(
+            folded[rows, :], act[0], (((1,), (1,)), ((), ())), preferred_element_type=jnp.float32
+        ).reshape(blocks, 2, width, chans)
+        at = pl.ds(k * blocks, blocks)
+
+        @pl.when(seq == 0)
+        def _():
+            lin_grad[layer, at] = value
+
+        @pl.when(seq > 0)
+        def _():
+            lin_grad[layer, at] += value
+
+    steps(2 * chans, MAT_ROWS, lin_back)
+
+    @pl.when(next_layer)
+    def _():
+        for kind in (0, 1):
+            advance(kind, top, 0)
+
+    @pl.when(ends)
+    def _():
+        begin(1, bottom, 0)
+
+    def act_back(rows, _):
+        for t in range(4):
+            cols = slice(t * QUARTER, (t + 1) * QUARTER)
+            pre_grad[rows, cols] = dot(weight_t[0, rows, :], folded[:, cols])
+
+    steps(chans, MAT_ROWS, act_back)
+
+    def gelu_back(rows, _):
+        skip_sum = jnp.zeros((STEP_ROWS, 128), jnp.float32)
+        outs = []
+        for q in range(4):
+            cols = slice(q * QUARTER, (q + 1) * QUARTER)
+            p = pre[0, rows, cols].astype(jnp.float32)
+            square = p * p
+            soft = jnp.tanh(p * (GELU_A + GELU_B * square))
+            slope = 0.5 * (1.0 + soft) + (0.5 * p) * (1.0 - soft * soft) * (GELU_A + (3.0 * GELU_B) * square)
+            grad = pre_grad[rows, cols] * slope
+            pre_grad[rows, cols] = grad
+            norm = hat[0, rows, cols].astype(jnp.float32) * vec[0, rows, GAIN : GAIN + 1] + vec[0, rows, SHIFT : SHIFT + 1]
+            skip_sum = skip_sum + lanes(grad * norm)
+            outs.append(grad)
+        vec_grad[2, rows, :] += skip_sum
+        put_folded(folded, rows, fold(*outs))
+
+    steps(chans, STEP_ROWS, gelu_back)
+
+    @pl.when(ends)
+    def _():
+        for kind in (0, 1):
+            advance(kind, top, 2)
+        advance(1, bottom, 0)
+
+    sums[...] = jnp.zeros_like(sums)
+
+    def correlate(rows, chunk):
+        for g, (at, width) in enumerate(GROUPS):
+            grad = dot(get_folded(folded, rows, at, width), table_of(fs, fl, g))
+            spec_grad[rows, at : at + width] += product(
+                spec[0, rows, at : at + width].astype(jnp.float32), grad, g == 0, True
+            )
+            both = product(ker_spec[rows, at : at + width], grad, g == 0, True)
+            mixed[:, at : at + width] = dot(both.astype(jnp.bfloat16), table_of(ts, tl, g))
+
+        def norm_back(k, carry):
+            here = pl.ds(pl.multiple_of(k * STEP_ROWS, STEP_ROWS), STEP_ROWS)
+            rows = pl.ds(pl.multiple_of(chunk * CHUNK_ROWS + k * STEP_ROWS, STEP_ROWS), STEP_ROWS)
+            skip = vec[0, rows, SKIP : SKIP + 1]
+            gain = vec[0, rows, GAIN : GAIN + 1]
+            gain_sum = jnp.zeros((STEP_ROWS, 128), jnp.float32)
+            shift_sum = jnp.zeros((STEP_ROWS, 128), jnp.float32)
+            plain, weighted = [], []
+            for q, part in enumerate(get_unfolded(mixed, here)):
+                cols = slice(q * QUARTER, (q + 1) * QUARTER)
+                grad = part + skip * pre_grad[rows, cols]
+                both = grad * hat[0, rows, cols].astype(jnp.float32)
+                gain_sum = gain_sum + lanes(both)
+                shift_sum = shift_sum + lanes(grad)
+                cent = grad * gain
+                pre_grad[rows, cols] = cent
+                both = both * gain
+                plain.append(cent[:8] + cent[8:])
+                weighted.append(both[:8] + both[8:])
+            vec_grad[0, rows, :] += gain_sum
+            vec_grad[1, rows, :] += shift_sum
+            return carry[0] + jnp.concatenate(plain, 1), carry[1] + jnp.concatenate(weighted, 1)
+
+        zero = jnp.zeros((8, BUCKET), jnp.float32)
+        plain, weighted = lax.fori_loop(0, CHUNK_ROWS // STEP_ROWS, norm_back, (zero, zero), unroll=2)
+        sums[0:8, :] += plain
+        sums[8:16, :] += weighted
+
+    steps(chans, CHUNK_ROWS, correlate)
+
+    @pl.when(seq == seqs - 1)
+    def _():
+        def to_time(rows, _):
+            for g, (at, width) in enumerate(GROUPS):
+                low = spec_grad[rows, at : at + width].astype(jnp.bfloat16)
+                ker_spec[rows, at : at + width] = dot(low, table_of(ts, tl, g))
+
+        steps(chans, CONV_ROWS, to_time)
+
+        def block_rows(b):
+            return pl.ds(pl.multiple_of(b * part, part), part)
+
+        def write(b, carry):
+            for q, value in enumerate(get_unfolded(ker_spec, block_rows(2 * b + core_bit))):
+                ker_kept[b, :, q * QUARTER : (q + 1) * QUARTER] = value
+            for q, value in enumerate(get_unfolded(ker_spec, block_rows(2 * b + 1 - core_bit))):
+                ker_sent[b, :, q * QUARTER : (q + 1) * QUARTER] = value.astype(jnp.bfloat16)
+            return carry
+
+        lax.fori_loop(0, total // 2, write, 0)
+
+    for i in range(layers):
+
+        @pl.when((step == i) & (seq == seqs - 1))
+        def _(i=i):
+            layer = layers - 1 - i
+            begin(0, layer, 0)
+            if layer == layers - 1:
+                begin(1, layer, 0)
+            else:
+                advance(1, layer, 1)
+
+    mean_plain = jnp.sum(sums[0:8, :], 0, keepdims=True) / chans
+    mean_weighted = jnp.sum(sums[8:16, :], 0, keepdims=True) / chans
+    sums[0:1, :] = mean_plain
+    sums[8:9, :] = mean_weighted
+
+    @pl.when(next_layer)
+    def _():
+        for kind in (0, 1):
+            advance(kind, top, 1)
+
+    def finish(rows, _):
+        scaled = hat[0, rows, :].astype(jnp.float32) * sums[8:9, :]
+        moved = back[rows, :] + stat[0, 0, 1:2, :] * (pre_grad[rows, :] - sums[0:1, :] - scaled)
+        back[rows, :] = moved
+        back_low[seq, rows, :] = (moved - first[rows, :].astype(jnp.float32)).astype(jnp.bfloat16)
+
+    steps(chans, STEP_ROWS, finish)
+
+    for k in range(seqs):
+
+        @pl.when((step == layers - 1) & (seq == k))
+        def _(k=k):
+            run(back_moves(k))
+
+    @pl.when(ends)
+    def _():
+        for kind in (0, 1):
+            advance(kind, top, 3)
+
+    for i in range(layers):
+
+        @pl.when((step == i) & (seq == seqs - 1))
+        def _(i=i):
+            layer = layers - 1 - i
+
+            def columns(rows, _):
+                lane = lax.broadcasted_iota(jnp.int32, (STEP_ROWS, LANES), 1)
+                out = vec_cols[rows, :]
+                for kind in range(5):
+                    out = jnp.where(lane == layer * 5 + kind, jnp.sum(vec_grad[kind, rows, :], 1, keepdims=True), out)
+                vec_cols[rows, :] = out
+
+            steps(chans, STEP_ROWS, columns)
+
+    @pl.when(ends)
+    def _():
+        for c in range(n_chan):
+            vec_rows[c] = columns_of(vec_cols[c * own : (c + 1) * own, :])[:16]
+        run(vec_moves())
+        states(top)
+        run(spreads(0, top) + spreads(1, top))
+        for s in range(last_stage + 1):
+            advance(0, bottom, s)
+            if s + 2 <= last_stage:
+                advance(1, bottom, s + 2)
+                if s + 2 == last_stage:
+                    run(spreads(1, bottom))
+            if s == 1:
+                for copy in vec_moves():
+                    copy.wait()
+                vec_own[...] = jnp.sum(vec_got[...], 0)
+                run(spread(vec_own, vec_all, 2 * layers))
+        states(bottom)
+        run(spreads(0, bottom))
+        for copy in moves:
+            copy.wait()
+        for k in range(seqs):
+            for copy in back_moves(k):
+                copy.wait()
+        for i in range(layers):
+            for copy in spreads(0, i) + spreads(1, i):
+                copy.wait()
+        for copy in spread(vec_own, vec_all, 2 * layers):
+            copy.wait()
+
+
+def backward_pass(cot, mask, saved, kers, weights_t, vecs, tables, params, delta_own, n_chan, n_batch):
+    chans, toks = cot.shape
+    seqs, layers = toks // BUCKET, kers.shape[0]
+    own, group = chans // n_chan, toks * n_chan
+    bits = halving_bits(n_chan, n_batch)
+    total = 1 << bits
+    part = chans // total
+    low_count, peers = total >> (LOW_STAGE + 1), bits + 1
+    shape, low, full = jax.ShapeDtypeStruct, jnp.bfloat16, jnp.float32
+    top = layers - 1
+    layered = lambda a: pl.BlockSpec((1,) + a.shape[1:], lambda i, s: (top - i, 0, 0), pipeline_mode=pl.Buffered(1))
+    block = pl.BlockSpec((1, chans, BUCKET), lambda i, s: (top - i, 0, s))
+    vmem, dma = pltpu.VMEM, pltpu.SemaphoreType.DMA
+    return pl.pallas_call(
+        functools.partial(backward_kernel, n_chan, n_batch),
+        grid=(layers, seqs),
+        in_specs=[
+            pl.BlockSpec((chans, BUCKET), lambda i, s: (0, s)),
+            pl.BlockSpec((1, 1, BUCKET), lambda i, s: (s, 0, 0)),
+            pl.BlockSpec((1, 1, 8, BUCKET), lambda i, s: (top - i, s, 0, 0)),
+            block, block, block, block, block,
+            pl.BlockSpec((1, chans, 2 * BUCKET), lambda i, s: (top - i, 0, s)),
+            layered(kers), layered(weights_t), layered(vecs),
+            *[whole(t) for t in tables],
+            whole(params),
+            ANYWHERE,
+        ],
+        out_specs=[ANYWHERE] * 5,
+        out_shape=[
+            shape((own, group), low),
+            shape((own, group), low),
+            shape((n_batch, layers * part // 2, 8, LANES), full),
+            shape((n_batch, layers, 2 * part, chans), full),
+            shape((n_batch, 16, LANES), full),
+        ],
+        scratch_shapes=[
+            vmem((seqs, chans, BUCKET), full),
+            vmem((chans, 2 * BUCKET), full),
+            vmem((chans, 2 * BUCKET), full),
+            vmem((2 * chans, BUCKET), low),
+            vmem((CHUNK_ROWS, 2 * BUCKET), full),
+            vmem((16, BUCKET), full),
+            vmem((chans, BUCKET), full),
+            vmem((seqs, chans, BUCKET), low),
+            vmem((layers, total // 2, 2, 2 * part, chans), full),
+            vmem((5, chans, LANES), full),
+            vmem((chans, LANES), full),
+            vmem((n_chan, 16, LANES), full),
+            vmem((n_chan, 16, LANES), full),
+            vmem((16, LANES), full),
+            vmem((total // 2, part, BUCKET), full),
+            vmem((total // 2, part, BUCKET), full),
+            vmem((total, part, BUCKET), low),
+            vmem((total, part, BUCKET), low),
+            vmem((total // 2, 2 * part, chans), full),
+            vmem((low_count, 2 * part, chans), full),
+            vmem((total - low_count, 2 * part, chans), full),
+            vmem((low_count, 2 * part, chans), low),
+            vmem((low_count, 2 * part, chans), low),
+            vmem((layers, part, BUCKET), full),
+            vmem((layers, 2 * part, chans), full),
+            vmem((layers * part // 2, 8, LANES), full),
+            dma((n_chan - 1,)), dma((n_chan - 1,)), dma,
+            dma((seqs, n_chan - 1)), dma((seqs, n_chan - 1)), dma((seqs,)),
+            dma((2, peers)), dma((2, peers)), pltpu.SemaphoreType.REGULAR((2, peers)),
+            dma((n_chan - 1,)), dma((n_chan - 1,)), dma,
+            dma((2 * layers + 1, n_batch - 1)), dma((2 * layers + 1, n_batch - 1)), dma((2 * layers + 1,)),
+        ],
+        compiler_params=pltpu.CompilerParams(vmem_limit_bytes=ROOM, collective_id=3, has_side_effects=True),
+        cost_estimate=pl.CostEstimate(flops=40 * 10**9, bytes_accessed=60 * 2**20, transcendentals=0),
+        name="backward_pass",
+    )(cot, mask, *saved, kers, weights_t, vecs, *tables, params, delta_own)
+
+
+def gather_kernel(
+    n_chan, n_batch, params, x_own, w_own, vec_own,
+    x_all, ker_all, w_all, vec_all,
+    ker_rows, ker_low, send, recv, own_sem, vec_send, vec_recv, own_sems, part_send, part_recv,
+):
+    layers, part = ker_low.shape[:2]
+    path = halving(n_chan, n_batch)
+    bits = len(path)
+    me, row, others = peers_of(n_chan)
+    greet([(row, other) for other in others] + [target for _, target in path if True][n_chan.bit_length() - 1 :])
+    place = tuple(bit for bit, _ in path)
+    own = [pltpu.make_async_copy(w_own.at[i], w_all.at[(i,) + place], own_sems.at[i]) for i in range(layers)]
+    for copy in own:
+        copy.start()
+    vec_copies = [pltpu.make_async_copy(vec_own, vec_all.at[me], own_sems.at[2 * layers])]
+    for k, other in enumerate(others):
+        vec_copies.append(remote(vec_own, vec_all.at[me], vec_send.at[k], vec_recv.at[k], (row, other)))
+    for copy in vec_copies:
+        copy.start()
+
+    orders = [(0, 1, 3, 2, 4)] * layers + [(0, 1, 2, 3, 4)] * layers
+
+    def stage(p, s):
+        ref = w_all.at[p] if p < layers else ker_all.at[p - layers]
+        done, dim = orders[p][:s], orders[p][s]
+        at = ref.at[tuple(slice(None) if d in done else place[d] for d in range(bits))]
+        return remote(at, at, part_send.at[p, s], part_recv.at[p, s], path[dim][1])
+
+    moves = to_tokens(x_own, x_all, send, recv, own_sem)
+    plan = [[0], [4], [5, 6], [7, 2], [1, 3], [], []]
+
+    def issue(k):
+        for m in plan[k]:
+            moves[m].start()
+
+    for copy in own:
+        copy.wait()
+    for p in range(layers):
+        stage(p, 0).start()
+    issue(0)
+
+    def make(h, carry):
+        first_row, second_row = kernel_rows(columns_of(params[h]))
+        ker_rows[2 * h] = first_row
+        ker_rows[2 * h + 1] = second_row
+        return carry
+
+    lax.fori_loop(0, layers * part // 2, make, 0, unroll=4)
+    for i in range(layers):
+        for k in range(BUCKET // LANES):
+            value = ker_rows[i * part : (i + 1) * part, k, :]
+            ker_low[i, :, k * LANES : (k + 1) * LANES] = value.astype(jnp.bfloat16)
+    own = [pltpu.make_async_copy(ker_low.at[i], ker_all.at[(i,) + place], own_sems.at[layers + i]) for i in range(layers)]
+    for copy in own:
+        copy.start()
+    for copy in own:
+        copy.wait()
+    for p in range(layers, 2 * layers):
+        stage(p, 0).start()
+    issue(1)
+    for s in range(1, bits + 1):
+        for p in range(2 * layers):
+            stage(p, s - 1).wait()
+            if s < bits:
+                stage(p, s).start()
+        issue(s + 1)
+    for copy in vec_copies + moves:
+        copy.wait()
+
+
+def gather_params(params, x_own, w_own, vec_own, n_chan, n_batch):
+    own, group = x_own.shape
+    chans, toks = own * n_chan, group // n_chan
+    layers, wide, _ = w_own.shape
+    part = wide // 2
+    bits = halving_bits(n_chan, n_batch)
+    shape, low = jax.ShapeDtypeStruct, jnp.bfloat16
+    vmem = pl.BlockSpec(memory_space=pltpu.VMEM)
+    return pl.pallas_call(
+        functools.partial(gather_kernel, n_chan, n_batch),
+        in_specs=[vmem, ANYWHERE, ANYWHERE, vmem],
+        out_specs=[ANYWHERE, ANYWHERE, ANYWHERE, vmem],
+        out_shape=[
+            shape((chans, toks), low),
+            shape((layers,) + (2,) * bits + (part, BUCKET), low),
+            shape((layers,) + (2,) * bits + (wide, chans), low),
+            shape((n_chan,) + vec_own.shape, jnp.float32),
+        ],
+        scratch_shapes=[
+            pltpu.VMEM((layers * part, BUCKET // LANES, LANES), jnp.float32),
+            pltpu.VMEM((layers, part, BUCKET), low),
+            pltpu.SemaphoreType.DMA((n_chan - 1,)),
+            pltpu.SemaphoreType.DMA((n_chan - 1,)),
+            pltpu.SemaphoreType.DMA,
+            pltpu.SemaphoreType.DMA((n_chan - 1,)),
+            pltpu.SemaphoreType.DMA((n_chan - 1,)),
+            pltpu.SemaphoreType.DMA((2 * layers + 1,)),
+            pltpu.SemaphoreType.DMA((2 * layers, bits)),
+            pltpu.SemaphoreType.DMA((2 * layers, bits)),
+        ],
+        compiler_params=pltpu.CompilerParams(vmem_limit_bytes=ROOM, collective_id=1, has_side_effects=True),
+        cost_estimate=pl.CostEstimate(flops=10**8, bytes_accessed=10 * 2**20, transcendentals=0),
+        name="gather_params",
+    )(params, x_own, w_own, vec_own)
+
+
+def adam(weight, grad, first, second, rate):
+    first_new = 0.9 * first + 0.1 * grad
+    second_new = 0.999 * second + 0.001 * grad * grad
+    fixed_first = first_new / (1.0 - 0.9**STEP)
+    fixed_second = second_new / (1.0 - 0.999**STEP)
+    new_weight = weight - rate * (fixed_first / (jnp.sqrt(fixed_second) + 1e-08) + 0.01 * weight)
+    return (first_new, second_new, new_weight)
+
+
+def local(
+    inputs, lengths, cotangent, ln_gain, ln_bias, log_step, skip_gain, lin_bias, log_decay, frequency,
+    w_re, w_im, lin_weight, lin_moment, lin_square, vec_moment, vec_square, state_moment, state_square,
+):
+    n_chan = lax.axis_size("chan")
+    n_batch = lax.axis_size("batch")
+    own = inputs.shape[0]
+    chans = own * n_chan
+    toks = inputs.shape[1] // n_chan
+    seqs = toks // BUCKET
+    part = own // n_batch
+    me = lax.axis_index("chan")
+    row = lax.axis_index("batch")
+    lens = lax.dynamic_slice_in_dim(lengths, me * seqs, seqs)
+    places = lax.iota(jnp.int32, BUCKET)
+    valid = (places[None, :] < lens[:, None]).astype(jnp.float32).reshape(seqs, 1, BUCKET)
+    tables = tuple(jnp.asarray(t) for t in transform_tables())
+
+    def mine(a):
+        return lax.dynamic_slice_in_dim(a, row * part, part, 1)
+
+    step_size = jnp.exp(log_step)[..., None]
+    decay_rate = step_size * jnp.exp(log_decay)
+    turn_rate = step_size * frequency
+    powers, total, moment = doubled_powers(decay_rate, turn_rate)
+    params = jnp.stack([mine(a).reshape(LAYERS * part // 2, -1) for a in powers + [w_re / total, w_im / total]], 1)
+    params = jnp.pad(params, ((0, 0), (0, -params.shape[1] % 8), (0, 0)))
+    w_own = mine(lin_weight).transpose(0, 2, 1, 3).reshape(LAYERS, 2 * part, chans).astype(jnp.bfloat16)
+    vec_own = jnp.stack([ln_gain, ln_bias, skip_gain, lin_bias[:, 0], lin_bias[:, 1]], 1).reshape(5 * LAYERS, own)
+    vec_own = jnp.pad(vec_own, ((0, 16 - 5 * LAYERS), (0, LANES - own)))
+    first, kers, weights, vec_all = gather_params(params, inputs, w_own, vec_own, n_chan, n_batch)
+    kers = kers.reshape(LAYERS, chans, BUCKET)
+    weights = weights.reshape(LAYERS, 2 * chans, chans)
+    vecs = vec_all[:, : 5 * LAYERS, :own].reshape(n_chan, LAYERS, 5, own).transpose(1, 0, 3, 2).reshape(LAYERS, chans, 5)
+
+    cot, out_delta, *saved = forward_pass(first, valid, kers, weights, vecs, tables, cotangent, n_chan)
+    out_delta, in_delta, state_all, lin_all, vec_all = backward_pass(
+        cot, valid, saved, kers, weights.transpose(0, 2, 1), vecs, tables, params, out_delta, n_chan, n_batch
+    )
+    output = inputs.astype(jnp.float32) + out_delta.astype(jnp.float32)
+    input_grad = cotangent.astype(jnp.float32) + in_delta.astype(jnp.float32)
+
+    state_all = state_all.reshape(n_batch, LAYERS, part // 2, 8, 2, LANES // 2)
+    state_all = state_all.transpose(3, 1, 0, 2, 4, 5).reshape(8, LAYERS, own, -1) / total
+    c_re, c_im, d_re, d_im = [state_all[k] for k in range(4)]
+    turn_grad = -(w_re * d_im + w_im * d_re)
+    decay_grad = ((w_re * c_re - w_im * c_im) * (moment / total) - (w_re * d_re - w_im * d_im)) * decay_rate
+    state_total = jnp.stack([decay_grad, turn_grad * step_size, c_re, -c_im], 1)
+    step_total = jnp.sum(decay_grad + turn_grad * turn_rate, -1)
+    lin_total = lin_all.reshape(n_batch, LAYERS, 2, part, chans).transpose(1, 0, 3, 2, 4).reshape(LAYERS, own, 2, chans)
+    vec_sum = jnp.sum(vec_all, 0)[: 5 * LAYERS, :own].reshape(LAYERS, 5, own)
+    vec_total = jnp.stack([vec_sum[:, 0], vec_sum[:, 1], step_total, vec_sum[:, 2], vec_sum[:, 3], vec_sum[:, 4]], 1)
+
+    vec_old = jnp.stack([ln_gain, ln_bias, log_step, skip_gain, lin_bias[:, 0], lin_bias[:, 1]], 1)
+    state_old = jnp.stack([log_decay, frequency, w_re, w_im], 1)
+    lin_first, lin_second, lin_new = adam(lin_weight, lin_total, lin_moment, lin_square, 0.05)
+    vec_first, vec_second, vec_new = adam(vec_old, vec_total, vec_moment, vec_square, 0.2)
+    state_first, state_second, state_new = adam(state_old, state_total, state_moment, state_square, 0.2)
+    return (
+        output, input_grad, lin_first, lin_second, lin_new, vec_first, vec_second, vec_new,
+        state_first, state_second, state_new,
+    )
 
 
 def tables(length):
@@ -55,16 +1178,7 @@
     return jax.nn.gelu(pre_act)
 
 
-def adam(weight, grad, first, second, rate):
-    first_new = 0.9 * first + 0.1 * grad
-    second_new = 0.999 * second + 0.001 * grad * grad
-    fixed_first = first_new / (1.0 - 0.9**STEP)
-    fixed_second = second_new / (1.0 - 0.999**STEP)
-    new_weight = weight - rate * (fixed_first / (jnp.sqrt(fixed_second) + 1e-08) + 0.01 * weight)
-    return (first_new, second_new, new_weight)
-
-
-def local(
+def wide_local(
     inputs,
     lengths,
     cotangent,
@@ -181,6 +1295,11 @@
     )
 
 
+def suits(own_seqs, chans, n_chan, n_batch):
+    powers = n_chan & (n_chan - 1) == 0 and n_batch & (n_batch - 1) == 0
+    return powers and own_seqs % n_chan == 0 and own_seqs > n_chan and chans == 16 * n_chan * n_batch
+
+
 def solution(mesh):
     in_specs = (
         P("chan", "batch"),
@@ -216,4 +1335,12 @@
         P(None, None, "chan", None),
         P(None, None, "chan", None),
     )
-    return jax.shard_map(local, mesh=mesh, in_specs=in_specs, out_specs=out_specs, check_vma=False)
+    n_chan = mesh.shape["chan"]
+
+    def run(*args):
+        own_seqs = args[1].shape[0] // mesh.shape["batch"]
+        fits = suits(own_seqs, args[3].shape[1], n_chan, mesh.shape["batch"])
+        body = local if fits else wide_local
+        return jax.shard_map(body, mesh=mesh, in_specs=in_specs, out_specs=out_specs, check_vma=False)(*args)
+
+    return run

time: 2840 us -> 289 us (0.10)
  waiting for transfers between devices: 1510 us -> 0 us
  matrix products: 738 us -> 0 us
  other arithmetic: 517 us -> 16.4 us
  Pallas kernels: 0 us -> 257 us
    reduce_scatter x2 -> x0, waiting for transfers between devices: 861 us -> none  [local(): lax.psum_scatter(act_part, 'chan', scatter_dimension=0, tiled=True)]
    dot_general x30 -> x0, matrix products: 738 us -> none  [the longest x4 137 us: mixer(): conv_out = jnp.einsum('csk,lk->csl', prod_re, cos_back, precision=top_prec)]
    reduce_sum x23 -> x2, other arithmetic: 468 us -> 1.71 us  [the longest x1 0.95 us: local(): step_total = jnp.sum(decay_grad + turn_grad * turn_rate, -1)]
    all_gather x2 -> x0, waiting for transfers between devices: 439 us -> none  [local(): act_all = lax.all_gather(act_low, 'chan', axis=0, tiled=True)]
    pallas_call x0 -> x3, Pallas kernels: none -> 257 us  [the longest x1 135 us: backward_pass(): pl.pallas_call(functools.partial(backward_kernel, n_chan, n_batch), grid=...]
    psum x5 -> x0, waiting for transfers between devices: 214 us -> none  [the longest x2 134 us: local(): lax.psum((jnp.sum(centred_grad, 0), jnp.sum(centred_grad * centred, 0)),...]
    unnamed x192 -> x45, local copies, waits for them, and re-layouts: 35.1 us -> 1.9 us
  transfers between devices with their start and end apart: 9 -> 0, of which waited for: 8 -> 0; matrix products, arithmetic and copies ran while one was open for 16% -> 0% of each run, Pallas kernels for 0% -> 0%
where the time goes in v2:
time: 289 us; the launch traced here: 288 us
  Pallas kernels  257 us (89%)
  other arithmetic  16.4 us (6%)
  local copies, waits for them, and re-layouts  13.4 us (5%)
    pallas_call x1, Pallas kernels, backward_pass(): pl.pallas_call(functools.partial(backward_kernel, n_chan, n_batch), grid=...  135 us
    pallas_call x1, Pallas kernels, gather_params(): pl.pallas_call(functools.partial(gather_kernel, n_chan, n_batch), in_spec...  72.1 us
    pallas_call x1, Pallas kernels, forward_pass(): pl.pallas_call(functools.partial(forward_kernel, n_chan), grid=(layers, s...  50.3 us

profile of v2, /device:TPU:0, one launch (start us, length us, event | category | flops | bytes accessed | tf_op | source)
XLA Modules:
  0.0 288.1 jit_solution(17881657179422831353)
XLA Ops:
  0.7 0.7 exp.36
  1.4 1.1 fusion.15
  2.5 0.1 sine_multiply_fusion.1
  3.0 0.1 sine_multiply_fusion.3
  3.5 0.1 sine_multiply_fusion.5
  3.9 0.8 dynamic-slice_divide_fusion
  5.3 0.3 stack.58
  5.6 0.7 pad.8.params
  6.3 0.6 copy.47
  7.0 0.6 pad.9.vec_own
  7.6 72.1 %gather_params.1 = (bf16[512,2048]{1,0:T(8,128)(2,1)}, bf16[2,2,2,2,2,2,16,1024]{7,6,5,4,3,2,1,0:T(8,128)(2,1)}, bf16[2,2,2,2,2,2,32,512]{7,6,5,4,3,2,1,0:T(8,128)(2,1)}, f32[8,16,128]{2,1,0:T(8,128)}) custom-call(f32[16,24,128]{2,1,0:T(8,128)} %pad.8.params, bf16[64,16384]{1,0:T(8,128)(2,1)} %x_own.1, bf16[2,32,512]{2,1,0:T(8,128)(2,1)} %bitcast.97, ...), custom_call_target="tpu_custom_call" | custom-call | flops 100000000 | bytes 10485760 | tf_op jit(solution)/shard_map/gather_params/pallas_call | solution.py:1035
  79.7 0.9 copy.51
  80.6 1.0 copy.52
  81.7 0.7 compare_convert_fusion.mask
  82.4 50.3 %forward_pass.1 = (bf16[512,2048]{1,0:T(8,128)(2,1)}, bf16[512,2048]{1,0:T(8,128)(2,1)}, f32[2,2,8,1024]{3,2,1,0:T(8,128)}, bf16[2,512,2048]{2,1,0:T(8,128)(2,1)...) custom-call(bf16[512,2048]{1,0:T(8,128)(2,1)} %get-tuple-element.29., ...), custom_call_target="tpu_custom_call" | custom-call | flops 24000000000 | bytes 41943040 | tf_op jit(solution)/shard_map/forward_pass/pallas_call | solution.py:431
  132.7 2.4 copy.53
  135.1 134.9 %backward_pass.1 = (bf16[64,16384]{1,0:T(8,128)(2,1)}, bf16[64,16384]{1,0:T(8,128)(2,1)}, f32[4,16,8,128]{3,2,1,0:T(8,128)}, f32[4,2,32,512]{3,2,1,0:T(8,128)}, f32[4,16,128]{2,1,0:T(8,128)}) custom-call(bf16[512,2048]{1,0:T(8,128)(2,1)} %get-tuple-element.33.first, f32[2,1,1024]{2,1,0:T(1,128)} %compare_convert_fusion.mask, ...), custom_call_target="tpu_custom_call" | custom-call | flops 40000000000 | bytes 62914560 | tf_op jit(solution)/shard_map/backward_pass/pallas_call | solution.py:896
  270.0 1.3 reshape.106
  271.3 0.3 copy.56
  271.7 0.1 multiply_bitcast_fusion
  271.8 0.9 add_reduce_fusion
  272.8 1.0 multiply_subtract_fusion.1
  273.8 0.8 reduce_sum.18
  274.6 0.7 stack.66
  275.4 0.7 multiply_subtract_fusion.2
  276.1 0.6 copy.66
  276.7 0.6 copy.67
  277.3 0.6 copy.68
  277.9 4.4 %convert_add_fusion = f32[64,16384]{1,0:T(8,128)} fusion(bf16[64,16384]{1,0:T(8,128)(2,1)} %get-tuple-element.43, bf16[64,16384]{1,0:T(8,128)(2,1)S(1)} %copy-done.2), kind=kLoop, calls=%fused_computation | loop fusion | flops 3145728 | bytes 8388608 | tf_op jit(solution)/shard_map/add | solution.py:1112
  282.4 2.4 convert_add_fusion.1
  284.8 0.4 copy.54
  285.2 2.9 multiply_subtract_fusion
  (71 shorter events, 1.9 us)
Async XLA Ops:
  0.6 5.6 %copy-start.6 = (f32[2,64,2,512]{3,2,1,0:T(2,128)S(1)}, f32[2,64,2,512]{3,2,1,0:T(2,128)}, u32[]{:S(2)}) copy-start(f32[2,64,2,512]{3,2,1,0:T(2,128)} %param.35) | copy-start | bytes 1572868
  0.7 6.3 %copy-start.19 = (f32[2,64]{1,0:T(2,128)S(1)}, f32[2,64]{1,0:T(2,128)}, u32[]{:S(2)}) copy-start(f32[2,64]{1,0:T(2,128)} %param.26) | copy-start | bytes 1540
  0.7 6.3 %copy-start.18 = (f32[2,64]{1,0:T(2,128)S(1)}, f32[2,64]{1,0:T(2,128)}, u32[]{:S(2)}) copy-start(f32[2,64]{1,0:T(2,128)} %param.27) | copy-start | bytes 1540
  0.7 6.3 %copy-start.17 = (f32[2,64]{1,0:T(2,128)S(1)}, f32[2,64]{1,0:T(2,128)}, u32[]{:S(2)}) copy-start(f32[2,64]{1,0:T(2,128)} %param.29) | copy-start | bytes 1540
  0.7 6.3 %copy-start.14 = (f32[2,2,64]{2,1,0:T(2,128)S(1)}, f32[2,2,64]{2,1,0:T(2,128)}, u32[]{:S(2)}) copy-start(f32[2,2,64]{2,1,0:T(2,128)} %param.30) | copy-start | bytes 3076
  5.1 76.5 %copy-start.20 = (s32[16]{0:T(128)S(1)}, s32[16]{0:T(128)}, u32[]{:S(2)}) copy-start(s32[16]{0:T(128)} %param.24) | copy-start | bytes 196
  82.4 50.3 %copy-start.1 = (bf16[2,2,2,2,2,2,32,512]{7,6,5,4,3,2,1,0:T(8,128)(2,1)S(1)}, bf16[2,2,2,2,2,2,32,512]{7,6,5,4,3,2,1,0:T(8,128)(2,1)}, u32[]{:S(2)}) copy-start(bf16[2,2,2,2,2,2,32,512]{7,6,5,4,3,2,1,0:T(8,128)(2,1)} %get-tuple-element.31) | copy-start | bytes 6291460
  269.9 1.8 copy-start.4
  269.9 1.8 copy-start.5
  270.0 1.9 copy-start.7
  270.0 2.8 copy-start.11
  270.0 2.8 copy-start.12
  270.0 2.8 copy-start.13
  271.6 3.8 %copy-start.15 = (f32[2,6,64]{2,0,1:T(2,128)S(1)}, f32[2,6,64]{2,0,1:T(2,128)}, u32[]{:S(2)}) copy-start(f32[2,6,64]{2,0,1:T(2,128)} %param.39) | copy-start | bytes 9220
  271.6 6.3 %copy-start.2 = (bf16[64,16384]{1,0:T(8,128)(2,1)S(1)}, bf16[64,16384]{1,0:T(8,128)(2,1)}, u32[]{:S(2)}) copy-start(bf16[64,16384]{1,0:T(8,128)(2,1)} %cot_own.1) | copy-start | bytes 6291460
  272.8 2.6 copy-start.16
  277.9 4.4 %copy-start = (bf16[64,16384]{1,0:T(8,128)(2,1)S(1)}, bf16[64,16384]{1,0:T(8,128)(2,1)}, u32[]{:S(2)}) copy-start(bf16[64,16384]{1,0:T(8,128)(2,1)} %x_own.1) | copy-start | bytes 6291460
  277.9 4.4 %copy-start.3 = (bf16[64,16384]{1,0:T(8,128)(2,1)S(1)}, bf16[64,16384]{1,0:T(8,128)(2,1)}, u32[]{:S(2)}) copy-start(bf16[64,16384]{1,0:T(8,128)(2,1)} %get-tuple-element.42) | copy-start | bytes 6291460
  282.4 2.5 copy-start.10
  282.4 2.9 copy-start.8
  282.4 2.9 copy-start.9

commit v3 on v0

--- a/solution.py
+++ b/solution.py
@@ -1,13 +1,1107 @@
+import functools
 import math
 
 import jax
 import jax.numpy as jnp
+import numpy as np
 from jax import lax
+from jax.experimental import pallas as pl
+from jax.experimental.pallas import tpu as pltpu
 from jax.sharding import PartitionSpec as P
 
 LAYERS = 2
 BUCKET = 1024
 STEP = 10
+
+
+QUARTER = BUCKET // 4
+HALF_ROOT = math.sqrt(0.5)
+STEP_ROWS = 16
+UNROLL = 4
+CONV_ROWS = 256
+CHUNK_ROWS = 256
+MAT_ROWS = 256
+LIN_ROWS = 256
+ROOM = 59 * 2**20
+GROUPS = ((0, 256), (256, 256), (512, 512), (1024, 512), (1536, 512))
+GELU_A = math.sqrt(2.0 / math.pi)
+GELU_B = GELU_A * 0.044715
+
+
+def transform_tables():
+    place = np.arange(QUARTER)[:, None]
+    to_spec, to_time = [], []
+    for residue in (0, 4):
+        bins = np.arange(QUARTER // 2)[None, :]
+        turn = (8 * bins + residue) * place % (2 * BUCKET) * (math.pi / BUCKET)
+        cosine, sine = np.cos(turn), -np.sin(turn)
+        weights = np.full_like(cosine, 2.0)
+        if residue == 0:
+            sine[:, 0] = 1 - 2 * (place[:, 0] % 2)
+            weights[:, 0] = 1.0
+        to_spec.append(np.concatenate([cosine, sine], 1))
+        to_time.append(np.concatenate([cosine * weights, sine * weights], 1).T / (2 * BUCKET))
+    for residue in (1, 2, 3):
+        bins = np.arange(QUARTER)[None, :]
+        turn = (8 * bins + residue) * place % (2 * BUCKET) * (math.pi / BUCKET)
+        cosine, sine = np.cos(turn), np.sin(turn)
+        sign = 1.0 if residue == 3 else -1.0
+        to_spec.append(np.block([[cosine, -sine], [sign * sine, sign * cosine]]))
+        to_time.append(np.block([[cosine.T, sine.T], [-sine.T, cosine.T]]) / BUCKET)
+    small = [np.stack(side[:2]).astype(jnp.bfloat16) for side in (to_spec, to_time)]
+    large = [np.stack(side[2:]).astype(jnp.bfloat16) for side in (to_spec, to_time)]
+    return small[0], large[0], small[1], large[1]
+
+
+def quarters(x):
+    return [x[:, q * QUARTER : (q + 1) * QUARTER] for q in range(4)]
+
+
+def fold(x0, x1, x2, x3):
+    even, odd = x0 + x2, x1 + x3
+    diff = x1 - x3
+    turned, tilted = diff * HALF_ROOT, odd * HALF_ROOT
+    return even + odd, even - odd, x0 + turned, x2 + tilted, x0 - x2, diff, x0 - turned, x2 - tilted
+
+
+def unfold(y0, y4, r1, i1, r2, i2, r3, i3):
+    even, odd = y0 + y4, y0 - y4
+    r_sum, r_diff, i_sum, i_diff = r1 + r3, r1 - r3, i1 + i3, i1 - i3
+    return (
+        even + (r2 + r_sum),
+        odd - i2 + (r_diff - i_sum) * HALF_ROOT,
+        even - (r2 + i_diff),
+        odd + i2 - (r_diff + i_sum) * HALF_ROOT,
+    )
+
+
+def dot(a, b):
+    return jnp.dot(a, b, preferred_element_type=jnp.float32)
+
+
+def product(a, b, first, conj):
+    half = a.shape[1] // 2
+    ar, ai, br, bi = a[:, :half], a[:, half:], b[:, :half], b[:, half:]
+    cross = ai * bi
+    if conj:
+        imag = ar * bi - ai * br
+    else:
+        imag = ar * bi + ai * br
+    if first:
+        lone = lax.broadcasted_iota(jnp.int32, cross.shape, 1) == 0
+        imag = jnp.where(lone, cross, imag)
+        cross = jnp.where(lone, 0.0, cross)
+    real = ar * br + cross if conj else ar * br - cross
+    return jnp.concatenate([real, imag], 1)
+
+
+def table_of(small, large, group):
+    return small[group] if group < 2 else large[group - 2]
+
+
+def put_folded(dest, rows, parts):
+    lower = pl.ds(rows.start + dest.shape[0] // 2, rows.size)
+    for k, part in enumerate(parts):
+        dest[rows if k < 4 else lower, k % 4 * QUARTER : (k % 4 + 1) * QUARTER] = part.astype(dest.dtype)
+
+
+def get_folded(src, rows, at, width):
+    if at >= BUCKET:
+        rows, at = pl.ds(rows.start + src.shape[0] // 2, rows.size), at - BUCKET
+    return src[rows, at : at + width]
+
+
+def get_unfolded(src, rows):
+    return unfold(*[src[rows, k * QUARTER : (k + 1) * QUARTER] for k in range(8)])
+
+
+def steps(total, size, body):
+    def one(k, carry):
+        body(pl.ds(pl.multiple_of(k * size, size), size), k)
+        return carry
+
+    lax.fori_loop(0, total // size, one, 0, unroll=UNROLL if size == STEP_ROWS else 1)
+
+
+def kernel_spectrum(ker, folded, spec, small, large, chunk):
+    chans = ker.shape[0]
+
+    def fold_rows(rows, _):
+        put_folded(folded, rows, fold(*quarters(ker[rows, :].astype(jnp.float32))))
+
+    steps(chans, STEP_ROWS, fold_rows)
+
+    def transform_rows(rows, _):
+        for g, (at, width) in enumerate(GROUPS):
+            spec[rows, at : at + width] = dot(get_folded(folded, rows, at, width), table_of(small, large, g))
+
+    steps(chans, chunk, transform_rows)
+
+
+def token_stats(stream, chans):
+    def add(k, carry):
+        v = stream[pl.ds(pl.multiple_of(k * STEP_ROWS, STEP_ROWS), STEP_ROWS), :].astype(jnp.float32)
+        return carry + v[:8] + v[8:]
+
+    total = lax.fori_loop(0, chans // STEP_ROWS, add, jnp.zeros((8, BUCKET), jnp.float32), unroll=UNROLL)
+    mean_val = jnp.sum(total, 0, keepdims=True) / chans
+
+    def add_square(k, carry):
+        v = stream[pl.ds(pl.multiple_of(k * STEP_ROWS, STEP_ROWS), STEP_ROWS), :].astype(jnp.float32) - mean_val
+        v = v * v
+        return carry + v[:8] + v[8:]
+
+    total = lax.fori_loop(0, chans // STEP_ROWS, add_square, jnp.zeros((8, BUCKET), jnp.float32), unroll=UNROLL)
+    return mean_val, lax.rsqrt(jnp.sum(total, 0, keepdims=True) / chans + 1e-05)
+
+
+def lanes(x):
+    total = x[:, :128]
+    for k in range(1, x.shape[1] // 128):
+        total = total + x[:, k * 128 : (k + 1) * 128]
+    return total
+
+
+GAIN, SHIFT, SKIP, BIAS_IN, BIAS_VAL = range(5)
+MESH = pl.DeviceIdType.MESH
+
+
+def bit_of(index, place):
+    return lax.rem(lax.div(index, 1 << place), 2)
+
+
+def flip(index, place):
+    return index + (1 - 2 * bit_of(index, place)) * (1 << place)
+
+
+def peers_of(n_chan):
+    me, row = lax.axis_index("chan"), lax.axis_index("batch")
+    others = []
+    for k in range(1, n_chan):
+        other = me
+        for place in range(n_chan.bit_length() - 1):
+            other = flip(other, place) if k >> place & 1 else other
+        others.append(other)
+    return me, row, others
+
+
+def greet(targets):
+    barrier = pltpu.get_barrier_semaphore()
+    for target in targets:
+        pl.semaphore_signal(barrier, inc=1, device_id=target, device_id_type=MESH)
+    pl.semaphore_wait(barrier, len(targets))
+
+
+LANES = 128
+POWERS = 8
+LOW_STAGE = 1
+
+
+def halving(n_chan, n_batch):
+    me, row = lax.axis_index("chan"), lax.axis_index("batch")
+    chan_bits, batch_bits = n_chan.bit_length() - 1, n_batch.bit_length() - 1
+    out = [(bit_of(me, k), (row, flip(me, k))) for k in reversed(range(chan_bits))]
+    return out + [(bit_of(row, k), (flip(row, k), me)) for k in reversed(range(batch_bits))]
+
+
+def doubled_powers(decay_rate, turn_rate):
+    spans = [2.0**k for k in range(BUCKET.bit_length() - 1)]
+    sizes = [jnp.exp(-span * decay_rate) for span in spans]
+    total, moment = jnp.ones_like(decay_rate), jnp.zeros_like(decay_rate)
+    for span, size in zip(spans, sizes):
+        moment = moment * (1.0 + size) + span * size * total
+        total = total * (1.0 + size)
+    powers = []
+    for span, size in list(zip(spans, sizes))[:POWERS]:
+        powers += [size * jnp.cos(span * turn_rate), size * jnp.sin(span * turn_rate)]
+    return powers, total, moment
+
+
+def times(a, b):
+    return a[0] * b[0] - a[1] * b[1], a[0] * b[1] + a[1] * b[0]
+
+
+def columns_of(rows):
+    pad = jnp.zeros((LANES - rows.shape[0], LANES), jnp.float32)
+    return jnp.transpose(jnp.concatenate([rows, pad], 0))
+
+
+def near_powers(params):
+    lane = lax.broadcasted_iota(jnp.int32, (params.shape[0], LANES), 1)
+    value = None
+    for k in range(POWERS - 1):
+        power = params[:, 2 * k : 2 * k + 1], params[:, 2 * k + 1 : 2 * k + 2]
+        here = (lane & (1 << k)) != 0
+        if value is None:
+            value = jnp.where(here, power[0], 1.0), jnp.where(here, power[1], 0.0)
+        else:
+            moved = times(value, power)
+            value = jnp.where(here, moved[0], value[0]), jnp.where(here, moved[1], value[1])
+    far = params[:, 2 * POWERS - 2 : 2 * POWERS - 1], params[:, 2 * POWERS - 1 : 2 * POWERS]
+    return value, tuple(jnp.broadcast_to(f, lane.shape) for f in far)
+
+
+def halves(x):
+    half = x.shape[0] // 2
+    return [jnp.sum(x[:half], 0, keepdims=True), jnp.sum(x[half:], 0, keepdims=True)]
+
+
+def kernel_rows(params):
+    value, far = near_powers(params)
+    value = times(value, (params[:, 2 * POWERS : 2 * POWERS + 1], params[:, 2 * POWERS + 1 : 2 * POWERS + 2]))
+    out = [halves(value[0])]
+    for _ in range(1, BUCKET // LANES):
+        value = times(value, far)
+        out.append(halves(value[0]))
+    return [jnp.concatenate([row[c] for row in out], 0) for c in range(2)]
+
+
+def state_rows(params, grads):
+    value, far = near_powers(params)
+    half = params.shape[0] // 2
+    place = lax.broadcasted_iota(jnp.int32, (1, LANES), 1).astype(jnp.float32)
+    plain = weighted = None
+    for k in reversed(range(BUCKET // LANES)):
+        rows = [g[:, k * LANES : (k + 1) * LANES] for g in grads]
+        g = jnp.concatenate([jnp.broadcast_to(r, (half, LANES)) for r in rows], 0)
+        w = jnp.concatenate([jnp.broadcast_to(r * (place + float(k * LANES)), (half, LANES)) for r in rows], 0)
+        if plain is None:
+            plain, weighted = (g, jnp.zeros_like(g)), (w, jnp.zeros_like(g))
+        else:
+            plain, weighted = times(plain, far), times(weighted, far)
+            plain, weighted = (plain[0] + g, plain[1]), (weighted[0] + w, weighted[1])
+    cols = times(plain, value) + times(weighted, value)
+    lane = lax.broadcasted_iota(jnp.int32, value[0].shape, 1)
+    out = jnp.zeros_like(value[0])
+    for k, col in enumerate(cols):
+        out = jnp.where(lane == k, jnp.sum(col, 1, keepdims=True), out)
+    return jnp.transpose(out)[:8]
+
+
+def remote(src, dst, send, recv, target):
+    return pltpu.make_async_remote_copy(
+        src_ref=src, dst_ref=dst, send_sem=send, recv_sem=recv, device_id=target, device_id_type=MESH
+    )
+
+
+def halving_bits(n_chan, n_batch):
+    return n_chan.bit_length() + n_batch.bit_length() - 2
+
+
+def whole(a):
+    return pl.BlockSpec(a.shape, lambda t, n=a.ndim: (0,) * n, pipeline_mode=pl.Buffered(1))
+
+
+ANYWHERE = pl.BlockSpec(memory_space=pl.ANY)
+GATHER_ORDER = ((0, 1, 2, 3, 4), (0, 1, 3, 2, 4))
+
+
+def train_kernel(
+    n_chan, n_batch, mask, params, fs, fl, ts, tl, vec_mine, x_own, cot_own, w_own,
+    out_all, in_all, state_all, lin_all, vec_all, cot_all, ker_all, w_all,
+    hat_far, pre_far, act_far, sigma_far, slope_far, spec_far,
+    x_low, hats, pres, acts, sigmas, slopes, specs, stats, streams, ker_spec, spec_grad, mixed, folded, pre_grad, back_low,
+    w_near, loaded, sums, vecs, vec_in, ker_rows, ker_low,
+    lin_grad, vec_grad, vec_cols, vec_rows, vec_got, vec_own,
+    ker_sums, ker_sent, ker_got, lin_sums, lin_sent, lin_got, low_sent, low_got, ker_final, lin_final, state_own,
+    move_send, move_recv, move_own, gather_send, gather_recv, gather_own, load_sem, far_sem,
+    part_send, part_recv, ready, vec_send, vec_recv, vec_sem, all_send, all_recv, all_own,
+):
+    step = pl.program_id(0)
+    layers, seqs = stats.shape[:2]
+    chans = x_low.shape[1]
+    own = chans // n_chan
+    part = ker_final.shape[1]
+    forward_steps = layers * seqs
+    me, row, others = peers_of(n_chan)
+    rows_of = [lax.rem(row + k, n_batch) for k in range(1, n_batch)]
+    above = halving(n_chan, n_batch)
+    path = list(reversed(above))
+    bits, batch_bits = len(path), n_batch.bit_length() - 1
+    total = 1 << bits
+    core_bit = path[0][0]
+    top, bottom = layers - 1, 0
+    mine = pl.ds(pl.multiple_of(me * own, own), own)
+
+    def trade(kind, k, source, dest):
+        copies = [pltpu.make_async_copy(source(me), dest, move_own.at[kind, k])]
+        for j, other in enumerate(others):
+            copies.append(remote(source(other), dest, move_send.at[kind, k, j], move_recv.at[kind, k, j], (row, other)))
+        return copies
+
+    def columns(device, k):
+        return pl.ds(pl.multiple_of((device * seqs + k) * BUCKET, BUCKET), BUCKET)
+
+    def x_moves(k):
+        return trade(0, k, lambda device: x_own.at[:, columns(device, k)], x_low.at[k, mine])
+
+    def cot_moves(k):
+        return trade(1, k, lambda device: cot_own.at[:, columns(device, k)], cot_all.at[k, mine])
+
+    def rows_for(device):
+        return pl.ds(pl.multiple_of(device * own, own), own)
+
+    def out_moves(k):
+        return trade(2, k, lambda device: back_low.at[k, rows_for(device)], out_all.at[:, columns(me, k)])
+
+    def in_moves(k):
+        return trade(3, k, lambda device: back_low.at[k, rows_for(device)], in_all.at[:, columns(me, k)])
+
+    def run(copies):
+        for copy in copies:
+            copy.start()
+
+    def finish_all(copies):
+        for copy in copies:
+            copy.wait()
+
+    place = tuple(bit for bit, _ in above)
+
+    def held(kind, i, s):
+        order = GATHER_ORDER[kind]
+        ref = (ker_all if kind == 0 else w_all).at[i]
+        ref = ref.at[tuple(slice(None) if d in order[:s] else place[d] for d in range(bits))]
+        k = 2 * i + kind
+        return remote(ref, ref, gather_send.at[k, s], gather_recv.at[k, s], above[order[s]][1])
+
+    def gather_next(i, s):
+        for kind in (1, 0):
+            held(kind, i, s).wait()
+            if s + 1 < bits:
+                held(kind, i, s + 1).start()
+
+    def vec_in_moves():
+        copies = [pltpu.make_async_copy(vec_mine, vec_in.at[me], gather_own.at[2 * layers])]
+        for k, other in enumerate(others):
+            copies.append(remote(vec_mine, vec_in.at[me], vec_send.at[1, k], vec_recv.at[1, k], (row, other)))
+        return copies
+
+    def make_kernels(i):
+        def make(h, carry):
+            first_row, second_row = kernel_rows(columns_of(params[i * part // 2 + h]))
+            ker_rows[2 * h] = first_row
+            ker_rows[2 * h + 1] = second_row
+            return carry
+
+        lax.fori_loop(0, part // 2, make, 0, unroll=4)
+        for k in range(BUCKET // LANES):
+            ker_low[i, :, k * LANES : (k + 1) * LANES] = ker_rows[:, k, :].astype(jnp.bfloat16)
+        return pltpu.make_async_copy(ker_low.at[i], ker_all.at[(i,) + place], gather_own.at[2 * i])
+
+    def load_kernels(layer):
+        copy = pltpu.make_async_copy(ker_all.at[layer].reshape(chans, BUCKET), loaded, load_sem)
+        copy.start()
+        copy.wait()
+        kernel_spectrum(loaded, folded, ker_spec, fs, fl, CONV_ROWS)
+
+    def far_copies(k, back):
+        pairs = zip((hats, pres, acts, sigmas, slopes, specs), (hat_far, pre_far, act_far, sigma_far, slope_far, spec_far))
+        copies = []
+        for j, (near, far) in enumerate(pairs):
+            ends = (far.at[k], near.at[k]) if back else (near.at[k], far.at[k])
+            copies.append(pltpu.make_async_copy(*ends, far_sem.at[j, k]))
+        return copies
+
+    groups = [[0], [1], [2, 3], [4]]
+    count, at, gone = [], [0], 0
+    for group in groups:
+        gone += len(group)
+        count.append(total >> gone)
+        at.append(at[-1] + count[-1] * ((1 << len(group)) - 1))
+    last_stage = len(groups) - 1
+
+    def side(s, mask):
+        chan, batch, index = me, row, 0
+        for t, dim in enumerate(groups[s]):
+            bit = path[dim][0]
+            across = mask >> t & 1
+            index = index + (1 - bit if across else bit) * (1 << t)
+            if across and dim < batch_bits:
+                batch = flip(batch, dim)
+            elif across:
+                chan = flip(chan, dim - batch_bits)
+        return (batch, chan), index
+
+    def masks(s):
+        return range(1, 1 << len(groups[s]))
+
+    def kept_rows(b):
+        return spec_grad[pl.ds(pl.multiple_of(b * part, part), part), :BUCKET]
+
+    def sums_at(s):
+        return sum(count[1 : s + 1])
+
+    def slot(kind, s, mask, sent):
+        first = (mask - 1) * count[s]
+        if kind == 0 or s == 0:
+            return at[s] + first
+        if s == LOW_STAGE:
+            return first
+        return first + at[s] - at[LOW_STAGE + 1] + (0 if sent else at[LOW_STAGE])
+
+    def stage(kind, layer, s, mask):
+        to, got = pl.ds(slot(kind, s, mask, True), count[s]), pl.ds(slot(kind, s, mask, False), count[s])
+        if kind == 0:
+            src, dst = ker_sent.at[to], ker_got.at[got]
+        elif s == 0:
+            src, dst = lin_grad.at[layer, :, 1 - core_bit], lin_got.at[got]
+        elif s == LOW_STAGE:
+            src, dst = low_sent.at[to], low_got.at[got]
+        else:
+            src, dst = lin_sent.at[to], lin_got.at[got]
+        k = at_peer[s] + mask - 1
+        return remote(src, dst, part_send.at[kind, k], part_recv.at[kind, k], side(s, mask)[0])
+
+    at_peer = [0]
+    for s in range(len(groups)):
+        at_peer.append(at_peer[-1] + (1 << len(groups[s])) - 1)
+
+    def begin(kind, layer, s):
+        for mask in masks(s):
+            if layer != layers - 1:
+                pl.semaphore_wait(ready.at[kind, at_peer[s] + mask - 1], 1)
+            stage(kind, layer, s, mask).start()
+
+    def advance(kind, layer, s):
+        for mask in masks(s):
+            stage(kind, layer, s, mask).wait()
+
+        def value(b):
+            if kind == 0:
+                result = kept_rows(b) if s == 0 else ker_sums[sums_at(s - 1) + b]
+            else:
+                result = lin_grad[layer, b, core_bit] if s == 0 else lin_sums[sums_at(s - 1) + b]
+            for mask in masks(s):
+                got = ker_got if kind == 0 else low_got if s == LOW_STAGE else lin_got
+                result = result + got[slot(kind, s, mask, False) + b].astype(jnp.float32)
+            return result
+
+        if s == last_stage:
+            final = ker_final if kind == 0 else lin_final
+            final[layer] = value(0)
+        else:
+            wide = 1 << len(groups[s + 1])
+
+            def one(b, carry):
+                sums = ker_sums if kind == 0 else lin_sums
+                sums[sums_at(s) + b] = value(wide * b + side(s + 1, 0)[1])
+                for mask in masks(s + 1):
+                    moved = value(wide * b + side(s + 1, mask)[1])
+                    to = slot(kind, s + 1, mask, True) + b
+                    if kind == 0:
+                        ker_sent[to] = moved.astype(jnp.bfloat16)
+                    elif s + 1 == LOW_STAGE:
+                        low_sent[to] = moved.astype(jnp.bfloat16)
+                    else:
+                        lin_sent[to] = moved
+                return carry
+
+            lax.fori_loop(0, count[s + 1], one, 0)
+        if layer == layers - 1:
+            for mask in masks(s):
+                there = side(s, mask)[0]
+                pl.semaphore_signal(ready.at[kind, at_peer[s] + mask - 1], inc=1, device_id=there, device_id_type=MESH)
+        if s < last_stage:
+            begin(kind, layer, s + 1)
+
+    def spread(own_ref, everyone, k):
+        copies = [pltpu.make_async_copy(own_ref, everyone.at[row], all_own.at[k])]
+        for j, other in enumerate(rows_of):
+            copies.append(remote(own_ref, everyone.at[row], all_send.at[k, j], all_recv.at[k, j], (other, me)))
+        return copies
+
+    def spreads(kind, layer):
+        if kind == 0:
+            half = pl.ds(layer * part // 2, part // 2)
+            return spread(state_own.at[half], state_all.at[:, half], layer)
+        return spread(lin_final.at[layer], lin_all.at[:, layer], layers + layer)
+
+    def vec_moves():
+        copies = [pltpu.make_async_copy(vec_rows.at[me], vec_got.at[me], vec_sem)]
+        for k, other in enumerate(others):
+            copies.append(remote(vec_rows.at[other], vec_got.at[me], vec_send.at[0, k], vec_recv.at[0, k], (row, other)))
+        return copies
+
+    def states(layer):
+        def one(h, carry):
+            at = layer * part // 2 + h
+            state_own[at] = state_rows(columns_of(params[at]), [ker_final[layer, pl.ds(2 * h + c, 1), :] for c in range(2)])
+            return carry
+
+        lax.fori_loop(0, part // 2, one, 0, unroll=4)
+
+    @pl.when(step == 0)
+    def _():
+        greet([(row, other) for other in others] + [(other, me) for other in rows_of])
+        locals_ = [pltpu.make_async_copy(w_own.at[i], w_all.at[(i,) + place], gather_own.at[2 * i + 1]) for i in range(layers)]
+        run(locals_)
+        run(vec_in_moves())
+        finish_all(locals_)
+        held(1, 0, 0).start()
+        moves = x_moves(0)
+        run(moves[:2])
+        copy = make_kernels(0)
+        copy.start()
+        copy.wait()
+        held(0, 0, 0).start()
+        run(moves[2:])
+        for i in range(1, layers):
+            copy = make_kernels(i)
+            copy.start()
+            copy.wait()
+            for kind in (1, 0):
+                held(kind, i, 0).start()
+        for s in range(bits):
+            gather_next(0, s)
+            if s == 1:
+                run(x_moves(1)[:4])
+            if s == 2:
+                run(x_moves(1)[4:])
+        finish_all(vec_in_moves())
+        for i in range(layers):
+            for c in range(n_chan):
+                vecs[i, c * own : (c + 1) * own, :] = columns_of(vec_in[c, 8 * i : 8 * i + 8, :])[:own]
+        vec_cols[...] = jnp.zeros_like(vec_cols)
+        finish_all(x_moves(0))
+
+    @pl.when(step == 1)
+    def _():
+        for k in range(1, seqs):
+            finish_all(x_moves(k))
+        for k in range(seqs):
+            run(cot_moves(k))
+
+    @pl.when(step < forward_steps)
+    def _():
+        layer, seq = lax.div(step, seqs), lax.rem(step, seqs)
+        stream, hat_out, pre_out, act_out = streams.at[seq], hats.at[seq], pres.at[seq], acts.at[seq]
+        sigma_out, slope_out, spec_out, first = sigmas.at[seq], slopes.at[seq], specs.at[seq], x_low.at[seq]
+        stat, vec, weight = stats.at[layer, seq], vecs.at[layer], w_near.at[layer]
+        hat, mixed = pre_grad, spec_grad
+
+        @pl.when(layer == 0)
+        def _():
+            def widen(rows, _):
+                stream[rows, :] = first[rows, :].astype(jnp.float32)
+
+            steps(chans, STEP_ROWS, widen)
+
+        @pl.when(seq == 0)
+        def _():
+            copy = pltpu.make_async_copy(w_all.at[layer].reshape(2 * chans, chans), weight, load_sem)
+            copy.start()
+            copy.wait()
+            load_kernels(layer)
+
+        @pl.when(layer > 0)
+        def _():
+            finish_all(far_copies(seq, False))
+
+        mean_val, inv_std = token_stats(stream, chans)
+        stat[0:1, :] = mean_val
+        stat[1:2, :] = inv_std
+
+        def normalise(rows, _):
+            v = (stream[rows, :] - stat[0:1, :]) * stat[1:2, :]
+            hat[rows, :] = v
+            hat_out[rows, :] = v.astype(hat_out.dtype)
+            v = v * vec[rows, GAIN : GAIN + 1] + vec[rows, SHIFT : SHIFT + 1]
+            put_folded(folded, rows, fold(*quarters(v)))
+
+        steps(chans, STEP_ROWS, normalise)
+
+        @pl.when(step == 0)
+        def _():
+            gather_next(1, 0)
+
+        def convolve(rows, _):
+            for g, (at, width) in enumerate(GROUPS):
+                spec = dot(get_folded(folded, rows, at, width), table_of(fs, fl, g))
+                spec_out[rows, at : at + width] = spec.astype(jnp.bfloat16)
+                both = product(ker_spec[rows, at : at + width], spec, g == 0, False)
+                mixed[rows, at : at + width] = dot(both.astype(jnp.bfloat16), table_of(ts, tl, g))
+
+        steps(chans, CONV_ROWS, convolve)
+
+        @pl.when(step == 0)
+        def _():
+            gather_next(1, 1)
+
+        def activate(rows, _):
+            gain, shift, skip = [vec[rows, k : k + 1] for k in (GAIN, SHIFT, SKIP)]
+            gain, shift = gain * skip, shift * skip
+            for q, value in enumerate(get_unfolded(mixed, rows)):
+                cols = slice(q * QUARTER, (q + 1) * QUARTER)
+                pre = value + (gain * hat[rows, cols] + shift)
+                pre_out[rows, cols] = pre.astype(pre_out.dtype)
+                soft = jnp.tanh(pre * (GELU_A + GELU_B * (pre * pre)))
+                act_out[rows, cols] = (0.5 * pre * (1.0 + soft)).astype(jnp.bfloat16)
+
+        steps(chans, STEP_ROWS, activate)
+
+        @pl.when(step == 0)
+        def _():
+            gather_next(1, 2)
+
+        block = 2 * LIN_ROWS
+        for t in range(4):
+            cols = slice(t * QUARTER, (t + 1) * QUARTER)
+
+            def linear(rows, k, cols=cols):
+                mixed[:block, :QUARTER] = dot(weight[rows, :], act_out[:, cols])
+                for o in range(LIN_ROWS // 16):
+                    at = pl.ds(pl.multiple_of(k * LIN_ROWS + o * 16, 16), 16)
+                    gate = mixed[o * 32 : o * 32 + 16, :QUARTER] + vec[at, BIAS_IN : BIAS_IN + 1]
+                    value = mixed[o * 32 + 16 : o * 32 + 32, :QUARTER] + vec[at, BIAS_VAL : BIAS_VAL + 1]
+                    sigma = 0.5 * jnp.tanh(0.5 * value) + 0.5
+                    gated = gate * sigma
+                    sigma_out[at, cols] = sigma.astype(sigma_out.dtype)
+                    slope_out[at, cols] = (gated - gated * sigma).astype(slope_out.dtype)
+                    moved = stream[at, cols] + mask[seq, :, cols] * gated
+                    stream[at, cols] = moved
+                    back_low[seq, at, cols] = (moved - first[at, cols].astype(jnp.float32)).astype(jnp.bfloat16)
+
+            steps(2 * chans, block, linear)
+
+        @pl.when(step == 0)
+        def _():
+            gather_next(1, 3)
+
+        @pl.when(step == 1)
+        def _():
+            gather_next(1, 4)
+
+        @pl.when(layer == 0)
+        def _():
+            run(far_copies(seq, False))
+
+    @pl.when(step >= forward_steps)
+    def _():
+        turn, seq = lax.div(step - forward_steps, seqs), lax.rem(step - forward_steps, seqs)
+        layer = layers - 1 - turn
+        back, hat, pre, act = streams.at[seq], hats.at[seq], pres.at[seq], acts.at[seq]
+        sigma_in, slope_in, spec, first = sigmas.at[seq], slopes.at[seq], specs.at[seq], x_low.at[seq]
+        stat, vec = stats.at[layer, seq], vecs.at[layer]
+        next_layer = (turn == 1) & (seq == 0)
+        ends = (turn == layers - 1) & (seq == seqs - 1)
+
+        for k in range(seqs):
+
+            @pl.when((turn == 0) & (seq == k))
+            def _(k=k):
+                finish_all(cot_moves(k))
+                copy = pltpu.make_async_copy(cot_all.at[k], x_low.at[k], load_sem)
+                copy.start()
+                run(out_moves(k))
+                copy.wait()
+
+            @pl.when((turn == 1) & (seq == k))
+            def _(k=k):
+                finish_all(far_copies(k, True))
+
+        @pl.when((turn == 0) & (seq > 0))
+        def _():
+            run(far_copies(seq - 1, True))
+
+        @pl.when((turn == 1) & (seq == 0))
+        def _():
+            run(far_copies(seqs - 1, True))
+
+        @pl.when(turn == 0)
+        def _():
+            def widen(rows, _):
+                back[rows, :] = first[rows, :].astype(jnp.float32)
+
+            steps(chans, STEP_ROWS, widen)
+
+        @pl.when(seq == 0)
+        def _():
+            load_kernels(layer)
+            for k in range(4):
+                cols = slice(k * QUARTER, (k + 1) * QUARTER)
+                loaded[:, cols] = jnp.transpose(w_near[layer, cols, :])
+            vec_grad[...] = jnp.zeros_like(vec_grad)
+
+        def gates(rows, k):
+            gated = back[rows, :] * mask[seq]
+            left = (gated * sigma_in[rows, :].astype(jnp.float32)).astype(jnp.bfloat16)
+            right = (gated * slope_in[rows, :].astype(jnp.float32)).astype(jnp.bfloat16)
+            at = pl.multiple_of(k * 32, 32)
+            folded[pl.ds(at, 16), :] = left
+            folded[pl.ds(at + 16, 16), :] = right
+            vec_grad[3, rows, :] += lanes(left.astype(jnp.float32))
+            vec_grad[4, rows, :] += lanes(right.astype(jnp.float32))
+
+        steps(chans, STEP_ROWS, gates)
+
+        width = 2 * chans // total
+        blocks = MAT_ROWS // (2 * width)
+
+        def lin_back(rows, k):
+            value = lax.dot_general(
+                folded[rows, :], act[...], (((1,), (1,)), ((), ())), preferred_element_type=jnp.float32
+            ).reshape(blocks, 2, width, chans)
+            at = pl.ds(k * blocks, blocks)
+
+            @pl.when(seq == 0)
+            def _():
+                lin_grad[layer, at] = value
+
+            @pl.when(seq > 0)
+            def _():
+                lin_grad[layer, at] += value
+
+        steps(2 * chans, MAT_ROWS, lin_back)
+
+        @pl.when(next_layer)
+        def _():
+            for kind in (0, 1):
+                advance(kind, top, 0)
+
+        @pl.when(ends)
+        def _():
+            begin(1, bottom, 0)
+
+        def act_back(rows, _):
+            for t in range(4):
+                cols = slice(t * QUARTER, (t + 1) * QUARTER)
+                pre_grad[rows, cols] = dot(loaded[rows, :], folded[:, cols])
+
+        steps(chans, MAT_ROWS, act_back)
+
+        def gelu_back(rows, _):
+            skip_sum = jnp.zeros((STEP_ROWS, 128), jnp.float32)
+            outs = []
+            for q in range(4):
+                cols = slice(q * QUARTER, (q + 1) * QUARTER)
+                p = pre[rows, cols].astype(jnp.float32)
+                square = p * p
+                soft = jnp.tanh(p * (GELU_A + GELU_B * square))
+                slope = 0.5 * (1.0 + soft) + (0.5 * p) * (1.0 - soft * soft) * (GELU_A + (3.0 * GELU_B) * square)
+                grad = pre_grad[rows, cols] * slope
+                pre_grad[rows, cols] = grad
+                norm = hat[rows, cols].astype(jnp.float32) * vec[rows, GAIN : GAIN + 1] + vec[rows, SHIFT : SHIFT + 1]
+                skip_sum = skip_sum + lanes(grad * norm)
+                outs.append(grad)
+            vec_grad[2, rows, :] += skip_sum
+            put_folded(folded, rows, fold(*outs))
+
+        steps(chans, STEP_ROWS, gelu_back)
+
+        @pl.when(ends)
+        def _():
+            for kind in (0, 1):
+                advance(kind, top, 2)
+            advance(1, bottom, 0)
+
+        sums[...] = jnp.zeros_like(sums)
+
+        @pl.when(seq == 0)
+        def _():
+            spec_grad[...] = jnp.zeros_like(spec_grad)
+
+        def correlate(rows, chunk):
+            for g, (at, width) in enumerate(GROUPS):
+                grad = dot(get_folded(folded, rows, at, width), table_of(fs, fl, g))
+                spec_grad[rows, at : at + width] += product(
+                    spec[rows, at : at + width].astype(jnp.float32), grad, g == 0, True
+                )
+                both = product(ker_spec[rows, at : at + width], grad, g == 0, True)
+                mixed[:, at : at + width] = dot(both.astype(jnp.bfloat16), table_of(ts, tl, g))
+
+            def norm_back(k, carry):
+                here = pl.ds(pl.multiple_of(k * STEP_ROWS, STEP_ROWS), STEP_ROWS)
+                rows = pl.ds(pl.multiple_of(chunk * CHUNK_ROWS + k * STEP_ROWS, STEP_ROWS), STEP_ROWS)
+                skip = vec[rows, SKIP : SKIP + 1]
+                gain = vec[rows, GAIN : GAIN + 1]
+                gain_sum = jnp.zeros((STEP_ROWS, 128), jnp.float32)
+                shift_sum = jnp.zeros((STEP_ROWS, 128), jnp.float32)
+                plain, weighted = [], []
+                for q, part in enumerate(get_unfolded(mixed, here)):
+                    cols = slice(q * QUARTER, (q + 1) * QUARTER)
+                    grad = part + skip * pre_grad[rows, cols]
+                    both = grad * hat[rows, cols].astype(jnp.float32)
+                    gain_sum = gain_sum + lanes(both)
+                    shift_sum = shift_sum + lanes(grad)
+                    cent = grad * gain
+                    pre_grad[rows, cols] = cent
+                    both = both * gain
+                    plain.append(cent[:8] + cent[8:])
+                    weighted.append(both[:8] + both[8:])
+                vec_grad[0, rows, :] += gain_sum
+                vec_grad[1, rows, :] += shift_sum
+                return carry[0] + jnp.concatenate(plain, 1), carry[1] + jnp.concatenate(weighted, 1)
+
+            zero = jnp.zeros((8, BUCKET), jnp.float32)
+            plain, weighted = lax.fori_loop(0, CHUNK_ROWS // STEP_ROWS, norm_back, (zero, zero), unroll=2)
+            sums[0:8, :] += plain
+            sums[8:16, :] += weighted
+
+        steps(chans, CHUNK_ROWS, correlate)
+
+        @pl.when(seq == seqs - 1)
+        def _():
+            def to_time(rows, _):
+                for g, (at, width) in enumerate(GROUPS):
+                    low = spec_grad[rows, at : at + width].astype(jnp.bfloat16)
+                    ker_spec[rows, at : at + width] = dot(low, table_of(ts, tl, g))
+
+            steps(chans, CONV_ROWS, to_time)
+
+            def block_rows(b):
+                return pl.ds(pl.multiple_of(b * part, part), part)
+
+            def write(b, carry):
+                for q, value in enumerate(get_unfolded(ker_spec, block_rows(2 * b + core_bit))):
+                    spec_grad[block_rows(b), q * QUARTER : (q + 1) * QUARTER] = value
+                for q, value in enumerate(get_unfolded(ker_spec, block_rows(2 * b + 1 - core_bit))):
+                    ker_sent[b, :, q * QUARTER : (q + 1) * QUARTER] = value.astype(jnp.bfloat16)
+                return carry
+
+            lax.fori_loop(0, total // 2, write, 0)
+
+        for i in range(layers):
+
+            @pl.when((turn == i) & (seq == seqs - 1))
+            def _(i=i):
+                layer = layers - 1 - i
+                begin(0, layer, 0)
+                if layer == layers - 1:
+                    begin(1, layer, 0)
+                else:
+                    advance(1, layer, 1)
+
+        mean_plain = jnp.sum(sums[0:8, :], 0, keepdims=True) / chans
+        mean_weighted = jnp.sum(sums[8:16, :], 0, keepdims=True) / chans
+        sums[0:1, :] = mean_plain
+        sums[8:9, :] = mean_weighted
+
+        @pl.when(next_layer)
+        def _():
+            for kind in (0, 1):
+                advance(kind, top, 1)
+
+        for k in range(seqs):
+
+            @pl.when((turn == layers - 1) & (seq == k))
+            def _(k=k):
+                finish_all(out_moves(k))
+
+        def finish(rows, _):
+            scaled = hat[rows, :].astype(jnp.float32) * sums[8:9, :]
+            moved = back[rows, :] + stat[1:2, :] * (pre_grad[rows, :] - sums[0:1, :] - scaled)
+            back[rows, :] = moved
+
+        def leave(rows, _):
+            scaled = hat[rows, :].astype(jnp.float32) * sums[8:9, :]
+            moved = back[rows, :] + stat[1:2, :] * (pre_grad[rows, :] - sums[0:1, :] - scaled)
+            back_low[seq, rows, :] = (moved - first[rows, :].astype(jnp.float32)).astype(jnp.bfloat16)
+
+        @pl.when(turn < layers - 1)
+        def _():
+            steps(chans, STEP_ROWS, finish)
+
+        @pl.when(turn == layers - 1)
+        def _():
+            steps(chans, STEP_ROWS, leave)
+
+        for k in range(seqs):
+
+            @pl.when((turn == layers - 1) & (seq == k))
+            def _(k=k):
+                run(in_moves(k))
+
+        @pl.when(ends)
+        def _():
+            for kind in (0, 1):
+                advance(kind, top, 3)
+
+        for i in range(layers):
+
+            @pl.when((turn == i) & (seq == seqs - 1))
+            def _(i=i):
+                layer = layers - 1 - i
+
+                def vec_columns(rows, _):
+                    lane = lax.broadcasted_iota(jnp.int32, (STEP_ROWS, LANES), 1)
+                    out = vec_cols[rows, :]
+                    for kind in range(5):
+                        out = jnp.where(lane == layer * 5 + kind, jnp.sum(vec_grad[kind, rows, :], 1, keepdims=True), out)
+                    vec_cols[rows, :] = out
+
+                steps(chans, STEP_ROWS, vec_columns)
+
+        @pl.when(ends)
+        def _():
+            for c in range(n_chan):
+                vec_rows[c] = columns_of(vec_cols[c * own : (c + 1) * own, :])[:16]
+            run(vec_moves())
+            states(top)
+            run(spreads(0, top) + spreads(1, top))
+            for s in range(last_stage + 1):
+                advance(0, bottom, s)
+                if s + 2 <= last_stage:
+                    advance(1, bottom, s + 2)
+                    if s + 2 == last_stage:
+                        run(spreads(1, bottom))
+                if s == 1:
+                    for copy in vec_moves():
+                        copy.wait()
+                    vec_own[...] = jnp.sum(vec_got[...], 0)
+                    run(spread(vec_own, vec_all, 2 * layers))
+            states(bottom)
+            run(spreads(0, bottom))
+            for k in range(seqs):
+                finish_all(in_moves(k))
+            for i in range(layers):
+                for copy in spreads(0, i) + spreads(1, i):
+                    copy.wait()
+            for copy in spread(vec_own, vec_all, 2 * layers):
+                copy.wait()
+
+
+def train(mask, params, tables, vec_mine, x_own, cot_own, w_own, n_chan, n_batch):
+    own, group = x_own.shape
+    chans, toks = own * n_chan, group // n_chan
+    seqs, layers = toks // BUCKET, w_own.shape[0]
+    bits = halving_bits(n_chan, n_batch)
+    total = 1 << bits
+    part = chans // total
+    low_count, peers = total >> (LOW_STAGE + 1), bits + 1
+    shape, low, full = jax.ShapeDtypeStruct, jnp.bfloat16, jnp.float32
+    vmem, dma = pltpu.VMEM, pltpu.SemaphoreType.DMA
+    there = (2,) * bits
+    slots, wide = (seqs, chans, BUCKET), (seqs, chans, 2 * BUCKET)
+    return pl.pallas_call(
+        functools.partial(train_kernel, n_chan, n_batch),
+        grid=(2 * layers * seqs,),
+        in_specs=[whole(a) for a in (mask, params, *tables, vec_mine)] + [ANYWHERE] * 3,
+        out_specs=[ANYWHERE] * 14,
+        out_shape=[
+            shape((own, group), low),
+            shape((own, group), low),
+            shape((n_batch, layers * part // 2, 8, LANES), full),
+            shape((n_batch, layers, 2 * part, chans), full),
+            shape((n_batch, 16, LANES), full),
+            shape(slots, low),
+            shape((layers,) + there + (part, BUCKET), low),
+            shape((layers,) + there + (2 * part, chans), low),
+        ]
+        + [shape(slots, low)] * 5
+        + [shape(wide, low)],
+        scratch_shapes=[vmem(slots, low)] * 6
+        + [
+            vmem(wide, low),
+            vmem((layers, seqs, 8, BUCKET), full),
+            vmem(slots, full),
+            vmem((chans, 2 * BUCKET), full),
+            vmem((chans, 2 * BUCKET), full),
+            vmem((CHUNK_ROWS, 2 * BUCKET), full),
+            vmem((2 * chans, BUCKET), low),
+            vmem((chans, BUCKET), full),
+            vmem(slots, low),
+            vmem((layers, 2 * chans, chans), low),
+            vmem((chans, BUCKET), low),
+            vmem((16, BUCKET), full),
+            vmem((layers, chans, LANES), full),
+            vmem((n_chan, 16, LANES), full),
+            vmem((part, BUCKET // LANES, LANES), full),
+            vmem((layers, part, BUCKET), low),
+            vmem((layers, total // 2, 2, 2 * part, chans), full),
+            vmem((5, chans, LANES), full),
+            vmem((chans, LANES), full),
+            vmem((n_chan, 16, LANES), full),
+            vmem((n_chan, 16, LANES), full),
+            vmem((16, LANES), full),
+            vmem((3 * total // 8, part, BUCKET), full),
+            vmem((total, part, BUCKET), low),
+            vmem((total, part, BUCKET), low),
+            vmem((3 * total // 8, 2 * part, chans), full),
+            vmem((low_count, 2 * part, chans), full),
+            vmem((total - low_count, 2 * part, chans), full),
+            vmem((low_count, 2 * part, chans), low),
+            vmem((low_count, 2 * part, chans), low),
+            vmem((layers, part, BUCKET), full),
+            vmem((layers, 2 * part, chans), full),
+            vmem((layers * part // 2, 8, LANES), full),
+            dma((4, seqs, n_chan - 1)), dma((4, seqs, n_chan - 1)), dma((4, seqs)),
+            dma((2 * layers, bits)), dma((2 * layers, bits)), dma((2 * layers + 1,)),
+            dma, dma((6, seqs)),
+            dma((2, peers)), dma((2, peers)), pltpu.SemaphoreType.REGULAR((2, peers)),
+            dma((2, n_chan - 1)), dma((2, n_chan - 1)), dma,
+            dma((2 * layers + 1, n_batch - 1)), dma((2 * layers + 1, n_batch - 1)), dma((2 * layers + 1,)),
+        ],
+        compiler_params=pltpu.CompilerParams(vmem_limit_bytes=ROOM, collective_id=1, has_side_effects=True),
+        cost_estimate=pl.CostEstimate(flops=60 * 10**9, bytes_accessed=60 * 2**20, transcendentals=0),
+        name="train",
+    )(mask, params, *tables, vec_mine, x_own, cot_own, w_own)
+
+
+def adam(weight, grad, first, second, rate):
+    first_new = 0.9 * first + 0.1 * grad
+    second_new = 0.999 * second + 0.001 * grad * grad
+    fixed_first = first_new / (1.0 - 0.9**STEP)
+    fixed_second = second_new / (1.0 - 0.999**STEP)
+    new_weight = weight - rate * (fixed_first / (jnp.sqrt(fixed_second) + 1e-08) + 0.01 * weight)
+    return (first_new, second_new, new_weight)
+
+
+def local(
+    inputs, lengths, cotangent, ln_gain, ln_bias, log_step, skip_gain, lin_bias, log_decay, frequency,
+    w_re, w_im, lin_weight, lin_moment, lin_square, vec_moment, vec_square, state_moment, state_square,
+):
+    n_chan = lax.axis_size("chan")
+    n_batch = lax.axis_size("batch")
+    own = inputs.shape[0]
+    chans = own * n_chan
+    toks = inputs.shape[1] // n_chan
+    seqs = toks // BUCKET
+    part = own // n_batch
+    me = lax.axis_index("chan")
+    row = lax.axis_index("batch")
+    lens = lax.dynamic_slice_in_dim(lengths, me * seqs, seqs)
+    places = lax.iota(jnp.int32, BUCKET)
+    valid = (places[None, :] < lens[:, None]).astype(jnp.float32).reshape(seqs, 1, BUCKET)
+    tables = tuple(jnp.asarray(t) for t in transform_tables())
+
+    def mine(a):
+        return lax.dynamic_slice_in_dim(a, row * part, part, 1)
+
+    step_size = jnp.exp(log_step)[..., None]
+    decay_rate = step_size * jnp.exp(log_decay)
+    turn_rate = step_size * frequency
+    powers, total, moment = doubled_powers(decay_rate, turn_rate)
+    params = jnp.stack([mine(a).reshape(LAYERS * part // 2, -1) for a in powers + [w_re / total, w_im / total]], 1)
+    params = jnp.pad(params, ((0, 0), (0, -params.shape[1] % 8), (0, 0)))
+    w_own = mine(lin_weight).transpose(0, 2, 1, 3).reshape(LAYERS, 2 * part, chans).astype(jnp.bfloat16)
+    vec_own = jnp.stack([ln_gain, ln_bias, skip_gain, lin_bias[:, 0], lin_bias[:, 1]], 1)
+    vec_own = jnp.pad(vec_own, ((0, 0), (0, 3), (0, LANES - own))).reshape(8 * LAYERS, LANES)
+    out_delta, in_delta, state_all, lin_all, vec_all, *_ = train(
+        valid, params, tables, vec_own, inputs, cotangent, w_own, n_chan, n_batch
+    )
+    output = inputs.astype(jnp.float32) + out_delta.astype(jnp.float32)
+    input_grad = cotangent.astype(jnp.float32) + in_delta.astype(jnp.float32)
+
+    state_all = state_all.reshape(n_batch, LAYERS, part // 2, 8, 2, LANES // 2)
+    state_all = state_all.transpose(3, 1, 0, 2, 4, 5).reshape(8, LAYERS, own, -1) / total
+    c_re, c_im, d_re, d_im = [state_all[k] for k in range(4)]
+    turn_grad = -(w_re * d_im + w_im * d_re)
+    decay_grad = ((w_re * c_re - w_im * c_im) * (moment / total) - (w_re * d_re - w_im * d_im)) * decay_rate
+    state_total = jnp.stack([decay_grad, turn_grad * step_size, c_re, -c_im], 1)
+    step_total = jnp.sum(decay_grad + turn_grad * turn_rate, -1)
+    lin_total = lin_all.reshape(n_batch, LAYERS, 2, part, chans).transpose(1, 0, 3, 2, 4).reshape(LAYERS, own, 2, chans)
+    vec_sum = jnp.sum(vec_all, 0)[: 5 * LAYERS, :own].reshape(LAYERS, 5, own)
+    vec_total = jnp.stack([vec_sum[:, 0], vec_sum[:, 1], step_total, vec_sum[:, 2], vec_sum[:, 3], vec_sum[:, 4]], 1)
+
+    vec_old = jnp.stack([ln_gain, ln_bias, log_step, skip_gain, lin_bias[:, 0], lin_bias[:, 1]], 1)
+    state_old = jnp.stack([log_decay, frequency, w_re, w_im], 1)
+    lin_first, lin_second, lin_new = adam(lin_weight, lin_total, lin_moment, lin_square, 0.05)
+    vec_first, vec_second, vec_new = adam(vec_old, vec_total, vec_moment, vec_square, 0.2)
+    state_first, state_second, state_new = adam(state_old, state_total, state_moment, state_square, 0.2)
+    return (
+        output, input_grad, lin_first, lin_second, lin_new, vec_first, vec_second, vec_new,
+        state_first, state_second, state_new,
+    )
 
 
 def tables(length):
@@ -55,16 +1149,7 @@
     return jax.nn.gelu(pre_act)
 
 
-def adam(weight, grad, first, second, rate):
-    first_new = 0.9 * first + 0.1 * grad
-    second_new = 0.999 * second + 0.001 * grad * grad
-    fixed_first = first_new / (1.0 - 0.9**STEP)
-    fixed_second = second_new / (1.0 - 0.999**STEP)
-    new_weight = weight - rate * (fixed_first / (jnp.sqrt(fixed_second) + 1e-08) + 0.01 * weight)
-    return (first_new, second_new, new_weight)
-
-
-def local(
+def wide_local(
     inputs,
     lengths,
     cotangent,
@@ -181,6 +1266,11 @@
     )
 
 
+def suits(own_seqs, chans, n_chan, n_batch):
+    powers = n_chan & (n_chan - 1) == 0 and n_batch & (n_batch - 1) == 0
+    return powers and own_seqs == 2 * n_chan and (n_chan, n_batch) == (8, 4) and chans == 16 * n_chan * n_batch
+
+
 def solution(mesh):
     in_specs = (
         P("chan", "batch"),
@@ -216,4 +1306,12 @@
         P(None, None, "chan", None),
         P(None, None, "chan", None),
     )
-    return jax.shard_map(local, mesh=mesh, in_specs=in_specs, out_specs=out_specs, check_vma=False)
+    n_chan = mesh.shape["chan"]
+
+    def run(*args):
+        own_seqs = args[1].shape[0] // mesh.shape["batch"]
+        fits = suits(own_seqs, args[3].shape[1], n_chan, mesh.shape["batch"])
+        body = local if fits else wide_local
+        return jax.shard_map(body, mesh=mesh, in_specs=in_specs, out_specs=out_specs, check_vma=False)(*args)
+
+    return run

time: 2840 us -> 278 us (0.10)
  waiting for transfers between devices: 1510 us -> 0 us
  matrix products: 738 us -> 0 us
  other arithmetic: 517 us -> 16.7 us
  Pallas kernels: 0 us -> 251 us
  local copies, waits for them, and re-layouts: 37.5 us -> 8.54 us
    reduce_scatter x2 -> x0, waiting for transfers between devices: 861 us -> none  [local(): lax.psum_scatter(act_part, 'chan', scatter_dimension=0, tiled=True)]
    dot_general x30 -> x0, matrix products: 738 us -> none  [the longest x4 137 us: mixer(): conv_out = jnp.einsum('csk,lk->csl', prod_re, cos_back, precision=top_prec)]
    reduce_sum x23 -> x2, other arithmetic: 468 us -> 1.71 us  [the longest x1 0.95 us: local(): step_total = jnp.sum(decay_grad + turn_grad * turn_rate, -1)]
    all_gather x2 -> x0, waiting for transfers between devices: 439 us -> none  [local(): act_all = lax.all_gather(act_low, 'chan', axis=0, tiled=True)]
    pallas_call x0 -> x1, Pallas kernels: none -> 251 us  [train(): pl.pallas_call(functools.partial(train_kernel, n_chan, n_batch), grid=(2...]
    psum x5 -> x0, waiting for transfers between devices: 214 us -> none  [the longest x2 134 us: local(): lax.psum((jnp.sum(centred_grad, 0), jnp.sum(centred_grad * centred, 0)),...]
    unnamed x192 -> x43, local copies, waits for them, and re-layouts: 35.1 us -> 1.9 us
  transfers between devices with their start and end apart: 9 -> 0, of which waited for: 8 -> 0; matrix products, arithmetic and copies ran while one was open for 16% -> 0% of each run, Pallas kernels for 0% -> 0%
where the time goes in v3:
time: 278 us; the launch traced here: 277 us
  Pallas kernels  251 us (90%)
  other arithmetic  16.7 us (6%)
  local copies, waits for them, and re-layouts  8.54 us (3%)
    pallas_call x1, Pallas kernels, train(): pl.pallas_call(functools.partial(train_kernel, n_chan, n_batch), grid=(2...  251 us

profile of v3, /device:TPU:0, one launch (start us, length us, event | category | flops | bytes accessed | tf_op | source)
XLA Modules:
  0.0 276.9 jit_solution(13272802400361179285)
XLA Ops:
  0.7 0.7 exp.36
  1.4 1.1 fusion.15
  2.6 0.1 sine_multiply_fusion.1
  2.7 0.1 stack_reshape.64
  3.0 0.1 sine_multiply_fusion.3
  3.1 0.1 stack_reshape.60
  3.2 0.1 stack_reshape.61
  3.5 0.1 sine_multiply_fusion.5
  3.9 0.8 dynamic-slice_divide_fusion
  4.8 0.1 stack_reshape.68
  5.2 0.1 stack_reshape.55
  5.3 0.3 stack.58
  5.6 0.7 pad.8.params
  6.3 0.6 copy.47
  7.0 0.7 compare_convert_fusion.mask
  7.7 0.6 fusion.18.vec_mine
  8.3 250.7 %train.1 = (bf16[64,16384]{1,0:T(8,128)(2,1)}, bf16[64,16384]{1,0:T(8,128)(2,1)}, f32[4,16,8,128]{3,2,1,0:T(8,128)}, f32[4,2,32,512]{3,2,1,0:T(8,128)}, f32[4,16...) custom-call(f32[2,1,1024]{2,1,0:T(1,128)} %compare_convert_fusion.ma, ...), custom_call_target="tpu_custom_call" | custom-call | flops 60000002048 | bytes 62914560 | tf_op jit(solution)/shard_map/train/pallas_call | solution.py:975
  259.1 1.3 reshape.90
  260.4 0.3 copy.50
  260.8 0.1 multiply_bitcast_fusion
  260.9 0.9 add_reduce_fusion
  261.9 1.0 multiply_subtract_fusion.1
  262.9 0.8 reduce_sum.18
  263.7 0.7 stack.66
  264.5 0.7 multiply_subtract_fusion.2
  265.2 0.6 copy.60
  265.8 0.6 copy.61
  266.4 0.6 copy.62
  267.0 4.2 %convert_add_fusion = f32[64,16384]{1,0:T(8,128)} fusion(bf16[64,16384]{1,0:T(8,128)(2,1)} %get-tuple-element.17, bf16[64,16384]{1,0:T(8,128)(2,1)S(1)} %copy-done), kind=kLoop, calls=%fused_computation | loop fusion | flops 3145728 | bytes 8388608 | tf_op jit(solution)/shard_map/add | solution.py:1083
  271.2 2.4 convert_add_fusion.1
  273.6 0.4 copy.48
  274.1 2.9 %multiply_subtract_fusion = (f32[2,64,2,512]{3,2,1,0:T(2,128)}, f32[2,64,2,512]{3,2,1,0:T(2,128)}, f32[2,64,2,512]{3,2,1,0:T(2,128)}) fusion(f32[2,64,2,512]{3,2,1,0:T(2,128)S(1)} %copy-done.5, f32[2,64,2,512]{3,2,1,0:T(2,128)S(1)} %bitcast.78, f32[2,64,2,512]{3,2,1,0:T(2,128)S(1)} %copy-done.7, f32[2,64,2,512]{3,2,1,0:T(2,128)S(1)} %copy-done.8), kind=kLoop, calls=%fused_computation.4 | loop fusion | flops 1966080 | bytes 3670016 | tf_op jit(solution)/shard_map/sub | solution.py:1045
  (62 shorter events, 1.5 us)
Async XLA Ops:
  0.6 5.6 %copy-start.5 = (f32[2,64,2,512]{3,2,1,0:T(2,128)S(1)}, f32[2,64,2,512]{3,2,1,0:T(2,128)}, u32[]{:S(2)}) copy-start(f32[2,64,2,512]{3,2,1,0:T(2,128)} %param.35) | copy-start | bytes 1572868
  0.7 6.3 %copy-start.19 = (s32[16]{0:T(128)S(1)}, s32[16]{0:T(128)}, u32[]{:S(2)}) copy-start(s32[16]{0:T(128)} %param.24) | copy-start | bytes 196
  0.7 7.1 %copy-start.18 = (f32[2,64]{1,0:T(2,128)S(1)}, f32[2,64]{1,0:T(2,128)}, u32[]{:S(2)}) copy-start(f32[2,64]{1,0:T(2,128)} %param.26) | copy-start | bytes 1540
  0.7 7.0 %copy-start.17 = (f32[2,64]{1,0:T(2,128)S(1)}, f32[2,64]{1,0:T(2,128)}, u32[]{:S(2)}) copy-start(f32[2,64]{1,0:T(2,128)} %param.27) | copy-start | bytes 1540
  0.7 7.0 %copy-start.16 = (f32[2,64]{1,0:T(2,128)S(1)}, f32[2,64]{1,0:T(2,128)}, u32[]{:S(2)}) copy-start(f32[2,64]{1,0:T(2,128)} %param.29) | copy-start | bytes 1540
  0.7 7.0 %copy-start.13 = (f32[2,2,64]{2,1,0:T(2,128)S(1)}, f32[2,2,64]{2,1,0:T(2,128)}, u32[]{:S(2)}) copy-start(f32[2,2,64]{2,1,0:T(2,128)} %param.30) | copy-start | bytes 3076
  259.0 1.8 copy-start.3
  259.0 1.8 copy-start.4
  259.0 1.9 copy-start.6
  259.1 2.8 %copy-start.10 = (f32[2,4,64,64]{3,2,1,0:T(8,128)S(1)}, f32[2,4,64,64]{3,2,1,0:T(8,128)}, u32[]{:S(2)}) copy-start(f32[2,4,64,64]{3,2,1,0:T(8,128)} %param.41) | copy-start | bytes 393220
  259.1 2.8 %copy-start.11 = (f32[2,4,64,64]{3,2,1,0:T(8,128)S(1)}, f32[2,4,64,64]{3,2,1,0:T(8,128)}, u32[]{:S(2)}) copy-start(f32[2,4,64,64]{3,2,1,0:T(8,128)} %param.40) | copy-start | bytes 393220
  259.1 2.8 %copy-start.12 = (f32[2,64,64]{2,1,0:T(8,128)S(1)}, f32[2,64,64]{2,1,0:T(8,128)}, u32[]{:S(2)}) copy-start(f32[2,64,64]{2,1,0:T(8,128)} %param.32) | copy-start | bytes 98308
  260.7 3.8 %copy-start.14 = (f32[2,6,64]{2,0,1:T(2,128)S(1)}, f32[2,6,64]{2,0,1:T(2,128)}, u32[]{:S(2)}) copy-start(f32[2,6,64]{2,0,1:T(2,128)} %param.39) | copy-start | bytes 9220
  260.7 6.3 %copy-start = (bf16[64,16384]{1,0:T(8,128)(2,1)S(1)}, bf16[64,16384]{1,0:T(8,128)(2,1)}, u32[]{:S(2)}) copy-start(bf16[64,16384]{1,0:T(8,128)(2,1)} %cot_own.1) | copy-start | bytes 6291460
  261.9 2.6 copy-start.15
  267.0 4.2 %copy-start.1 = (bf16[64,16384]{1,0:T(8,128)(2,1)S(1)}, bf16[64,16384]{1,0:T(8,128)(2,1)}, u32[]{:S(2)}) copy-start(bf16[64,16384]{1,0:T(8,128)(2,1)} %x_own.1) | copy-start | bytes 6291460
  267.0 4.2 %copy-start.2 = (bf16[64,16384]{1,0:T(8,128)(2,1)S(1)}, bf16[64,16384]{1,0:T(8,128)(2,1)}, u32[]{:S(2)}) copy-start(bf16[64,16384]{1,0:T(8,128)(2,1)} %get-tuple-element.16) | copy-start | bytes 6291460
  271.2 2.5 copy-start.9
  271.2 2.9 %copy-start.7 = (f32[2,64,2,512]{3,2,1,0:T(2,128)S(1)}, f32[2,64,2,512]{3,2,1,0:T(2,128)}, u32[]{:S(2)}) copy-start(f32[2,64,2,512]{3,2,1,0:T(2,128)} %param.37) | copy-start | bytes 1572868
  271.2 2.9 %copy-start.8 = (f32[2,64,2,512]{3,2,1,0:T(2,128)S(1)}, f32[2,64,2,512]{3,2,1,0:T(2,128)}, u32[]{:S(2)}) copy-start(f32[2,64,2,512]{3,2,1,0:T(2,128)} %param.36) | copy-start | bytes 1572868

commit v4 on v3

--- a/solution.py
+++ b/solution.py
@@ -18,9 +18,9 @@
 HALF_ROOT = math.sqrt(0.5)
 STEP_ROWS = 16
 UNROLL = 4
-CONV_ROWS = 256
+CONV_ROWS = 512
 CHUNK_ROWS = 256
-MAT_ROWS = 256
+MAT_ROWS = 512
 LIN_ROWS = 256
 ROOM = 59 * 2**20
 GROUPS = ((0, 256), (256, 256), (512, 512), (1024, 512), (1536, 512))
@@ -185,10 +185,11 @@
     return me, row, others
 
 
-def greet(targets):
+def greet(targets, between):
     barrier = pltpu.get_barrier_semaphore()
     for target in targets:
         pl.semaphore_signal(barrier, inc=1, device_id=target, device_id_type=MESH)
+    between()
     pl.semaphore_wait(barrier, len(targets))
 
 
@@ -204,17 +205,20 @@
     return out + [(bit_of(row, k), (flip(row, k), me)) for k in reversed(range(batch_bits))]
 
 
-def doubled_powers(decay_rate, turn_rate):
+def mode_rows(raw):
+    step_size = jnp.exp(raw[4])
+    decay_rate, turn_rate = step_size * jnp.exp(raw[0]), step_size * raw[1]
     spans = [2.0**k for k in range(BUCKET.bit_length() - 1)]
     sizes = [jnp.exp(-span * decay_rate) for span in spans]
     total, moment = jnp.ones_like(decay_rate), jnp.zeros_like(decay_rate)
     for span, size in zip(spans, sizes):
         moment = moment * (1.0 + size) + span * size * total
         total = total * (1.0 + size)
-    powers = []
+    rows = []
     for span, size in list(zip(spans, sizes))[:POWERS]:
-        powers += [size * jnp.cos(span * turn_rate), size * jnp.sin(span * turn_rate)]
-    return powers, total, moment
+        rows += [size * jnp.cos(span * turn_rate), size * jnp.sin(span * turn_rate)]
+    inverse = 1.0 / total
+    return rows + [raw[2] * inverse, raw[3] * inverse, inverse, moment * inverse, decay_rate, turn_rate, step_size, raw[2], raw[3]]
 
 
 def times(a, b):
@@ -256,7 +260,8 @@
     return [jnp.concatenate([row[c] for row in out], 0) for c in range(2)]
 
 
-def state_rows(params, grads):
+def state_rows(modes, grads):
+    params = columns_of(modes)
     value, far = near_powers(params)
     half = params.shape[0] // 2
     place = lax.broadcasted_iota(jnp.int32, (1, LANES), 1).astype(jnp.float32)
@@ -275,7 +280,14 @@
     out = jnp.zeros_like(value[0])
     for k, col in enumerate(cols):
         out = jnp.where(lane == k, jnp.sum(col, 1, keepdims=True), out)
-    return jnp.transpose(out)[:8]
+    out = jnp.transpose(out)
+    at = 2 * POWERS + 2
+    inverse, moment, decay_rate, turn_rate, step_size, w_re, w_im = [modes[at + k : at + k + 1] for k in range(7)]
+    c_re, c_im, d_re, d_im = [out[k : k + 1] * inverse for k in range(4)]
+    turn_grad = -(w_re * d_im + w_im * d_re)
+    decay_grad = ((w_re * c_re - w_im * c_im) * moment - (w_re * d_re - w_im * d_im)) * decay_rate
+    result = [decay_grad, turn_grad * step_size, c_re, -c_im, decay_grad + turn_grad * turn_rate]
+    return jnp.concatenate(result + [jnp.zeros_like(c_re)] * 3, 0)
 
 
 def remote(src, dst, send, recv, target):
@@ -293,14 +305,14 @@
 
 
 ANYWHERE = pl.BlockSpec(memory_space=pl.ANY)
-GATHER_ORDER = ((0, 1, 2, 3, 4), (0, 1, 3, 2, 4))
+GATHER_ORDER = (((0,), (1, 2), (3,), (4,)), ((0,), (3,), (1, 2), (4,)))
 
 
 def train_kernel(
-    n_chan, n_batch, mask, params, fs, fl, ts, tl, vec_mine, x_own, cot_own, w_own,
+    n_chan, n_batch, mask, raw, fs, fl, ts, tl, vec_mine, x_own, cot_own, w_own,
     out_all, in_all, state_all, lin_all, vec_all, cot_all, ker_all, w_all,
     hat_far, pre_far, act_far, sigma_far, slope_far, spec_far,
-    x_low, hats, pres, acts, sigmas, slopes, specs, stats, streams, ker_spec, spec_grad, mixed, folded, pre_grad, back_low,
+    params, x_low, hats, pres, acts, sigmas, slopes, specs, stats, streams, ker_spec, spec_grad, mixed, folded, pre_grad, back_low,
     w_near, loaded, sums, vecs, vec_in, ker_rows, ker_low,
     lin_grad, vec_grad, vec_cols, vec_rows, vec_got, vec_own,
     ker_sums, ker_sent, ker_got, lin_sums, lin_sent, lin_got, low_sent, low_got, ker_final, lin_final, state_own,
@@ -359,16 +371,27 @@
 
     def held(kind, i, s):
         order = GATHER_ORDER[kind]
+        done = [d for group in order[:s] for d in group]
         ref = (ker_all if kind == 0 else w_all).at[i]
-        ref = ref.at[tuple(slice(None) if d in order[:s] else place[d] for d in range(bits))]
-        k = 2 * i + kind
-        return remote(ref, ref, gather_send.at[k, s], gather_recv.at[k, s], above[order[s]][1])
+        ref = ref.at[tuple(slice(None) if d in done else place[d] for d in range(bits))]
+        slot = sum((1 << len(group)) - 1 for group in order[:s])
+        copies = []
+        for mask in range(1, 1 << len(order[s])):
+            chan, batch = me, row
+            for t, d in enumerate(order[s]):
+                if mask >> t & 1 and d < bits - batch_bits:
+                    chan = flip(chan, bits - batch_bits - 1 - d)
+                elif mask >> t & 1:
+                    batch = flip(batch, bits - 1 - d)
+            k, slot = 2 * i + kind, slot + 1
+            copies.append(remote(ref, ref, gather_send.at[k, slot - 1], gather_recv.at[k, slot - 1], (batch, chan)))
+        return copies
 
     def gather_next(i, s):
         for kind in (1, 0):
-            held(kind, i, s).wait()
-            if s + 1 < bits:
-                held(kind, i, s + 1).start()
+            finish_all(held(kind, i, s))
+            if s + 1 < len(GATHER_ORDER[kind]):
+                run(held(kind, i, s + 1))
 
     def vec_in_moves():
         copies = [pltpu.make_async_copy(vec_mine, vec_in.at[me], gather_own.at[2 * layers])]
@@ -525,38 +548,39 @@
     def states(layer):
         def one(h, carry):
             at = layer * part // 2 + h
-            state_own[at] = state_rows(columns_of(params[at]), [ker_final[layer, pl.ds(2 * h + c, 1), :] for c in range(2)])
+            state_own[at] = state_rows(params[at], [ker_final[layer, pl.ds(2 * h + c, 1), :] for c in range(2)])
             return carry
 
         lax.fori_loop(0, part // 2, one, 0, unroll=4)
 
     @pl.when(step == 0)
     def _():
-        greet([(row, other) for other in others] + [(other, me) for other in rows_of])
         locals_ = [pltpu.make_async_copy(w_own.at[i], w_all.at[(i,) + place], gather_own.at[2 * i + 1]) for i in range(layers)]
-        run(locals_)
-        run(vec_in_moves())
-        finish_all(locals_)
-        held(1, 0, 0).start()
+
+        def prepare():
+            run(locals_)
+            for k, value in enumerate(mode_rows([raw[k] for k in range(5)])):
+                params[:, k, :] = value
+            copy = make_kernels(0)
+            copy.start()
+            finish_all(locals_ + [copy])
+
+        greet([(row, other) for other in others] + [(other, me) for other in rows_of], prepare)
+        run(held(0, 0, 0) + held(1, 0, 0) + vec_in_moves())
         moves = x_moves(0)
-        run(moves[:2])
-        copy = make_kernels(0)
-        copy.start()
-        copy.wait()
-        held(0, 0, 0).start()
-        run(moves[2:])
+        run(moves[:4])
+        gather_next(0, 0)
+        run(moves[4:])
         for i in range(1, layers):
             copy = make_kernels(i)
             copy.start()
             copy.wait()
-            for kind in (1, 0):
-                held(kind, i, 0).start()
-        for s in range(bits):
-            gather_next(0, s)
-            if s == 1:
-                run(x_moves(1)[:4])
-            if s == 2:
-                run(x_moves(1)[4:])
+        gather_next(0, 1)
+        gather_next(0, 2)
+        run(x_moves(1))
+        for i in range(1, layers):
+            run(held(1, i, 0) + held(0, i, 0))
+        gather_next(0, 3)
         finish_all(vec_in_moves())
         for i in range(layers):
             for c in range(n_chan):
@@ -568,8 +592,7 @@
     def _():
         for k in range(1, seqs):
             finish_all(x_moves(k))
-        for k in range(seqs):
-            run(cot_moves(k))
+        run(cot_moves(0))
 
     @pl.when(step < forward_steps)
     def _():
@@ -610,9 +633,10 @@
 
         steps(chans, STEP_ROWS, normalise)
 
-        @pl.when(step == 0)
-        def _():
-            gather_next(1, 0)
+        @pl.when(step == forward_steps - 2)
+        def _():
+            for k in range(1, seqs):
+                run(cot_moves(k))
 
         def convolve(rows, _):
             for g, (at, width) in enumerate(GROUPS):
@@ -625,7 +649,11 @@
 
         @pl.when(step == 0)
         def _():
-            gather_next(1, 1)
+            gather_next(1, 0)
+
+        @pl.when(step == 1)
+        def _():
+            gather_next(1, 2)
 
         def activate(rows, _):
             gain, shift, skip = [vec[rows, k : k + 1] for k in (GAIN, SHIFT, SKIP)]
@@ -638,10 +666,6 @@
                 act_out[rows, cols] = (0.5 * pre * (1.0 + soft)).astype(jnp.bfloat16)
 
         steps(chans, STEP_ROWS, activate)
-
-        @pl.when(step == 0)
-        def _():
-            gather_next(1, 2)
 
         block = 2 * LIN_ROWS
         for t in range(4):
@@ -665,11 +689,11 @@
 
         @pl.when(step == 0)
         def _():
+            gather_next(1, 1)
+
+        @pl.when(step == 1)
+        def _():
             gather_next(1, 3)
-
-        @pl.when(step == 1)
-        def _():
-            gather_next(1, 4)
 
         @pl.when(layer == 0)
         def _():
@@ -692,7 +716,8 @@
                 finish_all(cot_moves(k))
                 copy = pltpu.make_async_copy(cot_all.at[k], x_low.at[k], load_sem)
                 copy.start()
-                run(out_moves(k))
+                if k > 0:
+                    run(out_moves(k))
                 copy.wait()
 
             @pl.when((turn == 1) & (seq == k))
@@ -716,7 +741,10 @@
 
         @pl.when(seq == 0)
         def _():
-            load_kernels(layer)
+            @pl.when(turn > 0)
+            def _():
+                load_kernels(layer)
+
             for k in range(4):
                 cols = slice(k * QUARTER, (k + 1) * QUARTER)
                 loaded[:, cols] = jnp.transpose(w_near[layer, cols, :])
@@ -752,11 +780,6 @@
                 lin_grad[layer, at] += value
 
         steps(2 * chans, MAT_ROWS, lin_back)
-
-        @pl.when(next_layer)
-        def _():
-            for kind in (0, 1):
-                advance(kind, top, 0)
 
         @pl.when(ends)
         def _():
@@ -788,11 +811,14 @@
 
         steps(chans, STEP_ROWS, gelu_back)
 
-        @pl.when(ends)
+        @pl.when((turn == 0) & (seq == 0))
+        def _():
+            run(out_moves(0))
+
+        @pl.when(next_layer)
         def _():
             for kind in (0, 1):
-                advance(kind, top, 2)
-            advance(1, bottom, 0)
+                advance(kind, top, 0)
 
         sums[...] = jnp.zeros_like(sums)
 
@@ -869,7 +895,9 @@
                 if layer == layers - 1:
                     begin(1, layer, 0)
                 else:
-                    advance(1, layer, 1)
+                    advance(1, layer, 0)
+                    for kind in (0, 1):
+                        advance(kind, top, 2)
 
         mean_plain = jnp.sum(sums[0:8, :], 0, keepdims=True) / chans
         mean_weighted = jnp.sum(sums[8:16, :], 0, keepdims=True) / chans
@@ -910,11 +938,6 @@
             @pl.when((turn == layers - 1) & (seq == k))
             def _(k=k):
                 run(in_moves(k))
-
-        @pl.when(ends)
-        def _():
-            for kind in (0, 1):
-                advance(kind, top, 3)
 
         for i in range(layers):
 
@@ -936,19 +959,21 @@
             for c in range(n_chan):
                 vec_rows[c] = columns_of(vec_cols[c * own : (c + 1) * own, :])[:16]
             run(vec_moves())
+            advance(0, bottom, 0)
+            advance(1, bottom, 1)
+            for kind in (0, 1):
+                advance(kind, top, last_stage)
+            run(spreads(1, top))
+            advance(0, bottom, 1)
             states(top)
-            run(spreads(0, top) + spreads(1, top))
-            for s in range(last_stage + 1):
-                advance(0, bottom, s)
-                if s + 2 <= last_stage:
-                    advance(1, bottom, s + 2)
-                    if s + 2 == last_stage:
-                        run(spreads(1, bottom))
-                if s == 1:
-                    for copy in vec_moves():
-                        copy.wait()
-                    vec_own[...] = jnp.sum(vec_got[...], 0)
-                    run(spread(vec_own, vec_all, 2 * layers))
+            run(spreads(0, top))
+            finish_all(vec_moves())
+            vec_own[...] = jnp.sum(vec_got[...], 0)
+            run(spread(vec_own, vec_all, 2 * layers))
+            for s in range(2, last_stage + 1):
+                for kind in (1, 0):
+                    advance(kind, bottom, s)
+            run(spreads(1, bottom))
             states(bottom)
             run(spreads(0, bottom))
             for k in range(seqs):
@@ -960,7 +985,7 @@
                 copy.wait()
 
 
-def train(mask, params, tables, vec_mine, x_own, cot_own, w_own, n_chan, n_batch):
+def train(mask, raw, tables, vec_mine, x_own, cot_own, w_own, n_chan, n_batch):
     own, group = x_own.shape
     chans, toks = own * n_chan, group // n_chan
     seqs, layers = toks // BUCKET, w_own.shape[0]
@@ -975,7 +1000,7 @@
     return pl.pallas_call(
         functools.partial(train_kernel, n_chan, n_batch),
         grid=(2 * layers * seqs,),
-        in_specs=[whole(a) for a in (mask, params, *tables, vec_mine)] + [ANYWHERE] * 3,
+        in_specs=[whole(a) for a in (mask, raw, *tables, vec_mine)] + [ANYWHERE] * 3,
         out_specs=[ANYWHERE] * 14,
         out_shape=[
             shape((own, group), low),
@@ -989,7 +1014,8 @@
         ]
         + [shape(slots, low)] * 5
         + [shape(wide, low)],
-        scratch_shapes=[vmem(slots, low)] * 6
+        scratch_shapes=[vmem((layers * part // 2, 32, LANES), full)]
+        + [vmem(slots, low)] * 6
         + [
             vmem(wide, low),
             vmem((layers, seqs, 8, BUCKET), full),
@@ -1025,7 +1051,7 @@
             vmem((layers, 2 * part, chans), full),
             vmem((layers * part // 2, 8, LANES), full),
             dma((4, seqs, n_chan - 1)), dma((4, seqs, n_chan - 1)), dma((4, seqs)),
-            dma((2 * layers, bits)), dma((2 * layers, bits)), dma((2 * layers + 1,)),
+            dma((2 * layers, peers)), dma((2 * layers, peers)), dma((2 * layers + 1,)),
             dma, dma((6, seqs)),
             dma((2, peers)), dma((2, peers)), pltpu.SemaphoreType.REGULAR((2, peers)),
             dma((2, n_chan - 1)), dma((2, n_chan - 1)), dma,
@@ -1034,7 +1060,7 @@
         compiler_params=pltpu.CompilerParams(vmem_limit_bytes=ROOM, collective_id=1, has_side_effects=True),
         cost_estimate=pl.CostEstimate(flops=60 * 10**9, bytes_accessed=60 * 2**20, transcendentals=0),
         name="train",
-    )(mask, params, *tables, vec_mine, x_own, cot_own, w_own)
+    )(mask, raw, *tables, vec_mine, x_own, cot_own, w_own)
 
 
 def adam(weight, grad, first, second, rate):
@@ -1067,28 +1093,22 @@
     def mine(a):
         return lax.dynamic_slice_in_dim(a, row * part, part, 1)
 
-    step_size = jnp.exp(log_step)[..., None]
-    decay_rate = step_size * jnp.exp(log_decay)
-    turn_rate = step_size * frequency
-    powers, total, moment = doubled_powers(decay_rate, turn_rate)
-    params = jnp.stack([mine(a).reshape(LAYERS * part // 2, -1) for a in powers + [w_re / total, w_im / total]], 1)
-    params = jnp.pad(params, ((0, 0), (0, -params.shape[1] % 8), (0, 0)))
+    step_all = jnp.broadcast_to(log_step[..., None], log_decay.shape)
+    raw = jnp.stack([mine(a) for a in (log_decay, frequency, w_re, w_im, step_all)])
+    raw = raw.reshape(5, LAYERS * part // 2, LANES)
     w_own = mine(lin_weight).transpose(0, 2, 1, 3).reshape(LAYERS, 2 * part, chans).astype(jnp.bfloat16)
     vec_own = jnp.stack([ln_gain, ln_bias, skip_gain, lin_bias[:, 0], lin_bias[:, 1]], 1)
     vec_own = jnp.pad(vec_own, ((0, 0), (0, 3), (0, LANES - own))).reshape(8 * LAYERS, LANES)
     out_delta, in_delta, state_all, lin_all, vec_all, *_ = train(
-        valid, params, tables, vec_own, inputs, cotangent, w_own, n_chan, n_batch
+        valid, raw, tables, vec_own, inputs, cotangent, w_own, n_chan, n_batch
     )
     output = inputs.astype(jnp.float32) + out_delta.astype(jnp.float32)
     input_grad = cotangent.astype(jnp.float32) + in_delta.astype(jnp.float32)
 
     state_all = state_all.reshape(n_batch, LAYERS, part // 2, 8, 2, LANES // 2)
-    state_all = state_all.transpose(3, 1, 0, 2, 4, 5).reshape(8, LAYERS, own, -1) / total
-    c_re, c_im, d_re, d_im = [state_all[k] for k in range(4)]
-    turn_grad = -(w_re * d_im + w_im * d_re)
-    decay_grad = ((w_re * c_re - w_im * c_im) * (moment / total) - (w_re * d_re - w_im * d_im)) * decay_rate
-    state_total = jnp.stack([decay_grad, turn_grad * step_size, c_re, -c_im], 1)
-    step_total = jnp.sum(decay_grad + turn_grad * turn_rate, -1)
+    state_all = state_all.transpose(1, 3, 0, 2, 4, 5).reshape(LAYERS, 8, own, -1)
+    state_total = state_all[:, :4]
+    step_total = jnp.sum(state_all[:, 4], -1)
     lin_total = lin_all.reshape(n_batch, LAYERS, 2, part, chans).transpose(1, 0, 3, 2, 4).reshape(LAYERS, own, 2, chans)
     vec_sum = jnp.sum(vec_all, 0)[: 5 * LAYERS, :own].reshape(LAYERS, 5, own)
     vec_total = jnp.stack([vec_sum[:, 0], vec_sum[:, 1], step_total, vec_sum[:, 2], vec_sum[:, 3], vec_sum[:, 4]], 1)

time: 278 us -> 260 us (0.935)
  Pallas kernels: 251 us -> 234 us
  other arithmetic: 16.7 us -> 13.6 us
    pallas_call x1, Pallas kernels: 251 us -> 234 us  [train(): pl.pallas_call(functools.partial(train_kernel, n_chan, n_batch), grid=(2...]
where the time goes in v4:
time: 260 us; the launch traced here: 259 us
  Pallas kernels  234 us (90%)
  other arithmetic  13.6 us (5%)
  local copies, waits for them, and re-layouts  10.8 us (4%)
    pallas_call x1, Pallas kernels, train(): pl.pallas_call(functools.partial(train_kernel, n_chan, n_batch), grid=(2...  234 us
    sub x3, other arithmetic, adam(): weight - rate * (fixed_first / (jnp.sqrt(fixed_second) + 1e-08) + 0.01 *...  5.65 us

profile of v4, /device:TPU:0, one launch (start us, length us, event | category | flops | bytes accessed | tf_op | source)
XLA Modules:
  0.0 259.0 jit_solution(16564348243945456378)
XLA Ops:
  0.6 0.7 constant_dynamic-slice_fusion.3
  1.4 0.1 stack.65
  1.5 0.1 stack.66
  1.6 0.7 constant_dynamic-slice_fusion.1
  2.3 0.1 stack.67
  2.4 0.1 stack.68
  2.4 0.8 constant_dynamic-slice_fusion
  3.2 0.1 stack.69
  3.3 0.1 stack.70
  3.4 1.0 fusion.2
  4.3 0.6 copy.44
  5.0 0.7 dynamic_slice.21
  5.7 0.7 compare_convert_fusion.mask
  6.4 1.3 fusion.4.vec_mine
  7.7 0.0 copy-start.12
  7.7 233.8 %train.1 = (bf16[64,16384]{1,0:T(8,128)(2,1)}, bf16[64,16384]{1,0:T(8,128)(2,1)}, f32[4,16,8,128]{3,2,1,0:T(8,128)}, f32[4,2,32,512]{3,2,1,0:T(8,128)}, f32[4,16...) custom-call(f32[2,1,1024]{2,1,0:T(1,128)} %compare_convert_fusion.ma, ...), custom_call_target="tpu_custom_call" | custom-call | flops 60000002048 | bytes 62914560 | tf_op jit(solution)/shard_map/train/pallas_call | solution.py:1000
  241.5 0.0 copy-start.9
  241.5 1.3 reshape.92
  242.9 0.2 copy.47
  243.2 0.1 slice_reduce_fusion
  243.3 0.9 reduce_sum.18
  244.2 0.7 stack.79
  244.9 0.7 multiply_subtract_fusion.2
  245.6 0.6 copy.54
  246.2 0.6 copy.55
  246.8 0.6 copy.56
  247.4 2.0 multiply_subtract_fusion.1
  249.5 0.4 copy.45
  249.9 2.9 %multiply_subtract_fusion = (f32[2,64,2,512]{3,2,1,0:T(2,128)}, f32[2,64,2,512]{3,2,1,0:T(2,128)}, f32[2,64,2,512]{3,2,1,0:T(2,128)}) fusion(f32[2,64,2,512]{3,2,1,0:T(2,128)S(1)} %copy-done.4, f32[2,64,2,512]{3,2,1,0:T(2,128)S(1)} %bitcast.33, f32[2,64,2,512]{3,2,1,0:T(2,128)S(1)} %copy-done.5, f32[2,64,2,512]{3,2,1,0:T(2,128)S(1)} %copy-done.6), kind=kLoop, calls=%fused_computation.4 | loop fusion | flops 1966080 | bytes 3670016 | tf_op jit(solution)/shard_map/sub | solution.py:1071
  252.8 2.5 convert_add_fusion
  255.4 1.2 copy-done.2
  256.6 2.4 convert_add_fusion.1
  (35 shorter events, 0.1 us)
Async XLA Ops:
  3.4 4.4 %copy-start.14 = (f32[5,16,128]{2,1,0:T(8,128)}, f32[5,16,128]{2,1,0:T(8,128)S(1)}, u32[]{:S(2)}) copy-start(f32[5,16,128]{2,1,0:T(8,128)S(1)} %constant_dynamic-update-slice_fusion.raw) | copy-start | bytes 122884
  7.7 236.5 %copy-start.11 = (f32[2,2,64]{2,1,0:T(2,128)S(1)}, f32[2,2,64]{2,1,0:T(2,128)}, u32[]{:S(2)}) copy-start(f32[2,2,64]{2,1,0:T(2,128)} %param.30) | copy-start | bytes 3076
  7.7 236.5 %copy-start.13 = (f32[2,64]{1,0:T(2,128)S(1)}, f32[2,64]{1,0:T(2,128)}, u32[]{:S(2)}) copy-start(f32[2,64]{1,0:T(2,128)} %param.28) | copy-start | bytes 1540
  7.7 237.2 %copy-start.12 = (f32[2,6,64]{2,0,1:T(2,128)S(1)}, f32[2,6,64]{2,0,1:T(2,128)}, u32[]{:S(2)}) copy-start(f32[2,6,64]{2,0,1:T(2,128)} %param.39) | copy-start | bytes 9220
  241.5 5.9 %copy-start.8 = (f32[2,4,64,64]{3,2,1,0:T(8,128)S(1)}, f32[2,4,64,64]{3,2,1,0:T(8,128)}, u32[]{:S(2)}) copy-start(f32[2,4,64,64]{3,2,1,0:T(8,128)} %param.41) | copy-start | bytes 393220
  241.5 5.9 %copy-start.9 = (f32[2,64,64]{2,1,0:T(8,128)S(1)}, f32[2,64,64]{2,1,0:T(8,128)}, u32[]{:S(2)}) copy-start(f32[2,64,64]{2,1,0:T(8,128)} %param.32) | copy-start | bytes 98308
  241.5 5.9 %copy-start.10 = (f32[2,64,64]{2,1,0:T(8,128)S(1)}, f32[2,64,64]{2,1,0:T(8,128)}, u32[]{:S(2)}) copy-start(f32[2,64,64]{2,1,0:T(8,128)} %param.31) | copy-start | bytes 98308
  241.5 8.0 %copy-start.7 = (f32[4,2,32,512]{3,2,1,0:T(8,128)S(1)}, f32[4,2,32,512]{3,2,1,0:T(8,128)}, u32[]{:S(2)}) copy-start(f32[4,2,32,512]{3,2,1,0:T(8,128)} %get-tuple-element.18) | copy-start | bytes 1572868
  242.9 7.0 %copy-start.4 = (f32[2,64,2,512]{3,2,1,0:T(2,128)S(1)}, f32[2,64,2,512]{3,2,1,0:T(2,128)}, u32[]{:S(2)}) copy-start(f32[2,64,2,512]{3,2,1,0:T(2,128)} %param.35) | copy-start | bytes 1572868
  242.9 7.0 %copy-start.5 = (f32[2,64,2,512]{3,2,1,0:T(2,128)S(1)}, f32[2,64,2,512]{3,2,1,0:T(2,128)}, u32[]{:S(2)}) copy-start(f32[2,64,2,512]{3,2,1,0:T(2,128)} %param.37) | copy-start | bytes 1572868
  242.9 7.0 %copy-start.6 = (f32[2,64,2,512]{3,2,1,0:T(2,128)S(1)}, f32[2,64,2,512]{3,2,1,0:T(2,128)}, u32[]{:S(2)}) copy-start(f32[2,64,2,512]{3,2,1,0:T(2,128)} %param.36) | copy-start | bytes 1572868
  249.5 3.3 %copy-start.3 = (bf16[64,16384]{1,0:T(8,128)(2,1)S(1)}, bf16[64,16384]{1,0:T(8,128)(2,1)}, u32[]{:S(2)}) copy-start(bf16[64,16384]{1,0:T(8,128)(2,1)} %get-tuple-element.17) | copy-start | bytes 6291460
  249.9 2.9 %copy-start = (bf16[64,16384]{1,0:T(8,128)(2,1)S(1)}, bf16[64,16384]{1,0:T(8,128)(2,1)}, u32[]{:S(2)}) copy-start(bf16[64,16384]{1,0:T(8,128)(2,1)} %cot_own.1) | copy-start | bytes 6291460
  252.8 2.6 copy-start.1
  252.8 3.7 %copy-start.2 = (bf16[64,16384]{1,0:T(8,128)(2,1)S(1)}, bf16[64,16384]{1,0:T(8,128)(2,1)}, u32[]{:S(2)}) copy-start(bf16[64,16384]{1,0:T(8,128)(2,1)} %get-tuple-element.16) | copy-start | bytes 6291460

commit v5 on v4

--- a/solution.py
+++ b/solution.py
@@ -332,6 +332,7 @@
     bits, batch_bits = len(path), n_batch.bit_length() - 1
     total = 1 << bits
     core_bit = path[0][0]
+    near = n_chan // 2
     top, bottom = layers - 1, 0
     mine = pl.ds(pl.multiple_of(me * own, own), own)
 
@@ -557,27 +558,24 @@
     def _():
         locals_ = [pltpu.make_async_copy(w_own.at[i], w_all.at[(i,) + place], gather_own.at[2 * i + 1]) for i in range(layers)]
 
-        def prepare():
-            run(locals_)
-            for k, value in enumerate(mode_rows([raw[k] for k in range(5)])):
-                params[:, k, :] = value
-            copy = make_kernels(0)
-            copy.start()
-            finish_all(locals_ + [copy])
-
-        greet([(row, other) for other in others] + [(other, me) for other in rows_of], prepare)
-        run(held(0, 0, 0) + held(1, 0, 0) + vec_in_moves())
-        moves = x_moves(0)
-        run(moves[:4])
-        gather_next(0, 0)
-        run(moves[4:])
+        greet([(row, other) for other in others] + [(other, me) for other in rows_of], lambda: run(locals_))
+        finish_all(locals_)
+        run(held(1, 0, 0))
+        run(x_moves(0))
+        for k, value in enumerate(mode_rows([raw[k] for k in range(5)])):
+            params[:, k, :] = value
+        copy = make_kernels(0)
+        copy.start()
+        copy.wait()
+        run(held(0, 0, 0) + vec_in_moves())
         for i in range(1, layers):
             copy = make_kernels(i)
             copy.start()
             copy.wait()
+        gather_next(0, 0)
         gather_next(0, 1)
+        run(x_moves(1))
         gather_next(0, 2)
-        run(x_moves(1))
         for i in range(1, layers):
             run(held(1, i, 0) + held(0, i, 0))
         gather_next(0, 3)
@@ -681,7 +679,7 @@
                     gated = gate * sigma
                     sigma_out[at, cols] = sigma.astype(sigma_out.dtype)
                     slope_out[at, cols] = (gated - gated * sigma).astype(slope_out.dtype)
-                    moved = stream[at, cols] + mask[seq, :, cols] * gated
+                    moved = stream[at, cols] + mask[me * seqs + seq, :, cols] * gated
                     stream[at, cols] = moved
                     back_low[seq, at, cols] = (moved - first[at, cols].astype(jnp.float32)).astype(jnp.bfloat16)
 
@@ -751,7 +749,7 @@
             vec_grad[...] = jnp.zeros_like(vec_grad)
 
         def gates(rows, k):
-            gated = back[rows, :] * mask[seq]
+            gated = back[rows, :] * mask[me * seqs + seq]
             left = (gated * sigma_in[rows, :].astype(jnp.float32)).astype(jnp.bfloat16)
             right = (gated * slope_in[rows, :].astype(jnp.float32)).astype(jnp.bfloat16)
             at = pl.multiple_of(k * 32, 32)
@@ -937,7 +935,7 @@
 
             @pl.when((turn == layers - 1) & (seq == k))
             def _(k=k):
-                run(in_moves(k))
+                run(in_moves(k) if k < seqs - 1 else in_moves(k)[:near])
 
         for i in range(layers):
 
@@ -965,6 +963,7 @@
                 advance(kind, top, last_stage)
             run(spreads(1, top))
             advance(0, bottom, 1)
+            run(in_moves(seqs - 1)[near:])
             states(top)
             run(spreads(0, top))
             finish_all(vec_moves())
@@ -1083,11 +1082,9 @@
     toks = inputs.shape[1] // n_chan
     seqs = toks // BUCKET
     part = own // n_batch
-    me = lax.axis_index("chan")
     row = lax.axis_index("batch")
-    lens = lax.dynamic_slice_in_dim(lengths, me * seqs, seqs)
     places = lax.iota(jnp.int32, BUCKET)
-    valid = (places[None, :] < lens[:, None]).astype(jnp.float32).reshape(seqs, 1, BUCKET)
+    valid = (places[None, None, :] < lengths[:, None, None]).astype(jnp.float32)
     tables = tuple(jnp.asarray(t) for t in transform_tables())
 
     def mine(a):
@@ -1111,12 +1108,13 @@
     step_total = jnp.sum(state_all[:, 4], -1)
     lin_total = lin_all.reshape(n_batch, LAYERS, 2, part, chans).transpose(1, 0, 3, 2, 4).reshape(LAYERS, own, 2, chans)
     vec_sum = jnp.sum(vec_all, 0)[: 5 * LAYERS, :own].reshape(LAYERS, 5, own)
-    vec_total = jnp.stack([vec_sum[:, 0], vec_sum[:, 1], step_total, vec_sum[:, 2], vec_sum[:, 3], vec_sum[:, 4]], 1)
-
-    vec_old = jnp.stack([ln_gain, ln_bias, log_step, skip_gain, lin_bias[:, 0], lin_bias[:, 1]], 1)
+    vec_total = jnp.stack([vec_sum[:, 0], vec_sum[:, 1], step_total, vec_sum[:, 2], vec_sum[:, 3], vec_sum[:, 4]])
+
+    vec_old = jnp.stack([ln_gain, ln_bias, log_step, skip_gain, lin_bias[:, 0], lin_bias[:, 1]])
     state_old = jnp.stack([log_decay, frequency, w_re, w_im], 1)
     lin_first, lin_second, lin_new = adam(lin_weight, lin_total, lin_moment, lin_square, 0.05)
-    vec_first, vec_second, vec_new = adam(vec_old, vec_total, vec_moment, vec_square, 0.2)
+    turned = [a.transpose(1, 0, 2) for a in (vec_moment, vec_square)]
+    vec_first, vec_second, vec_new = [a.transpose(1, 0, 2) for a in adam(vec_old, vec_total, *turned, 0.2)]
     state_first, state_second, state_new = adam(state_old, state_total, state_moment, state_square, 0.2)
     return (
         output, input_grad, lin_first, lin_second, lin_new, vec_first, vec_second, vec_new,

time: 260 us -> 253 us (0.973)
  Pallas kernels: 234 us -> 230 us
  local copies, waits for them, and re-layouts: 10.8 us -> 7.63 us
    pallas_call x1, Pallas kernels: 234 us -> 230 us  [train(): pl.pallas_call(functools.partial(train_kernel, n_chan, n_batch), grid=(2...]
    sub x3 -> x2, other arithmetic: 5.65 us -> 3.89 us  [adam(): weight - rate * (fixed_first / (jnp.sqrt(fixed_second) + 1e-08) + 0.01 *...]
where the time goes in v5:
time: 253 us; the launch traced here: 252 us
  Pallas kernels  230 us (91%)
  other arithmetic  13.2 us (5%)
  local copies, waits for them, and re-layouts  7.63 us (3%)
    pallas_call x1, Pallas kernels, train(): pl.pallas_call(functools.partial(train_kernel, n_chan, n_batch), grid=(2...  230 us

profile of v5, /device:TPU:0, one launch (start us, length us, event | category | flops | bytes accessed | tf_op | source)
XLA Modules:
  0.0 251.9 jit_solution(948369305206485083)
XLA Ops:
  0.6 0.7 constant_dynamic-slice_fusion.3
  1.4 0.1 stack.69
  1.5 0.1 stack.70
  1.6 0.7 constant_dynamic-slice_fusion.1
  2.3 0.1 stack.71
  2.4 0.1 stack.72
  2.4 0.8 constant_dynamic-slice_fusion
  3.2 0.1 stack.73
  3.3 0.1 stack.74
  3.4 1.0 fusion.2
  4.3 0.6 copy.43
  5.0 1.4 compare_convert_fusion.mask
  6.4 1.3 fusion.3.vec_mine
  7.7 0.0 copy-start.20
  7.7 0.0 copy-start.15
  7.8 230.1 %train.1 = (bf16[64,16384]{1,0:T(8,128)(2,1)}, bf16[64,16384]{1,0:T(8,128)(2,1)}, f32[4,16,8,128]{3,2,1,0:T(8,128)}, f32[4,2,32,512]{3,2,1,0:T(8,128)}, f32[4,16...) custom-call(f32[16,1,1024]{2,1,0:T(1,128)} %compare_convert_fusion.m, ...), custom_call_target="tpu_custom_call" | custom-call | flops 60000002048 | bytes 62914560 | tf_op jit(solution)/shard_map/train/pallas_call | solution.py:999
  237.9 0.0 copy-start.9
  237.9 0.0 copy-start.10
  238.0 0.0 copy-start.13
  238.0 0.9 reduce_sum.18
  238.9 1.3 reshape.96
  240.2 0.0 copy-start.6
  240.2 0.2 copy.45
  240.4 0.1 slice_reduce_fusion
  240.7 0.6 subtract_bitcast_fusion
  241.4 1.0 multiply_subtract_fusion.1
  242.4 0.4 copy.44
  242.8 0.0 copy-start
  242.9 2.9 %multiply_subtract_fusion = (f32[2,64,2,512]{3,2,1,0:T(2,128)}, f32[2,64,2,512]{3,2,1,0:T(2,128)}, f32[2,64,2,512]{3,2,1,0:T(2,128)}) fusion(f32[2,64,2,512]{3,2,1,0:T(2,128)S(1)} %copy-done.4, f32[2,64,2,512]{3,2,1,0:T(2,128)S(1)} %bitcast.62, f32[2,64,2,512]{3,2,1,0:T(2,128)S(1)} %copy-done.5, f32[2,64,2,512]{3,2,1,0:T(2,128)S(1)} %copy-done.6), kind=kLoop, calls=%fused_computation.4 | loop fusion | flops 1966080 | bytes 3670016 | tf_op jit(solution)/shard_map/sub | solution.py:1070
  245.8 2.5 %convert_add_fusion = f32[64,16384]{1,0:T(8,128)} fusion(bf16[64,16384]{1,0:T(8,128)(2,1)S(1)} %copy-done.3, bf16[64,16384]{1,0:T(8,128)(2,1)S(1)} %copy-done), kind=kLoop, calls=%fused_computation | loop fusion | flops 3145728 | bytes 8388608 | tf_op jit(solution)/shard_map/add | solution.py:1103
  248.3 1.2 copy-done.2
  249.5 2.4 convert_add_fusion.1
  (56 shorter events, 0.2 us)
Async XLA Ops:
  3.4 4.3 %copy-start.21 = (f32[5,16,128]{2,1,0:T(8,128)}, f32[5,16,128]{2,1,0:T(8,128)S(1)}, u32[]{:S(2)}) copy-start(f32[5,16,128]{2,1,0:T(8,128)S(1)} %constant_dynamic-update-slice_fusion.raw) | copy-start | bytes 122884
  7.7 232.9 %copy-start.14 = (f32[2,2,64]{2,1,0:T(2,128)S(1)}, f32[2,2,64]{2,1,0:T(2,128)}, u32[]{:S(2)}) copy-start(f32[2,2,64]{2,1,0:T(2,128)} %param.30) | copy-start | bytes 3076
  7.7 232.9 %copy-start.18 = (f32[2,64]{1,0:T(2,128)S(1)}, f32[2,64]{1,0:T(2,128)}, u32[]{:S(2)}) copy-start(f32[2,64]{1,0:T(2,128)} %param.26) | copy-start | bytes 1540
  7.7 232.9 %copy-start.19 = (f32[2,64]{1,0:T(2,128)S(1)}, f32[2,64]{1,0:T(2,128)}, u32[]{:S(2)}) copy-start(f32[2,64]{1,0:T(2,128)} %param.27) | copy-start | bytes 1540
  7.7 232.9 %copy-start.17 = (f32[2,64]{1,0:T(2,128)S(1)}, f32[2,64]{1,0:T(2,128)}, u32[]{:S(2)}) copy-start(f32[2,64]{1,0:T(2,128)} %param.28) | copy-start | bytes 1540
  7.7 232.9 %copy-start.20 = (f32[2,64]{1,0:T(2,128)S(1)}, f32[2,64]{1,0:T(2,128)}, u32[]{:S(2)}) copy-start(f32[2,64]{1,0:T(2,128)} %param.29) | copy-start | bytes 1540
  7.7 233.0 %copy-start.15 = (f32[2,6,64]{2,0,1:T(2,128)S(1)}, f32[2,6,64]{2,0,1:T(2,128)}, u32[]{:S(2)}) copy-start(f32[2,6,64]{2,0,1:T(2,128)} %param.38) | copy-start | bytes 9220
  7.7 233.0 %copy-start.16 = (f32[2,6,64]{2,0,1:T(2,128)S(1)}, f32[2,6,64]{2,0,1:T(2,128)}, u32[]{:S(2)}) copy-start(f32[2,6,64]{2,0,1:T(2,128)} %param.39) | copy-start | bytes 9220
  237.9 3.5 %copy-start.8 = (f32[2,4,64,64]{3,2,1,0:T(8,128)S(1)}, f32[2,4,64,64]{3,2,1,0:T(8,128)}, u32[]{:S(2)}) copy-start(f32[2,4,64,64]{3,2,1,0:T(8,128)} %param.41) | copy-start | bytes 393220
  237.9 3.5 %copy-start.9 = (f32[2,4,64,64]{3,2,1,0:T(8,128)S(1)}, f32[2,4,64,64]{3,2,1,0:T(8,128)}, u32[]{:S(2)}) copy-start(f32[2,4,64,64]{3,2,1,0:T(8,128)} %param.40) | copy-start | bytes 393220
  237.9 3.5 %copy-start.10 = (f32[2,64,64]{2,1,0:T(8,128)S(1)}, f32[2,64,64]{2,1,0:T(8,128)}, u32[]{:S(2)}) copy-start(f32[2,64,64]{2,1,0:T(8,128)} %param.32) | copy-start | bytes 98308
  237.9 3.4 %copy-start.11 = (f32[2,64,64]{2,1,0:T(8,128)S(1)}, f32[2,64,64]{2,1,0:T(8,128)}, u32[]{:S(2)}) copy-start(f32[2,64,64]{2,1,0:T(8,128)} %param.31) | copy-start | bytes 98308
  237.9 3.4 %copy-start.12 = (f32[2,64,64]{2,1,0:T(8,128)S(1)}, f32[2,64,64]{2,1,0:T(8,128)}, u32[]{:S(2)}) copy-start(f32[2,64,64]{2,1,0:T(8,128)} %param.34) | copy-start | bytes 98308
  238.0 3.4 %copy-start.13 = (f32[2,64,64]{2,1,0:T(8,128)S(1)}, f32[2,64,64]{2,1,0:T(8,128)}, u32[]{:S(2)}) copy-start(f32[2,64,64]{2,1,0:T(8,128)} %param.33) | copy-start | bytes 98308
  238.0 4.4 %copy-start.7 = (f32[4,2,32,512]{3,2,1,0:T(8,128)S(1)}, f32[4,2,32,512]{3,2,1,0:T(8,128)}, u32[]{:S(2)}) copy-start(f32[4,2,32,512]{3,2,1,0:T(8,128)} %get-tuple-element.18) | copy-start | bytes 1572868
  240.2 2.7 %copy-start.4 = (f32[2,64,2,512]{3,2,1,0:T(2,128)S(1)}, f32[2,64,2,512]{3,2,1,0:T(2,128)}, u32[]{:S(2)}) copy-start(f32[2,64,2,512]{3,2,1,0:T(2,128)} %param.35) | copy-start | bytes 1572868
  240.2 2.7 %copy-start.5 = (f32[2,64,2,512]{3,2,1,0:T(2,128)S(1)}, f32[2,64,2,512]{3,2,1,0:T(2,128)}, u32[]{:S(2)}) copy-start(f32[2,64,2,512]{3,2,1,0:T(2,128)} %param.37) | copy-start | bytes 1572868
  240.2 2.7 %copy-start.6 = (f32[2,64,2,512]{3,2,1,0:T(2,128)S(1)}, f32[2,64,2,512]{3,2,1,0:T(2,128)}, u32[]{:S(2)}) copy-start(f32[2,64,2,512]{3,2,1,0:T(2,128)} %param.36) | copy-start | bytes 1572868
  242.4 3.3 %copy-start.3 = (bf16[64,16384]{1,0:T(8,128)(2,1)S(1)}, bf16[64,16384]{1,0:T(8,128)(2,1)}, u32[]{:S(2)}) copy-start(bf16[64,16384]{1,0:T(8,128)(2,1)} %get-tuple-element.17) | copy-start | bytes 6291460
  242.8 2.9 %copy-start = (bf16[64,16384]{1,0:T(8,128)(2,1)S(1)}, bf16[64,16384]{1,0:T(8,128)(2,1)}, u32[]{:S(2)}) copy-start(bf16[64,16384]{1,0:T(8,128)(2,1)} %cot_own.1) | copy-start | bytes 6291460
  245.8 2.6 %copy-start.1 = (bf16[64,16384]{1,0:T(8,128)(2,1)S(1)}, bf16[64,16384]{1,0:T(8,128)(2,1)}, u32[]{:S(2)}) copy-start(bf16[64,16384]{1,0:T(8,128)(2,1)} %x_own.1) | copy-start | bytes 6291460
  245.8 3.7 %copy-start.2 = (bf16[64,16384]{1,0:T(8,128)(2,1)S(1)}, bf16[64,16384]{1,0:T(8,128)(2,1)}, u32[]{:S(2)}) copy-start(bf16[64,16384]{1,0:T(8,128)(2,1)} %get-tuple-element.16) | copy-start | bytes 6291460
